TPU v7x, 32 devices: a whole 2x2x4 slice. The times are simulated.
32 devices in a mesh: expert: 4 (over z), ctx: 2 (over core), dp: 4 (over y, x).
Axes of the slice: x: 2, y: 2, z: 4, core: 2. Of those that a mesh axis runs over, the one named last changes fastest.
Arguments:
- tokens: bfloat16 [16, 2048, 768], P(('expert', 'dp'), 'ctx'), may hold values from -6 to 6
- cotangent: bfloat16 [16, 2048, 768], P(('expert', 'dp'), 'ctx'), may hold values from -6 to 6
- router_noise: float32 [16, 2048, 16], P(('expert', 'dp'), 'ctx'), may hold values from -2.4 to 2.4
- expert_ids: int32 [16, 2048, 2], P(('expert', 'dp'), 'ctx'), may hold values from 0 to 15, all different within a row
- seat_order: int32 [16, 2048], P(('expert', 'dp'), 'ctx'), may hold values from 0 to 63
- gain_attn: float32 [768], replicated, may hold values from 0.5 to 1.5
- w_qkv: bfloat16 [768, 2304], replicated, may hold values from -0.21875 to 0.21875
- w_out: bfloat16 [768, 768], replicated, may hold values from -2 to 2
- gain_moe: float32 [768], replicated, may hold values from 0.5 to 1.5
- w_router: bfloat16 [768, 16], replicated, may hold values from -0.15625 to 0.15625
- w_up: bfloat16 [16, 768, 3072], P('expert'), may hold values from -0.21875 to 0.21875
- w_down: bfloat16 [16, 3072, 768], P('expert'), may hold values from -1.75 to 1.75
Outputs:
- out_tokens: bfloat16 [16, 2048, 768], P(('expert', 'dp'), 'ctx')
- grad_tokens: float32 [16, 2048, 768], P(('expert', 'dp'), 'ctx')
- grad_gain_attn: float32 [768], replicated
- grad_w_qkv: float32 [768, 2304], replicated
- grad_w_out: float32 [768, 768], replicated
- grad_gain_moe: float32 [768], replicated
- grad_w_router: float32 [768, 16], replicated
- grad_w_up: float32 [16, 768, 3072], P('expert', None, ('ctx', 'dp'))
- grad_w_down: float32 [16, 3072, 768], P('expert', ('ctx', 'dp'))
Inputs may be any that keep to these rules, and one draw needn't show every extreme that they name: `expert_ids`: each token names two different experts; every expert is named by some token.
All inputs are finite; a program needn't handle non-finite values.
Results may differ from a plain program's by a relative error of at most 0.015.
Values may be sent and summed in bfloat16 or wider, within the bound.
No kernel may reach another device: no remote copies, remote signals or barrier semaphores. Data moves between devices by JAX's collectives and lax.ppermute only.
A program may use at most 576 MiB of HBM per device.

v0:
```python
import math

import jax
import jax.numpy as jnp
from jax import lax
from jax.sharding import PartitionSpec as P

HEADS = 12


NORM_EPS = 1e-06
HIGHEST_PREC = lax.Precision.HIGHEST


def norm_forward(values_in, gain_vec):
    centre_mean = jnp.mean(values_in, axis=-1, keepdims=True)
    centred = values_in - centre_mean
    inv_scale = lax.rsqrt(jnp.mean(centred * centred, axis=-1, keepdims=True) + NORM_EPS)
    unit_rows = centred * inv_scale
    return (unit_rows * gain_vec, unit_rows, inv_scale)


def norm_backward(gradient, unit_rows, inv_scale, gain_vec):
    scaled = gradient * gain_vec
    inner_sum = (
        scaled
        - jnp.mean(scaled, axis=-1, keepdims=True)
        - unit_rows * jnp.mean(scaled * unit_rows, axis=-1, keepdims=True)
    )
    return (inner_sum * inv_scale, jnp.sum(gradient * unit_rows, axis=0))


def gelu_tanh(values_in):
    return jax.nn.gelu(values_in, approximate=True)


def seating(expert_ids, seat_order, expert_count, capacity):
    token_count = expert_ids.shape[0]
    places = jnp.arange(token_count, dtype=jnp.int32)
    earlier = (seat_order[:, None] < seat_order[None, :]) | (
        seat_order[:, None] == seat_order[None, :]
    ) & (places[:, None] < places[None, :])
    earlier = earlier.astype(jnp.bfloat16)
    lane_ids = jnp.arange(expert_count, dtype=jnp.int32)
    first_hot = expert_ids[:, 0:1] == lane_ids[None, :]
    second_hot = expert_ids[:, 1:2] == lane_ids[None, :]
    ahead_first = jnp.einsum(
        "st,se->te", earlier, first_hot.astype(jnp.bfloat16), preferred_element_type=jnp.float32
    )
    rank_first = jnp.sum(jnp.where(first_hot, ahead_first, 0.0), axis=-1)
    ahead_second = jnp.einsum(
        "st,se->te", earlier, second_hot.astype(jnp.bfloat16), preferred_element_type=jnp.float32
    )
    ahead_second = ahead_second + jnp.sum(first_hot.astype(jnp.float32), axis=0)[None, :]
    rank_second = jnp.sum(jnp.where(second_hot, ahead_second, 0.0), axis=-1)
    slot_ids = jnp.arange(expert_count * capacity, dtype=jnp.int32)

    def slot_table(picked, rank_of):
        target = picked * capacity + rank_of.astype(jnp.int32)
        is_live = rank_of < capacity
        return ((slot_ids[:, None] == target[None, :]) & is_live[None, :]).astype(jnp.bfloat16)

    return (
        slot_table(expert_ids[:, 0], rank_first),
        slot_table(expert_ids[:, 1], rank_second),
        first_hot,
        second_hot,
    )


def body(
    tokens,
    cotangent,
    router_noise,
    expert_ids,
    seat_order,
    gain_attn,
    w_qkv,
    w_out,
    gain_moe,
    w_router,
    w_up,
    w_down,
):
    image_count, half_len, model_width = tokens.shape
    row_count = image_count * half_len
    head_dim = model_width // HEADS
    scaling = 1.0 / math.sqrt(head_dim)
    expert_count = router_noise.shape[-1]
    owner_count = lax.axis_size("expert")
    experts_here = w_up.shape[0]
    capacity = (2 * row_count + expert_count - 1) // expert_count
    tokens_f = tokens.reshape(row_count, model_width).astype(jnp.float32)
    normed_a, unit_a, inv_a = norm_forward(tokens_f, gain_attn)
    normed_ab = normed_a.astype(jnp.bfloat16)
    qkv_b = jnp.dot(normed_ab, w_qkv, preferred_element_type=jnp.float32).astype(jnp.bfloat16)
    queries = qkv_b[:, :model_width].reshape(image_count, half_len, HEADS, head_dim)
    keys_here = qkv_b[:, model_width : 2 * model_width].reshape(image_count, half_len, model_width)
    values_here = qkv_b[:, 2 * model_width :].reshape(image_count, half_len, model_width)
    keys_all, values_all = (
        lax.all_gather(keys_here, "ctx", axis=1, tiled=True),
        lax.all_gather(values_here, "ctx", axis=1, tiled=True),
    )
    keys_all = keys_all.reshape(image_count, -1, HEADS, head_dim)
    values_all = values_all.reshape(image_count, -1, HEADS, head_dim)

    def score_rows():
        return (
            jnp.einsum("iqhd,ikhd->ihqk", queries, keys_all, preferred_element_type=jnp.float32)
            * scaling
        )

    scores = score_rows()
    row_peak = jnp.max(scores, axis=-1, keepdims=True)
    log_total = row_peak + jnp.log(jnp.sum(jnp.exp(scores - row_peak), axis=-1, keepdims=True))
    attn_probs = jnp.exp(scores - log_total)
    mixed_out = jnp.einsum(
        "ihqk,ikhd->iqhd",
        attn_probs.astype(jnp.bfloat16),
        values_all,
        preferred_element_type=jnp.float32,
    )
    mixed_b = mixed_out.reshape(row_count, model_width).astype(jnp.bfloat16)
    branch = jnp.dot(mixed_b, w_out, preferred_element_type=jnp.float32)
    middle = tokens_f + branch
    normed_m, unit_m, inv_m = norm_forward(middle, gain_moe)
    routed_b = normed_m.astype(jnp.bfloat16)
    logits = jnp.dot(routed_b, w_router, preferred_element_type=jnp.float32) + router_noise.reshape(
        row_count, expert_count
    )
    gate_probs = jax.nn.softmax(logits, axis=-1)
    first_table, second_table, first_hot, second_hot = seating(
        expert_ids.reshape(row_count, 2), seat_order.reshape(row_count), expert_count, capacity
    )
    both_tables = first_table + second_table
    gate_first = jnp.sum(jnp.where(first_hot, gate_probs, 0.0), axis=-1, keepdims=True)
    gate_second = jnp.sum(jnp.where(second_hot, gate_probs, 0.0), axis=-1, keepdims=True)
    slots_b = jnp.einsum(
        "pt,td->pd", both_tables, routed_b, preferred_element_type=jnp.float32
    ).astype(jnp.bfloat16)
    slots_b = slots_b.reshape(owner_count, experts_here, capacity, model_width)
    received = lax.all_to_all(slots_b, "expert", split_axis=0, concat_axis=0, tiled=True)
    hidden_pre = jnp.einsum("sjcd,jdf->sjcf", received, w_up, preferred_element_type=jnp.float32)
    active_b = gelu_tanh(hidden_pre).astype(jnp.bfloat16)
    produced_b = jnp.einsum(
        "sjcf,jfd->sjcd", active_b, w_down, preferred_element_type=jnp.float32
    ).astype(jnp.bfloat16)
    returned = lax.all_to_all(
        produced_b, "expert", split_axis=0, concat_axis=0, tiled=True
    ).reshape(expert_count * capacity, model_width)
    rows_first = jnp.einsum("pt,pd->td", first_table, returned, preferred_element_type=jnp.float32)
    rows_second = jnp.einsum(
        "pt,pd->td", second_table, returned, preferred_element_type=jnp.float32
    )
    result = middle + gate_first * rows_first + gate_second * rows_second
    d_result = cotangent.reshape(row_count, model_width).astype(jnp.float32)
    d_gate_first = jnp.sum(d_result * rows_first, axis=-1, keepdims=True)
    d_gate_second = jnp.sum(d_result * rows_second, axis=-1, keepdims=True)
    sent_first = (gate_first * d_result).astype(jnp.bfloat16)
    sent_second = (gate_second * d_result).astype(jnp.bfloat16)
    d_slots = jnp.einsum("pt,td->pd", first_table, sent_first, preferred_element_type=jnp.float32)
    d_slots = d_slots + jnp.einsum(
        "pt,td->pd", second_table, sent_second, preferred_element_type=jnp.float32
    )
    d_slots_b = d_slots.astype(jnp.bfloat16).reshape(
        owner_count, experts_here, capacity, model_width
    )
    d_produced = lax.all_to_all(d_slots_b, "expert", split_axis=0, concat_axis=0, tiled=True)
    d_active = jnp.einsum("sjcd,jfd->sjcf", d_produced, w_down, preferred_element_type=jnp.float32)
    gelu_value, gelu_back = jax.vjp(gelu_tanh, hidden_pre)
    d_hidden_b = gelu_back(d_active)[0].astype(jnp.bfloat16)
    d_received = jnp.einsum(
        "sjcf,jdf->sjcd", d_hidden_b, w_up, preferred_element_type=jnp.float32
    ).astype(jnp.bfloat16)
    d_returned = lax.all_to_all(
        d_received, "expert", split_axis=0, concat_axis=0, tiled=True
    ).reshape(expert_count * capacity, model_width)
    grad_up = jnp.einsum("sjcd,sjcf->jdf", received, d_hidden_b, preferred_element_type=jnp.float32)
    grad_down = jnp.einsum(
        "sjcf,sjcd->jfd", active_b, d_produced, preferred_element_type=jnp.float32
    )
    grad_up, grad_down = (
        lax.psum_scatter(grad_up, ("ctx", "dp"), scatter_dimension=2, tiled=True),
        lax.psum_scatter(grad_down, ("ctx", "dp"), scatter_dimension=1, tiled=True),
    )
    d_gates = jnp.where(first_hot, d_gate_first, 0.0) + jnp.where(second_hot, d_gate_second, 0.0)
    d_logits = gate_probs * (d_gates - jnp.sum(gate_probs * d_gates, axis=-1, keepdims=True))
    d_w_router = jnp.einsum(
        "td,te->de", routed_b.astype(jnp.float32), d_logits, precision=HIGHEST_PREC
    )
    d_routed = jnp.einsum(
        "te,de->td", d_logits, w_router.astype(jnp.float32), precision=HIGHEST_PREC
    )
    d_routed = d_routed + jnp.einsum(
        "pt,pd->td", both_tables, d_returned, preferred_element_type=jnp.float32
    )
    d_norm_m, d_gain_moe = norm_backward(d_routed, unit_m, inv_m, gain_moe)
    d_middle = d_result + d_norm_m
    d_branch_b = d_middle.astype(jnp.bfloat16)
    d_w_out = jnp.einsum("td,te->de", mixed_b, d_branch_b, preferred_element_type=jnp.float32)
    d_mixed_b = jnp.einsum(
        "te,de->td", d_branch_b, w_out, preferred_element_type=jnp.float32
    ).astype(jnp.bfloat16)
    d_mixed_b = d_mixed_b.reshape(image_count, half_len, HEADS, head_dim)
    scores = score_rows()
    attn_probs = jnp.exp(scores - log_total)
    d_probs = jnp.einsum(
        "iqhd,ikhd->ihqk", d_mixed_b, values_all, preferred_element_type=jnp.float32
    )
    d_values = jnp.einsum(
        "ihqk,iqhd->ikhd",
        attn_probs.astype(jnp.bfloat16),
        d_mixed_b,
        preferred_element_type=jnp.float32,
    )
    d_scores_b = (
        attn_probs * (d_probs - jnp.sum(attn_probs * d_probs, axis=-1, keepdims=True))
    ).astype(jnp.bfloat16)
    d_queries = (
        jnp.einsum("ihqk,ikhd->iqhd", d_scores_b, keys_all, preferred_element_type=jnp.float32)
        * scaling
    )
    d_keys = (
        jnp.einsum("ihqk,iqhd->ikhd", d_scores_b, queries, preferred_element_type=jnp.float32)
        * scaling
    )
    d_keys_here, d_values_here = (
        lax.psum_scatter(
            d_keys.reshape(image_count, -1, model_width), "ctx", scatter_dimension=1, tiled=True
        ),
        lax.psum_scatter(
            d_values.reshape(image_count, -1, model_width), "ctx", scatter_dimension=1, tiled=True
        ),
    )
    d_qkv_b = jnp.concatenate(
        [
            d_queries.reshape(row_count, model_width),
            d_keys_here.reshape(row_count, model_width),
            d_values_here.reshape(row_count, model_width),
        ],
        axis=-1,
    ).astype(jnp.bfloat16)
    d_w_qkv = jnp.einsum("td,tf->df", normed_ab, d_qkv_b, preferred_element_type=jnp.float32)
    d_normed_a = jnp.einsum("tf,df->td", d_qkv_b, w_qkv, preferred_element_type=jnp.float32)
    d_tokens_norm, d_gain_attn = norm_backward(d_normed_a, unit_a, inv_a, gain_attn)
    d_tokens = d_middle + d_tokens_norm
    summed = lax.psum(
        (d_gain_attn, d_w_qkv, d_w_out, d_gain_moe, d_w_router), ("expert", "ctx", "dp")
    )
    return (
        result.reshape(image_count, half_len, model_width).astype(jnp.bfloat16),
        d_tokens.reshape(image_count, half_len, model_width),
        summed[0],
        summed[1],
        summed[2],
        summed[3],
        summed[4],
        grad_up,
        grad_down,
    )


def solution(mesh):
    placed = (
        P(("expert", "dp"), "ctx", None),
        P(("expert", "dp"), "ctx", None),
        P(("expert", "dp"), "ctx", None),
        P(("expert", "dp"), "ctx", None),
        P(("expert", "dp"), "ctx"),
        P(),
        P(),
        P(),
        P(),
        P(),
        P("expert", None, None),
        P("expert", None, None),
    )
    return jax.shard_map(
        body,
        mesh=mesh,
        in_specs=placed,
        out_specs=(
            P(("expert", "dp"), "ctx", None),
            P(("expert", "dp"), "ctx", None),
            P(),
            P(),
            P(),
            P(),
            P(),
            P("expert", None, ("ctx", "dp")),
            P("expert", ("ctx", "dp"), None),
        ),
        check_vma=False,
    )
```

profile of v0, /device:TPU:0, one launch (start us, length us, event | category | flops | bytes accessed | tf_op | source)
XLA Modules:
  0.0 1511.8 jit_solution(14110590836729032877)
XLA Ops:
  26.4 9.0 all-gather.7.cloned.1.call-done
  40.1 38.4 %multiply_reduce_fusion.1 = (f32[12,1024]{1,0:T(8,128)}, f32[12,1024,2048]{2,1,0:T(8,128)}) fusion(bf16[1024,12,64]{0,2,1:T(8,128)(2,1)} %bitcast.180, bf16[2048,12,64]{0,2,1:T(8,128)(2,1)} %bitcast.174), kind=kOutput, calls=%fused_computation.4 | convolution fusion | flops 3271544832 | bytes 105431040 | tf_op jit(solution)/shard_map/iqhd,ikhd->ihqk/dot_general | solution.py:109
  78.5 31.8 %exponential_reduce_fusion = f32[12,1024]{1,0:T(8,128)} fusion(f32[12,1024,2048]{2,1,0:T(8,128)} %get-tuple-element.60, f32[12,1024]{1,0:T(8,128)} %get-tuple-element.59), kind=kLoop, calls=%fused_computation.3 | loop fusion | flops 75485184 | bytes 100761600 | tf_op jit(solution)/shard_map/reduce_sum | solution.py:115
  111.9 4.6 copy.49
  116.5 35.1 %fusion.92 = bf16[12,64,1024]{2,1,0:T(8,128)(2,1)} fusion(bf16[2048,12,64]{0,2,1:T(8,128)(2,1)} %bitcast.176, f32[12,1024,2048]{2,1,0:T(8,128)} %get-tuple-element.60, f32[12,1024]{1,0:T(8,128)} %log_add_fusion), kind=kOutput, calls=%fused_computation.110 | convolution fusion | flops 3297509376 | bytes 105431040 | tf_op jit(solution)/shard_map/ihqk,ikhd->iqhd/dot_general | solution.py:117
  157.1 5.6 fusion.62
  162.7 76.1 %all_to_all.20 = bf16[4,4,128,768]{3,2,1,0:T(8,128)(2,1)} all-to-all(bf16[4,4,128,768]{3,2,1,0:T(8,128)(2,1)S(1)} %bitcast.186), channel_id=1, replica_groups=mesh['expert'=4,'ctx'=2,'dp'=4] {'expert'}, dimensions={0} | all-to-all | bytes 6291456 | tf_op jit(solution)/shard_map/all_to_all | solution.py:142
  238.8 21.5 %fusion.14 = f32[4,4,128,3072]{3,2,1,0:T(8,128)} fusion(bf16[4,768,3072]{2,1,0:T(8,128)(2,1)} %param.22, bf16[4,4,128,768]{3,2,1,0:T(8,128)(2,1)} %all_to_all.20), kind=kOutput, calls=%fused_computation.24 | convolution fusion | flops 9663676416 | bytes 47185920 | tf_op jit(solution)/shard_map/sjcd,jdf->sjcf/dot_general | solution.py:143
  260.4 22.5 %convert_bitcast_fusion.2 = bf16[4,4,128,768]{3,2,0,1:T(8,128)(2,1)} fusion(bf16[4,3072,768]{2,1,0:T(8,128)(2,1)} %param.23, f32[4,4,128,3072]{3,2,1,0:T(8,128)} %fusion.14), kind=kOutput, calls=%fused_computation.97 | convolution fusion | flops 9721872384 | bytes 47185920 | tf_op jit(solution)/shard_map/sjcf,jfd->sjcd/dot_general | solution.py:145
  286.8 4.7 all-to-all-start.1
  296.9 64.9 %all-to-all-done.1 = bf16[4,4,128,768]{3,2,1,0:T(8,128)(2,1)} async-done(((bf16[4,4,128,768]{3,2,1,0:T(8,128)(2,1)}), bf16[4,4,128,768]{3,2,1,0:T(8,128)(2,1)}, u32[]{:S(2)}, u32[]{:S(2)}) %all-to-all-start.1) | async-done | bytes 3145760 | tf_op jit(solution)/shard_map/all_to_all | solution.py:148
  361.9 5.6 fusion.32
  367.6 8.8 fusion.73
  386.0 73.5 %all_to_all.21 = bf16[4,4,128,768]{3,2,1,0:T(8,128)(2,1)} all-to-all(bf16[4,4,128,768]{3,2,1,0:T(8,128)(2,1)S(1)} %bitcast.185), channel_id=1, replica_groups=mesh['expert'=4,'ctx'=2,'dp'=4] {'expert'}, dimensions={0} | all-to-all | bytes 6291456 | tf_op jit(solution)/shard_map/all_to_all | solution.py:168
  459.5 29.0 %fusion.7 = bf16[4,4,128,3072]{3,2,0,1:T(8,128)(2,1)} fusion(f32[4,4,128,3072]{3,2,1,0:T(8,128)} %fusion.14, bf16[4,3072,768]{2,1,0:T(8,128)(2,1)} %param.23, bf16[4,4,128,768]{3,2,1,0:T(8,128)(2,1)} %all_to_all.21), kind=kOutput, calls=%fused_computation.14 | convolution fusion | flops 9789505536 | bytes 59768832 | tf_op jit(solution)/shard_map/sjcd,jfd->sjcf/dot_general | solution.py:169
  488.6 17.8 %convert_bitcast_fusion.1 = bf16[4,4,128,768]{3,2,0,1:T(8,128)(2,1)} fusion(bf16[4,4,128,3072]{3,2,0,1:T(8,128)(2,1)} %fusion.7, bf16[4,768,3072]{2,1,0:T(8,128)(2,1)} %param.22), kind=kOutput, calls=%fused_computation.95 | convolution fusion | flops 9665249280 | bytes 34603008 | tf_op jit(solution)/shard_map/sjcf,jdf->sjcd/dot_general | solution.py:172
  508.6 72.9 %all_to_all.22 = bf16[4,4,128,768]{3,2,1,0:T(8,128)(2,1)S(1)} all-to-all(bf16[4,4,128,768]{3,2,1,0:T(8,128)(2,1)S(1)} %copy.56), channel_id=1, replica_groups=mesh['expert'=4,'ctx'=2,'dp'=4] {'expert'}, dimensions={0} | all-to-all | bytes 6291456 | tf_op jit(solution)/shard_map/all_to_all | solution.py:175
  594.5 37.1 %fusion.35 = f32[12,64,2048]{2,1,0:T(8,128)} fusion(bf16[1024,12,64]{0,2,1:T(8,128)(2,1)S(1)} %bitcast.182, f32[12,1024,2048]{2,1,0:T(8,128)} %get-tuple-element.60, f32[12,1024]{1,0:T(8,128)S(1)} %copy-done.6), kind=kOutput, calls=%fused_computation.43 | convolution fusion | flops 3296722944 | bytes 108576768 | tf_op jit(solution)/shard_map/ihqk,iqhd->ikhd/dot_general | solution.py:210
  631.6 70.9 %multiply_reduce_fusion = (f32[12,1024]{1,0:T(8,128)}, f32[12,1024,2048]{2,1,0:T(8,128)}) fusion(f32[12,1024,2048]{2,1,0:T(8,128)} %get-tuple-element.60, f32[12,1024]{1,0:T(8,128)} %log_add_fusion, bf16[1024,12,64]{0,2,1:T(8,128)(2,1)} %bitcast.183, bf16[2048,12,64]{0,2,1:T(8,128)(2,1)} %bitcast.177), kind=kOutput, calls=%fused_computation.1 | convolution fusion | flops 3321876480 | bytes 206143488 | tf_op jit(solution)/shard_map/iqhd,ikhd->ihqk/dot_general | solution.py:207
  702.6 78.4 %multiply_convert_fusion = bf16[12,1024,2048]{2,1,0:T(8,128)(2,1)} fusion(f32[12,1024,2048]{2,1,0:T(8,128)} %get-tuple-element.68, f32[12,1024,2048]{2,1,0:T(8,128)} %get-tuple-element.60, f32[12,1024]{1,0:T(8,128)} %get-tuple-element.67, f32[12,1024]{1,0:T(8,128)} %log_add_fusion), kind=kLoop, calls=%fused_computation | loop fusion | flops 125829120 | bytes 251756544 | tf_op jit(solution)/shard_map/convert_element_type | solution.py:218
  780.9 21.1 %convolution_multiply_fusion = f32[12,64,2048]{2,1,0:T(8,128)} fusion(bf16[1024,12,64]{0,2,1:T(8,128)(2,1)} %bitcast.181, bf16[12,1024,2048]{2,1,0:T(8,128)(2,1)} %multiply_convert_fusion), kind=kOutput, calls=%fused_computation.71 | convolution fusion | flops 3222798336 | bytes 58195968 | tf_op jit(solution)/shard_map/ihqk,iqhd->ikhd/dot_general | solution.py:224
  802.1 5.3 fusion.117
  807.4 25.2 %multiply_convert_fusion.1 = bf16[12,64,1024]{2,1,0:T(8,128)(2,1)} fusion(bf16[2048,12,64]{0,2,1:T(8,128)(2,1)} %bitcast.175, bf16[12,1024,2048]{2,1,0:T(8,128)(2,1)} %multiply_convert_fusion), kind=kOutput, calls=%fused_computation.93 | convolution fusion | flops 3222798336 | bytes 55050240 | tf_op jit(solution)/shard_map/ihqk,ikhd->iqhd/dot_general | solution.py:220
  839.5 6.9 fusion.90
  846.4 27.0 %convolution_bitcast_fusion = f32[4,3072,768]{2,1,0:T(8,128)} fusion(bf16[4,4,128,768]{3,2,1,0:T(8,128)(2,1)} %all_to_all.21, f32[4,4,128,3072]{3,2,1,0:T(8,128)} %fusion.14), kind=kOutput, calls=%fused_computation.30 | convolution fusion | flops 9720299520 | bytes 66060288 | tf_op jit(solution)/shard_map/sjcf,sjcd->jfd/dot_general | solution.py:179
  873.5 21.7 %convolution_bitcast_fusion.1 = f32[4,768,3072]{2,1,0:T(8,128)} fusion(bf16[4,4,128,768]{3,2,1,0:T(8,128)(2,1)} %all_to_all.20, bf16[4,4,128,3072]{3,2,0,1:T(8,128)(2,1)} %fusion.7), kind=kOutput, calls=%fused_computation.31 | convolution fusion | flops 9663676416 | bytes 53477376 | tf_op jit(solution)/shard_map/sjcd,sjcf->jdf/dot_general | solution.py:178
  902.0 7.7 fusion.71
  915.9 40.4 %all-reduce = (f32[768]{0:T(1024)}, f32[768]{0:T(1024)}, f32[768,16]{0,1:T(8,128)}) all-reduce(f32[768]{0:T(1024)S(1)} %get-tuple-element.38, f32[768]{0:T(1024)S(1)} %copy-done.48, f32[768,16]{0,1:T(8,128)} %fusion.124), channel_id=1, replica_groups=mesh['expert'=4,'ctx'=2,'dp'=4] {'expert','ctx','dp'}, use_global_device_ids=true, to_apply=%region_24.25 | all-reduce | flops 13824 | bytes 110592 | tf_op jit(solution)/shard_map/psum | solution.py:247
  956.3 80.9 %all-reduce.4.cloned.1.call-done = (f32[768,2304]{1,0:T(8,128)}, f32[768,768]{1,0:T(8,128)}) async-done(((f32[768,2304]{1,0:T(8,128)}, f32[768,768]{1,0:T(8,128)}), (f32[768,2304]{1,0:T(8,128)}, f32[768,768]{1,0:T(8,128)})) %all-reduce.4.cloned.1.call-update) | async-done | bytes 9437200 | tf_op jit(solution)/shard_map/psum | solution.py:247
  1037.2 229.9 %reduce-scatter.11.cloned.1.call-done = f32[4,384,768]{2,1,0:T(8,128)} async-done(((f32[4,3072,768]{2,1,0:T(8,128)}), f32[4,384,768]{2,1,0:T(8,128)}) %reduce-scatter.11.cloned.1.call-update) | async-done | bytes 4718608 | tf_op jit(solution)/shard_map/reduce_scatter | solution.py:184
  1267.2 229.6 %reduce-scatter.9.cloned.1.call-done = f32[4,768,384]{2,1,0:T(8,128)} async-done(((f32[4,768,3072]{2,1,0:T(8,128)}), f32[4,768,384]{2,1,0:T(8,128)}) %reduce-scatter.9.cloned.1.call-update) | async-done | bytes 4718608 | tf_op jit(solution)/shard_map/reduce_scatter | solution.py:183
  1496.7 6.6 copy.78
  (209 shorter events, 85.7 us)
Async XLA Ops:
  7.2 6.5 copy-start
  7.2 6.5 copy-start.57
  7.2 28.3 %all-gather.7.cloned.1.call-start = ((), (), s32[]{:S(2)}) async-start(), calls=%async_computation.13 | async-start | bytes 4718592 | tf_op jit(solution)/shard_map/all_gather | solution.py:101
  20.4 91.4 %all-gather.5.cloned.1.call-start = ((), (), s32[]{:S(2)}) async-start(), calls=%async_computation.12 | async-start | bytes 4718592 | tf_op jit(solution)/shard_map/all_gather | solution.py:102
  23.6 133.4 %copy-start.69 = (pred[1024]{0:T(1024)(128)(4,1)}, pred[1024]{0:T(1024)(128)(4,1)S(1)}, u32[]{:S(2)}) copy-start(pred[1024]{0:T(1024)(128)(4,1)S(1)} %get-tuple-element.73) | copy-start | bytes 3076
  23.6 338.2 %copy-start.66 = (pred[1024]{0:T(1024)(128)(4,1)}, pred[1024]{0:T(1024)(128)(4,1)S(1)}, u32[]{:S(2)}) copy-start(pred[1024]{0:T(1024)(128)(4,1)S(1)} %get-tuple-element.72) | copy-start | bytes 3076
  23.6 133.4 %copy-start.63 = (s32[1024]{0:T(1024)}, s32[1024]{0:T(1024)S(1)}, u32[]{:S(2)}) copy-start(s32[1024]{0:T(1024)S(1)} %get-tuple-element.71) | copy-start | bytes 12292
  23.7 338.2 %copy-start.60 = (s32[1024]{0:T(1024)}, s32[1024]{0:T(1024)S(1)}, u32[]{:S(2)}) copy-start(s32[1024]{0:T(1024)S(1)} %get-tuple-element.70) | copy-start | bytes 12292
  156.1 6.6 copy-start.36
  286.8 75.1 %all-to-all-start.1 = ((bf16[4,4,128,768]{3,2,1,0:T(8,128)(2,1)}), bf16[4,4,128,768]{3,2,1,0:T(8,128)(2,1)}, u32[]{:S(2)}, u32[]{:S(2)}) async-start(bf16[4,4,128,768]{3,2,1,0:T(8,128)(2,1)} %copy.53), calls=%async_computation.1 | async-start | bytes 6291456 | tf_op jit(solution)/shard_map/all_to_all | solution.py:148
  291.5 541.1 %reduce-scatter.7.cloned.1.call-start = ((), (), s32[]{:S(2)}) async-start(), calls=%async_computation.9 | async-start | bytes 9437184 | tf_op jit(solution)/shard_map/reduce_scatter | solution.py:231
  296.3 289.7 %copy-start.26 = (f32[1024]{0:T(1024)}, f32[1024]{0:T(1024)S(1)}, u32[]{:S(2)}) copy-start(f32[1024]{0:T(1024)S(1)} %get-tuple-element.64) | copy-start | bytes 12292
  296.9 289.0 %copy-start.34 = (f32[1024]{0:T(1024)}, f32[1024]{0:T(1024)S(1)}, u32[]{:S(2)}) copy-start(f32[1024]{0:T(1024)S(1)} %fusion.123) | copy-start | bytes 12292
  367.5 8.8 copy-start.13
  367.5 8.8 copy-start.18
  367.6 8.8 copy-start.24
  367.6 8.8 copy-start.29
  508.5 73.0 %copy-start.62 = (s32[1024]{0:T(1024)S(1)}, s32[1024]{0:T(1024)}, u32[]{:S(2)}) copy-start(s32[1024]{0:T(1024)} %copy-done.60) | copy-start | bytes 12292
  508.5 73.0 %copy-start.65 = (s32[1024]{0:T(1024)S(1)}, s32[1024]{0:T(1024)}, u32[]{:S(2)}) copy-start(s32[1024]{0:T(1024)} %copy-done.63) | copy-start | bytes 12292
  508.5 72.9 %copy-start.68 = (pred[1024]{0:T(1024)(128)(4,1)S(1)}, pred[1024]{0:T(1024)(128)(4,1)}, u32[]{:S(2)}) copy-start(pred[1024]{0:T(1024)(128)(4,1)} %copy-done.66) | copy-start | bytes 3076
  508.6 72.9 %copy-start.71 = (pred[1024]{0:T(1024)(128)(4,1)S(1)}, pred[1024]{0:T(1024)(128)(4,1)}, u32[]{:S(2)}) copy-start(pred[1024]{0:T(1024)(128)(4,1)} %copy-done.69) | copy-start | bytes 3076
  594.5 37.1 %copy-start.12 = (bf16[1024,768]{0,1:T(8,128)(2,1)}, bf16[1024,768]{0,1:T(8,128)(2,1)S(1)}, u32[]{:S(2)}) copy-start(bf16[1024,768]{0,1:T(8,128)(2,1)S(1)} %convolution_convert_fusion.1) | copy-start | bytes 4718596
  631.6 204.3 %reduce-scatter.5.cloned.1.call-start = ((), (), s32[]{:S(2)}) async-start(), calls=%async_computation.8 | async-start | bytes 9437184 | tf_op jit(solution)/shard_map/reduce_scatter | solution.py:228
  802.0 235.2 %all-reduce.4.cloned.1.call-start = ((), (), s32[]{:S(2)}) async-start(), calls=%async_computation.14 | async-start | bytes 18874368 | tf_op jit(solution)/shard_map/psum | solution.py:247
  832.6 6.8 copy-start.44
  832.6 6.8 copy-start.50
  832.6 6.8 copy-start.58
  846.4 420.8 %reduce-scatter.11.cloned.1.call-start = ((), (), s32[]{:S(2)}) async-start(), calls=%async_computation.11 | async-start | bytes 42467328 | tf_op jit(solution)/shard_map/reduce_scatter | solution.py:184
  873.5 623.3 %reduce-scatter.9.cloned.1.call-start = ((), (), s32[]{:S(2)}) async-start(), calls=%async_computation.10 | async-start | bytes 42467328 | tf_op jit(solution)/shard_map/reduce_scatter | solution.py:183
  902.0 7.8 copy-start.5
  902.0 7.8 copy-start.9
  1496.7 6.6 copy-start.16
  (50 other events, 165.2 us)
Sparse Core Ops, SparseCore 0:
  20.6 14.8 all-gather.6
  37.6 13.2 all-gather.4
  631.7 13.4 reduce-scatter.6
  802.1 13.2 reduce-scatter.4
  846.5 190.6 all-reduce.3
  1041.7 225.3 reduce-scatter.10
  1271.4 225.3 reduce-scatter.8
where the time goes:
time: 1520 us; the launch traced here: 1510 us
  waiting for transfers between devices  615 us (40%)
  matrix products  441 us (29%)
  blocking collectives  263 us (17%)
  other arithmetic  129 us (8%)
  local copies, waits for them, and re-layouts  44.3 us (3%)
    reduce_scatter x1, waiting for transfers between devices, body(): lax.psum_scatter(grad_down, ('ctx', 'dp'), scatter_dimension=1, tiled=True)  230 us
    reduce_scatter x1, waiting for transfers between devices, body(): lax.psum_scatter(grad_up, ('ctx', 'dp'), scatter_dimension=2, tiled=True)  230 us
    psum x1, waiting for transfers between devices, body(): lax.psum((d_gain_attn, d_w_qkv, d_w_out, d_gain_moe, d_w_router), ('exper...  80.9 us
    convert_element_type x1, other arithmetic, body(): d_scores_b = (attn_probs * (d_probs - jnp.sum(attn_probs * d_probs, axis=...  78.4 us
    all_to_all x1, blocking collectives, body(): lax.all_to_all(slots_b, 'expert', split_axis=0, concat_axis=0, tiled=True)  76.1 us
    all_to_all x1, blocking collectives, body(): lax.all_to_all(d_slots_b, 'expert', split_axis=0, concat_axis=0, tiled=True)  73.5 us
    all_to_all x1, blocking collectives, body(): lax.all_to_all(d_received, 'expert', split_axis=0, concat_axis=0, tiled=T...  72.9 us
    dot_general x1, matrix products, body(): jnp.einsum('iqhd,ikhd->ihqk', d_mixed_b, values_all, preferred_element_ty...  70.9 us
  transfers between devices with their start and end apart: 8, of which 5 were waited for; matrix products, arithmetic and copies ran while one was open for 24% of the time, Pallas kernels for 0%

commit v1 on v0

v1 whole, which is shorter than its diff:
```python
import functools
import math

import jax
import jax.numpy as jnp
from jax import lax
from jax.experimental import pallas as pl
from jax.experimental.pallas import tpu as pltpu
from jax.sharding import PartitionSpec as P

HEADS = 12
NORM_EPS = 1e-06
BF = jnp.bfloat16
F32 = jnp.float32
NN = (((1,), (0,)), ((), ()))
NT = (((1,), (1,)), ((), ()))
VMEM_BYTES = 60 << 20
EXTRA = 8
SMALL = 128


def estimate(flops, moved, slow=0):
    return pl.CostEstimate(flops=flops // 4, bytes_accessed=moved // 4, transcendentals=slow // 4)


def mm(left, right, dims=NN):
    return lax.dot_general(left, right, dims, preferred_element_type=F32)


def norm_forward(values_in, gain_vec):
    centre_mean = jnp.mean(values_in, axis=-1, keepdims=True)
    centred = values_in - centre_mean
    inv_scale = lax.rsqrt(jnp.mean(centred * centred, axis=-1, keepdims=True) + NORM_EPS)
    unit_rows = centred * inv_scale
    return (unit_rows * gain_vec, unit_rows, inv_scale)


def norm_backward(gradient, unit_rows, inv_scale, gain_vec):
    scaled = gradient * gain_vec
    inner_sum = (
        scaled
        - jnp.mean(scaled, axis=-1, keepdims=True)
        - unit_rows * jnp.mean(scaled * unit_rows, axis=-1, keepdims=True)
    )
    return (inner_sum * inv_scale, jnp.sum(gradient * unit_rows, axis=0))


def attend_kernel(q_ref, k0, k1, v0, v1, o_ref, p_ref, li_ref, vext, *, scale):
    half = k0.shape[0]

    @pl.when(pl.program_id(1) == 0)
    def _():
        ones = jnp.ones((half, 128), BF)
        vext[0:half, 0:128] = v0[...]
        vext[half:, 0:128] = v1[...]
        vext[0:half, 128:256] = ones
        vext[half:, 128:256] = ones

    low = lax.broadcasted_iota(jnp.int32, q_ref.shape, 1) < 64
    q = q_ref[...]
    outs, sums = [], []
    factor = scale * math.log2(math.e)
    for h in range(2):
        picked = jnp.where(low if h == 0 else jnp.logical_not(low), q, jnp.zeros_like(q))
        s0 = mm(picked, k0[...], NT)
        s1 = mm(picked, k1[...], NT)
        peak = factor * jnp.maximum(
            jnp.max(s0, axis=1, keepdims=True), jnp.max(s1, axis=1, keepdims=True)
        )
        p_ref[h, :, 0:half] = jnp.exp2(s0 * factor - peak).astype(BF)
        p_ref[h, :, half:] = jnp.exp2(s1 * factor - peak).astype(BF)
        both = mm(p_ref[h], vext[...])
        outs.append(both[:, 0:128])
        sums.append(both[:, 128:256])
    inv = 1.0 / jnp.where(low, sums[0], sums[1])
    o_ref[...] = (jnp.where(low, outs[0], outs[1]) * inv).astype(BF)
    li_ref[...] = inv


def attend(qkv, kv_other, block):
    rows = qkv.shape[0]
    width = qkv.shape[1] // 3
    pairs = width // 128
    tile = pl.BlockSpec((block, 128), lambda h, i: (i, h))
    return pl.pallas_call(
        functools.partial(attend_kernel, scale=1.0 / math.sqrt(width // HEADS)),
        grid=(pairs, rows // block),
        in_specs=[
            tile,
            pl.BlockSpec((rows, 128), lambda h, i: (0, pairs + h)),
            pl.BlockSpec((rows, 128), lambda h, i: (0, h)),
            pl.BlockSpec((rows, 128), lambda h, i: (0, 2 * pairs + h)),
            pl.BlockSpec((rows, 128), lambda h, i: (0, pairs + h)),
        ],
        out_specs=[tile, pl.BlockSpec((2, block, 2 * rows), lambda h, i: (h, i, 0)), tile],
        out_shape=[
            jax.ShapeDtypeStruct((rows, width), BF),
            jax.ShapeDtypeStruct((HEADS, rows, 2 * rows), BF),
            jax.ShapeDtypeStruct((rows, width), F32),
        ],
        scratch_shapes=[pltpu.VMEM((2 * rows, 256), BF)],
        compiler_params=pltpu.CompilerParams(vmem_limit_bytes=VMEM_BYTES),
        cost_estimate=estimate(8 * 12 * rows * rows * 256, HEADS * rows * rows * 4, HEADS * rows * rows * 2),
        name="attend",
    )(qkv, qkv, kv_other, qkv, kv_other)


def attend_back_kernel(
    q_ref, k0, k1, v0, v1, o_ref, g_ref, li_ref, p_ref,
    dq_ref, own_ref, far_ref, vext, kacc, vacc, *, scale, steps,
):
    i = pl.program_id(1)
    half = k0.shape[0]
    lane = lax.broadcasted_iota(jnp.int32, q_ref.shape, 1)
    low = lane < 64

    @pl.when(i == 0)
    def _():
        ones = jnp.where(lax.broadcasted_iota(jnp.int32, (half, 128), 1) < 2, 1.0, 0.0).astype(BF)
        vext[0:half, 0:128] = v0[...]
        vext[half:, 0:128] = v1[...]
        vext[0:half, 128:256] = ones
        vext[half:, 128:256] = ones

    g = g_ref[...].astype(F32) * li_ref[...]
    gb = g.astype(BF)
    go = g * o_ref[...].astype(F32)
    qt = q_ref[...].T
    gt = gb.T
    dqs = []
    for h in range(2):
        mine = low if h == 0 else jnp.logical_not(low)
        delta = -jnp.sum(jnp.where(mine, go, 0.0), axis=1, keepdims=True)
        high = delta.astype(BF).astype(F32)
        extra = jnp.where(lane == 0, high, jnp.where(lane == 1, delta - high, 0.0)).astype(BF)
        gext = jnp.concatenate([jnp.where(mine, gb, jnp.zeros_like(gb)), extra], axis=1)
        p = p_ref[h]
        ds = (p.astype(F32) * mm(gext, vext[...], NT)).astype(BF)
        dqs.append(mm(ds[:, 0:half], k0[...]) + mm(ds[:, half:], k1[...]))
        rows = slice(64 * h, 64 * h + 64)
        dk = mm(qt[rows], ds)
        dv = mm(gt[rows], p)

        @pl.when(i == 0)
        def _():
            kacc[rows] = dk
            vacc[rows] = dv

        @pl.when(i > 0)
        def _():
            kacc[rows] += dk
            vacc[rows] += dv

    dq_ref[...] = (jnp.where(low, dqs[0], dqs[1]) * scale).astype(BF)

    @pl.when(i == steps - 1)
    def _():
        own_ref[0] = kacc[:, 0:half].T * scale
        own_ref[1] = vacc[:, 0:half].T
        far_ref[0] = (kacc[:, half:].T * scale).astype(BF)
        far_ref[1] = vacc[:, half:].T.astype(BF)


def attend_back(qkv, kv_other, mixed, grad, inv_sum, probs, block, first, count):
    rows = qkv.shape[0]
    width = qkv.shape[1] // 3
    pairs = width // 128
    steps = rows // block
    tile = pl.BlockSpec((block, 128), lambda h, i: (i, first + h))
    both = pl.BlockSpec((2, rows, 128), lambda h, i: (0, 0, h))
    return pl.pallas_call(
        functools.partial(attend_back_kernel, scale=1.0 / math.sqrt(width // HEADS), steps=steps),
        grid=(count, steps),
        in_specs=[
            tile,
            pl.BlockSpec((rows, 128), lambda h, i: (0, pairs + first + h)),
            pl.BlockSpec((rows, 128), lambda h, i: (0, first + h)),
            pl.BlockSpec((rows, 128), lambda h, i: (0, 2 * pairs + first + h)),
            pl.BlockSpec((rows, 128), lambda h, i: (0, pairs + first + h)),
            tile,
            tile,
            tile,
            pl.BlockSpec((2, block, 2 * rows), lambda h, i: (first + h, i, 0)),
        ],
        out_specs=[pl.BlockSpec((block, 128), lambda h, i: (i, h)), both, both],
        out_shape=[
            jax.ShapeDtypeStruct((rows, 128 * count), BF),
            jax.ShapeDtypeStruct((2, rows, 128 * count), F32),
            jax.ShapeDtypeStruct((2, rows, 128 * count), BF),
        ],
        scratch_shapes=[
            pltpu.VMEM((2 * rows, 256), BF),
            pltpu.VMEM((128, 2 * rows), F32),
            pltpu.VMEM((128, 2 * rows), F32),
        ],
        compiler_params=pltpu.CompilerParams(vmem_limit_bytes=VMEM_BYTES),
        cost_estimate=estimate(16 * 2 * count * rows * rows * 256, 2 * count * rows * rows * 4, 0),
        name="attend_back",
    )(qkv, qkv, kv_other, qkv, kv_other, mixed, grad, inv_sum, probs)


def grad_qkv_kernel(normed, *refs, count, with_out):
    grad_ref, dqkv_ref = refs[-2:]
    cols = dqkv_ref.shape[1]
    wide = cols // 3
    at = 0
    for n in range(count):
        dq, own, far = refs[n], refs[count + n], refs[2 * count + n]
        size = dq.shape[1]
        dqkv_ref[:, at : at + size] = dq[...]
        for m in range(2):
            start = (m + 1) * wide + at
            dqkv_ref[:, start : start + size] = (own[m] + far[m].astype(F32)).astype(BF)
        at += size
    grad_ref[:, 0:cols] = mm(normed[...].T, dqkv_ref[...]).astype(BF)
    if with_out:
        mixed, branch, small = refs[3 * count : 3 * count + 3]
        width = branch.shape[1]
        grad_ref[:, cols : cols + width] = mm(mixed[...].T, branch[...]).astype(BF)
        value = small[...]
        high = value.astype(BF).astype(F32)
        rest = jnp.zeros((SMALL - 2 * value.shape[0], value.shape[1]), F32)
        grad_ref[:, cols + width :] = jnp.concatenate([high, value - high, rest], axis=0).T.astype(BF)


def grad_qkv(normed, dqs, owns, fars, more=()):
    rows, width = normed.shape
    cols = 3 * sum(dq.shape[1] for dq in dqs)
    out_cols = cols + (more[1].shape[1] + SMALL if more else 0)
    return pl.pallas_call(
        functools.partial(grad_qkv_kernel, count=len(dqs), with_out=bool(more)),
        out_shape=[
            jax.ShapeDtypeStruct((width, out_cols), BF),
            jax.ShapeDtypeStruct((rows, cols), BF),
        ],
        compiler_params=pltpu.CompilerParams(vmem_limit_bytes=VMEM_BYTES),
        cost_estimate=estimate(2 * rows * width * out_cols, 8 * rows * out_cols),
        name="grad_qkv",
    )(normed, *dqs, *owns, *fars, *more)


GELU_A = math.sqrt(2.0 / math.pi)
GELU_B = 0.044715


def gelu_both(v):
    square = v * v
    t = jnp.tanh(v * (GELU_A + GELU_A * GELU_B * square))
    half = 0.5 + 0.5 * t
    slope = half + (0.5 * v) * (1.0 - t * t) * (GELU_A + 3 * GELU_A * GELU_B * square)
    return v * half, slope


def expert_kernel(
    which, x_in, dy_in, up_ref, down_ref, out_ref, back_ref, grad_ref,
    x, xt, dp, dpt, gate, out_acc, dx_acc, act, dhid, *, steps, pieces,
):
    f = pl.program_id(0)
    peers, cap = dy_in.shape[0], dy_in.shape[1]

    @pl.when(f == 0)
    def _():
        sent = [x_in[r, cap : cap + EXTRA, 0:cap].astype(F32) for r in range(peers)]
        gates = jnp.concatenate([g[0:1] + g[1:2] + g[2:3] for g in sent], axis=0).T
        for r in range(peers):
            at = slice(r * cap, (r + 1) * cap)
            x[at] = x_in[r, 0:cap, :]
            g = gates[:, r : r + 1]
            gate[at] = g
            dp[at] = (dy_in[r].astype(F32) * g).astype(BF)
        xt[...] = x[...].T
        dpt[...] = dp[...].T

    up = up_ref[0]
    down = down_ref[0]
    value, slope = gelu_both(mm(x[...], up))
    act[...] = value.astype(BF)
    dhid[...] = (mm(dp[...], down, NT) * slope).astype(BF)

    @pl.when(f == 0)
    def _():
        out_acc[...] = mm(act[...], down)
        dx_acc[...] = mm(dhid[...], up, NT)

    @pl.when(f > 0)
    def _():
        out_acc[...] += mm(act[...], down)
        dx_acc[...] += mm(dhid[...], up, NT)

    gup = mm(xt[...], dhid[...]).astype(BF)
    gdown = mm(dpt[...], act[...]).astype(BF)
    wide = gup.shape[1] // pieces
    for s in range(pieces):
        grad_ref[s, 0, 0] = gup[:, s * wide : (s + 1) * wide]
        grad_ref[s, 0, 1] = gdown[:, s * wide : (s + 1) * wide]

    @pl.when(f == steps - 1)
    def _():
        sums = []
        for r in range(peers):
            at = slice(r * cap, (r + 1) * cap)
            produced = out_acc[at].astype(BF).astype(F32)
            back_ref[r, 0:cap, :] = dx_acc[at].astype(BF)
            out_ref[r] = (produced * gate[at]).astype(BF)
            sums.append(jnp.sum(produced * dy_in[r].astype(F32), axis=1, keepdims=True))
        sums = jnp.concatenate(sums, axis=1).T
        for r in range(peers):
            put_extra(back_ref, r, cap, sums[r : r + 1])


def put_extra(ref, r, cap, row):
    width = ref.shape[2]
    high, mid, low = three_parts(row)
    line = lax.broadcasted_iota(jnp.int32, (EXTRA, cap), 0)
    full = jnp.where(
        line == 0, high.astype(F32), jnp.where(line == 1, mid.astype(F32), jnp.where(line == 2, low.astype(F32), 0.0))
    )
    ref[r, cap:, :] = jnp.concatenate([full, jnp.zeros((EXTRA, width - cap), F32)], axis=1).astype(BF)


def run_expert(which, part, x, dy, w_up, w_down, n_ctx, n_dp, chunk=768):
    peers, cap, width = x.shape[0], x.shape[1] - EXTRA, x.shape[2]
    mine = jax.ShapeDtypeStruct((peers, cap, width), BF)
    rows = peers * cap
    hidden = w_up.shape[-1]
    steps = hidden // chunk
    wide = hidden // (n_ctx * n_dp)
    pieces = chunk // wide
    per = n_dp // pieces
    full = lambda shape: pl.BlockSpec(shape, lambda f, j: (0,) * len(shape))
    return pl.pallas_call(
        functools.partial(expert_kernel, steps=steps, pieces=pieces),
        grid_spec=pltpu.PrefetchScalarGridSpec(
            num_scalar_prefetch=1,
            grid=(steps,),
            in_specs=[
                full(x.shape),
                pl.BlockSpec(mine.shape, lambda f, j: (0, part, 0)),
                pl.BlockSpec((1, width, chunk), lambda f, j: (j[0], 0, f)),
                pl.BlockSpec((1, chunk, width), lambda f, j: (j[0], f, 0)),
            ],
            out_specs=[
                full(mine.shape),
                full(x.shape),
                pl.BlockSpec((pieces, 1, 2, width, wide), lambda f, j: (f % per, f // per, 0, 0, 0)),
            ],
            scratch_shapes=[
                pltpu.VMEM((rows, width), BF),
                pltpu.VMEM((width, rows), BF),
                pltpu.VMEM((rows, width), BF),
                pltpu.VMEM((width, rows), BF),
                pltpu.VMEM((rows, 1), F32),
                pltpu.VMEM((rows, width), F32),
                pltpu.VMEM((rows, width), F32),
                pltpu.VMEM((rows, chunk), BF),
                pltpu.VMEM((rows, chunk), BF),
            ],
        ),
        out_shape=[
            mine,
            jax.ShapeDtypeStruct(x.shape, BF),
            jax.ShapeDtypeStruct((n_dp, n_ctx, 2, width, wide), BF),
        ],
        compiler_params=pltpu.CompilerParams(vmem_limit_bytes=VMEM_BYTES),
        cost_estimate=estimate(12 * rows * width * hidden, 8 * width * hidden, rows * hidden),
        name="expert",
    )(which, x, dy, w_up, w_down)


def seats(expert_ids, seat_order, expert_count, capacity, place_of):
    token_count = expert_ids.shape[0]
    places = jnp.arange(token_count, dtype=jnp.int32)
    earlier = (seat_order[:, None] < seat_order[None, :]) | (
        seat_order[:, None] == seat_order[None, :]
    ) & (places[:, None] < places[None, :])
    earlier = earlier.astype(BF)
    lane_ids = jnp.arange(expert_count, dtype=jnp.int32)
    first_hot = expert_ids[:, 0:1] == lane_ids[None, :]
    second_hot = expert_ids[:, 1:2] == lane_ids[None, :]
    both_hot = jnp.concatenate([first_hot, second_hot], axis=1).astype(BF)
    ahead = jnp.einsum("st,se->te", earlier, both_hot, preferred_element_type=F32)
    ahead_first = ahead[:, :expert_count]
    ahead_second = ahead[:, expert_count:] + jnp.sum(first_hot.astype(F32), axis=0)[None, :]
    rank_first = jnp.sum(jnp.where(first_hot, ahead_first, 0.0), axis=-1)
    rank_second = jnp.sum(jnp.where(second_hot, ahead_second, 0.0), axis=-1)

    def slot(picked, rank):
        at = rank.astype(jnp.int32)
        return jnp.where(at < capacity, place_of(picked) * capacity + at, -1)

    return (
        slot(expert_ids[:, 0], rank_first),
        slot(expert_ids[:, 1], rank_second),
        first_hot,
        second_hot,
    )


def three_parts(v):
    high = v.astype(BF)
    rest = v - high.astype(F32)
    mid = rest.astype(BF)
    return high, mid, (rest - mid.astype(F32)).astype(BF)


def seat_rows_kernel(t1, t2, *refs, parts):
    *gate_refs, rows_ref, out_ref = refs
    peers = out_ref.shape[0]
    cap = (out_ref.shape[1] - (EXTRA if gate_refs else 0)) // len(parts)
    tokens = t1.shape[1]

    def hot_of(t, block):
        ids = lax.broadcasted_iota(jnp.int32, (cap, tokens), 0) + block * cap
        return ids == t[...]

    if gate_refs:
        left1 = jnp.concatenate(three_parts(gate_refs[0][...]), axis=0)
        left2 = jnp.concatenate(three_parts(gate_refs[1][...]), axis=0)
    for r in range(peers):
        for n, part in enumerate(parts):
            first = hot_of(t1, part * peers + r)
            second = hot_of(t2, part * peers + r)
            hot = jnp.where(first | second, 1.0, 0.0).astype(BF)
            out_ref[r, n * cap : (n + 1) * cap, :] = mm(hot, rows_ref[...]).astype(BF)
            if gate_refs:
                got = mm(left1, jnp.where(first, 1.0, 0.0).astype(BF), NT) + mm(
                    left2, jnp.where(second, 1.0, 0.0).astype(BF), NT
                )
                put_extra(out_ref, r, cap, jnp.sum(got, axis=0, keepdims=True))


def seat_rows(t1, t2, rows, gates, parts, peers, cap):
    tokens, width = rows.shape
    per_peer = len(parts) * cap + (EXTRA if gates else 0)
    return pl.pallas_call(
        functools.partial(seat_rows_kernel, parts=parts),
        out_shape=jax.ShapeDtypeStruct((peers, per_peer, width), BF),
        compiler_params=pltpu.CompilerParams(vmem_limit_bytes=VMEM_BYTES),
        cost_estimate=estimate(2 * peers * per_peer * tokens * width, 4 * tokens * width),
        name="seat_rows",
    )(t1[None], t2[None], *[g[None] for g in gates], rows)


def rows_back(t1, t2, back, extra):
    tokens = t1.shape[0]
    total, place = None, 0
    firsts = jnp.zeros((tokens, 1), F32)
    seconds = firsts
    for ref in back:
        cap = ref.shape[1] - extra
        group = max(1, 512 // cap)
        for b in range(0, ref.shape[0], group):
            ids = lax.broadcasted_iota(jnp.int32, (tokens, group * cap), 1) + place
            place += group * cap
            first = ids == t1
            second = ids == t2
            hot = jnp.where(first | second, 1.0, 0.0).astype(BF)
            add = mm(hot, jnp.concatenate([ref[b + n, 0:cap, :] for n in range(group)], axis=0))
            total = add if total is None else total + add
            if extra:
                sent = [ref[b + n, cap:, 0:cap].astype(F32) for n in range(group)]
                dg = jnp.concatenate([g[0:1] + g[1:2] + g[2:3] for g in sent], axis=1)
                firsts += jnp.sum(jnp.where(first, dg, 0.0), axis=1, keepdims=True)
                seconds += jnp.sum(jnp.where(second, dg, 0.0), axis=1, keepdims=True)
    return total, firsts, seconds


def unseat_kernel(t1, t2, base, *refs):
    out_ref = refs[-1]
    total, _, _ = rows_back(t1[...], t2[...], refs[:-1], 0)
    out_ref[...] = (base[...] + total).astype(BF)


def unseat(t1, t2, base, parts, block=256):
    tokens, width = base.shape
    col = pl.BlockSpec((block, 1), lambda i: (i, 0))
    rows = pl.BlockSpec((block, width), lambda i: (i, 0))
    return pl.pallas_call(
        unseat_kernel,
        grid=(tokens // block,),
        in_specs=[col, col, rows] + [pl.BlockSpec(part.shape, lambda i: (0, 0, 0)) for part in parts],
        out_specs=rows,
        out_shape=jax.ShapeDtypeStruct((tokens, width), BF),
        compiler_params=pltpu.CompilerParams(vmem_limit_bytes=VMEM_BYTES),
        cost_estimate=estimate(4 * tokens * tokens * width, 8 * tokens * width),
        name="unseat",
    )(t1[:, None], t2[:, None], base, *parts)


def route_back_kernel(
    t1, t2, ids, probs, dy, middle, gain, w_router, w_out, *refs,
):
    dmiddle_ref, dbranch_ref, dmixed_ref, small_ref = refs[-4:]
    total, dg1, dg2 = rows_back(t1[...], t2[...], refs[:-4], EXTRA)
    p = probs[...]
    experts = p.shape[1]
    lane = lax.broadcasted_iota(jnp.int32, p.shape, 1)
    d_gates = jnp.where(lane == ids[:, 0:1], dg1, 0.0) + jnp.where(lane == ids[:, 1:2], dg2, 0.0)
    d_logits = p * (d_gates - jnp.sum(p * d_gates, axis=1, keepdims=True))
    d_routed = total
    for piece in three_parts(d_logits):
        d_routed = d_routed + mm(piece, w_router[...], NT)
    v = middle[...]
    centred = v - jnp.mean(v, axis=1, keepdims=True)
    inv = lax.rsqrt(jnp.mean(centred * centred, axis=1, keepdims=True) + NORM_EPS)
    unit = centred * inv
    routed = (unit * gain[...]).astype(BF)
    scaled = d_routed * gain[...]
    d_norm = inv * (
        scaled
        - jnp.mean(scaled, axis=1, keepdims=True)
        - unit * jnp.mean(scaled * unit, axis=1, keepdims=True)
    )
    d_middle = dy[...].astype(F32) + d_norm
    d_branch = d_middle.astype(BF)
    dmiddle_ref[...] = d_middle
    dbranch_ref[...] = d_branch
    dmixed_ref[...] = mm(d_branch, w_out[...], NT).astype(BF)
    to_router = 0.0
    for piece in three_parts(d_logits.T):
        to_router = to_router + mm(piece, routed)
    to_gain = jnp.sum(d_routed * unit, axis=0, keepdims=True)

    @pl.when(pl.program_id(0) == 0)
    def _():
        small_ref[...] = jnp.zeros_like(small_ref)

    small_ref[0:experts, :] += to_router
    small_ref[experts : experts + 1, :] += to_gain


def route_back(t1, t2, ids, probs, dy, middle, gain, w_router, w_out, parts, block=256):
    tokens, width = dy.shape
    experts = probs.shape[1]
    line = lambda cols: pl.BlockSpec((block, cols), lambda i: (i, 0))
    full = lambda a: pl.BlockSpec(a.shape, lambda i: (0,) * a.ndim)
    gain = gain[None]
    return pl.pallas_call(
        route_back_kernel,
        grid=(tokens // block,),
        in_specs=[
            line(1), line(1), line(2), line(experts), line(width), line(width),
            full(gain), full(w_router), full(w_out),
        ]
        + [full(part) for part in parts],
        out_specs=[
            line(width), line(width), line(width),
            pl.BlockSpec((experts + 8, width), lambda i: (0, 0)),
        ],
        out_shape=[
            jax.ShapeDtypeStruct((tokens, width), F32),
            jax.ShapeDtypeStruct((tokens, width), BF),
            jax.ShapeDtypeStruct((tokens, width), BF),
            jax.ShapeDtypeStruct((experts + 8, width), F32),
        ],
        compiler_params=pltpu.CompilerParams(vmem_limit_bytes=VMEM_BYTES),
        cost_estimate=estimate(6 * tokens * tokens * width, 20 * tokens * width),
        name="route_back",
    )(t1[:, None], t2[:, None], ids, probs, dy, middle, gain, w_router, w_out, *parts)


def swap(value):
    n = lax.axis_size("ctx")
    return lax.ppermute(value, "ctx", [(i, (i + 1) % n) for i in range(n)])


def exchange(value, axes):
    return lax.all_to_all(value, axes, 0, 0, tiled=True)


def shift(value, axis, by):
    n = lax.axis_size(axis)
    return lax.ppermute(value, axis, [(i, (i + by) % n) for i in range(n)])


def scatter_sum(x, axis):
    n = lax.axis_size(axis)
    me = lax.axis_index(axis)
    got = [
        shift(lax.dynamic_index_in_dim(x, lax.rem(me + s, n), 0, keepdims=False), axis, s)
        for s in range(1, n)
    ]
    total = lax.dynamic_index_in_dim(x, me, 0, keepdims=False).astype(F32)
    for piece in got:
        total = total + piece.astype(F32)
    return total.astype(BF)


def gather_back(x, axis):
    n = lax.axis_size(axis)
    return jnp.stack([x] + [shift(x, axis, s) for s in range(1, n)])


def sum_everywhere(value):
    part = value
    for axis in ("ctx", "dp", "expert"):
        n = lax.axis_size(axis)
        part = scatter_sum(part.reshape(n, part.shape[0] // n, value.shape[1]), axis)
    full = gather_back(gather_back(part, "expert"), "dp")
    return full, swap(full)


def assemble_kernel(at, w_ref, *refs, groups, spans):
    ins, outs = refs[: 2 * groups], refs[2 * groups :]
    here, me = at[0], at[2]
    core = pl.program_id(0)
    owners, rows = ins[0].shape[1], ins[0].shape[2]
    for z in range(owners):
        back = lax.rem(me + owners - z, owners)
        for mine, other, span in zip(ins[:groups], ins[groups:], spans):
            piece = jnp.where(core == here, mine[0, back].astype(F32), other[0, back].astype(F32))
            for src, which, dst, size in span:
                outs[which][z * rows : (z + 1) * rows, dst : dst + size] = piece[:, src : src + size]
    outs[-1][...] = jnp.sum(outs[0][...] * w_ref[...].astype(F32), axis=1, keepdims=True)


def assemble(sums, spans, widths, w_qkv):
    n_dp, owners, rows, _ = sums[0][0].shape
    n_ctx = lax.axis_size("ctx")
    block = owners * rows
    height = n_ctx * n_dp * block
    at = jnp.stack([lax.axis_index(axis) for axis in ("ctx", "dp", "expert")]).astype(jnp.int32)
    back = lambda c, d, at: ((at[1] + n_dp - d) % n_dp, 0, 0, 0)
    line = lambda cols: pl.BlockSpec((block, cols), lambda c, d, at: (c * n_dp + d, 0))
    arrays = [full for full, _ in sums] + [other for _, other in sums]
    widths = [*widths, 1]
    return pl.pallas_call(
        functools.partial(assemble_kernel, groups=len(sums), spans=spans),
        grid_spec=pltpu.PrefetchScalarGridSpec(
            num_scalar_prefetch=1,
            grid=(n_ctx, n_dp),
            in_specs=[line(w_qkv.shape[1])] + [pl.BlockSpec((1,) + full.shape[1:], back) for full in arrays],
            out_specs=[line(cols) for cols in widths],
        ),
        out_shape=[jax.ShapeDtypeStruct((height, cols), F32) for cols in widths],
        compiler_params=pltpu.CompilerParams(vmem_limit_bytes=VMEM_BYTES),
        cost_estimate=estimate(height * 2304, 12 * height * 2304),
        name="assemble",
    )(at, w_qkv, *arrays)


def spread_kernel(at, *refs, parts):
    mine, other = refs[:parts], refs[parts : 2 * parts]
    up_ref, down_ref = refs[2 * parts :]
    j = pl.program_id(0)
    for part in range(parts):
        for src, kept in ((mine, True), (other, False)):

            @pl.when((j % parts == part) & ((j // parts == at[0]) == kept))
            def _():
                value = src[part][0] if kept else src[part]
                up_ref[0] = value[0].astype(F32)
                down_ref[0] = value[1].astype(F32).T


def spread(summed):
    parts = len(summed)
    n_ctx, _, width, cols = summed[0].shape
    here = lax.axis_index("ctx")
    other = [swap(lax.dynamic_index_in_dim(s, 1 - here, 0, keepdims=False)) for s in summed]
    mine = pl.BlockSpec((1, 2, width, cols), lambda j, at: (at[0], 0, 0, 0))
    return pl.pallas_call(
        functools.partial(spread_kernel, parts=parts),
        grid_spec=pltpu.PrefetchScalarGridSpec(
            num_scalar_prefetch=1,
            grid=(n_ctx * parts,),
            in_specs=[mine] * parts + [pl.BlockSpec((2, width, cols), lambda j, at: (0, 0, 0))] * parts,
            out_specs=[
                pl.BlockSpec((1, width, cols), lambda j, at: (j, 0, 0)),
                pl.BlockSpec((1, cols, width), lambda j, at: (j, 0, 0)),
            ],
        ),
        out_shape=[
            jax.ShapeDtypeStruct((n_ctx * parts, width, cols), F32),
            jax.ShapeDtypeStruct((n_ctx * parts, cols, width), F32),
        ],
        compiler_params=pltpu.CompilerParams(vmem_limit_bytes=VMEM_BYTES),
        cost_estimate=estimate(width * cols, 24 * parts * n_ctx * width * cols),
        name="spread",
    )(here.astype(jnp.int32)[None], *summed, *other)


def after(value, *others):
    return lax.optimization_barrier((value, others))[0]


def body(
    tokens,
    cotangent,
    router_noise,
    expert_ids,
    seat_order,
    gain_attn,
    w_qkv,
    w_out,
    gain_moe,
    w_router,
    w_up,
    w_down,
):
    image_count, half_len, width = tokens.shape
    rows = image_count * half_len
    expert_count = router_noise.shape[-1]
    n_owner = lax.axis_size("expert")
    n_ctx = lax.axis_size("ctx")
    n_dp = lax.axis_size("dp")
    here = lax.axis_index("ctx")
    per_device = w_up.shape[0] // n_ctx
    capacity = (2 * rows + expert_count - 1) // expert_count
    peers = n_owner * n_ctx
    to_owner = ("expert", "ctx")

    def place_of(e):
        return (e % per_device) * peers + e // per_device

    t1, t2, first_hot, second_hot = seats(
        expert_ids.reshape(rows, 2), seat_order.reshape(rows), expert_count, capacity, place_of
    )
    dy_b = cotangent.reshape(rows, width)
    every = tuple(range(per_device))
    dy_slots = seat_rows(t1, t2, dy_b, (), every, peers, capacity)
    dy_got = exchange(dy_slots, to_owner)

    tokens_f = after(tokens, dy_slots).reshape(rows, width).astype(F32)
    normed_a, unit_a, inv_a = norm_forward(tokens_f, gain_attn)
    normed_ab = normed_a.astype(BF)
    qkv_b = mm(normed_ab, w_qkv).astype(BF)
    kv_other = swap(qkv_b[:, width:])
    mixed_b, probs, inv_sum = attend(qkv_b, kv_other, 512)

    middle = tokens_f + mm(mixed_b, w_out)
    normed_m, _, _ = norm_forward(middle, gain_moe)
    routed_b = normed_m.astype(BF)
    logits = mm(routed_b, w_router) + router_noise.reshape(rows, expert_count)
    gate_probs = jax.nn.softmax(logits, axis=-1)
    gate_first = jnp.sum(jnp.where(first_hot, gate_probs, 0.0), axis=-1)
    gate_second = jnp.sum(jnp.where(second_hot, gate_probs, 0.0), axis=-1)

    gates = (gate_first, gate_second)
    sent = [seat_rows(t1, t2, routed_b, gates, (part,), peers, capacity) for part in every]
    sent[0], dy_got = lax.optimization_barrier((sent[0], dy_got))
    x_next = exchange(sent[0], to_owner)
    out_parts, dx_back, summed = [], [], []
    for part in every:
        which = (here * per_device + part).astype(jnp.int32)[None]
        x = x_next
        if part + 1 < per_device:
            x, following = lax.optimization_barrier((x, sent[part + 1]))
            x_next = exchange(following, to_owner)
        out, dx, grads = run_expert(which, part, x, dy_got, w_up, w_down, n_ctx, n_dp)
        out_parts.append(out)
        if part + 1 < per_device:
            dx, x_next, grads = lax.optimization_barrier((dx, x_next, grads))
        if dx_back:
            dx, dx_back[-1], grads = lax.optimization_barrier((dx, dx_back[-1], grads))
        dx_back.append(exchange(dx, to_owner))
        summed.append(
            lax.psum_scatter(
                grads.reshape(-1, grads.shape[-1]), "dp", scatter_dimension=0, tiled=True
            ).reshape(grads.shape[1:])
        )
    out_parts, dx_back = lax.optimization_barrier((out_parts, dx_back))

    d_middle, d_branch_b, d_mixed_b, small = route_back(
        t1, t2, expert_ids.reshape(rows, 2), gate_probs, dy_b, middle, gain_moe, w_router, w_out, dx_back
    )

    pairs = width // 128
    cut = pairs - pairs // 3
    groups = [(0, cut), (cut, pairs - cut)]
    d_normed_a = 0.0
    qkv_sums, spans, returned = [], [], []
    for n, (first, count) in enumerate(groups):
        returned.append(exchange(out_parts[n], to_owner) if n < per_device else None)
        dq, own, far = attend_back(
            qkv_b, kv_other, mixed_b, d_mixed_b, inv_sum, probs, 512, first, count
        )
        if n == 0:
            far, own, returned[0], d_mixed_b = lax.optimization_barrier(
                (far, own, returned[0], d_mixed_b)
            )
            out_parts[1:] = after(out_parts[1:], returned[0])
        if n == 1:
            far, returned, summed = lax.optimization_barrier((far, returned, summed))
        more = (mixed_b, d_branch_b, small) if n == 0 else ()
        grad, d_qkv = grad_qkv(normed_ab, [dq], [own], [swap(far)], more)
        qkv_sums.append(sum_everywhere(grad))
        start, wide = 128 * first, 128 * count
        spans.append([(m * wide, 0, m * width + start, wide) for m in range(3)])
        if n == 0:
            spans[0] += [(3 * wide, 1, 0, width), (3 * wide + width, 2, 0, SMALL)]
        columns = [w_qkv[:, m * width + start : m * width + start + wide] for m in range(3)]
        d_normed_a = d_normed_a + mm(d_qkv, jnp.concatenate(columns, axis=1), NT)
    returned += [exchange(part, to_owner) for part in out_parts[len(groups) :]]
    d_tokens_norm, _ = norm_backward(d_normed_a, unit_a, inv_a, gain_attn)
    d_tokens = d_middle + d_tokens_norm

    result = unseat(t1, t2, middle, returned)
    grad_up, grad_down = spread(summed)

    grad_w_qkv, grad_w_out, small_sum, gain_sum = assemble(
        qkv_sums, spans, (3 * width, width, SMALL), w_qkv
    )
    n_small = small.shape[0]
    small_sum = small_sum[:, :n_small] + small_sum[:, n_small : 2 * n_small]
    return (
        result.reshape(image_count, half_len, width),
        d_tokens.reshape(image_count, half_len, width),
        gain_sum[:, 0] / gain_attn,
        grad_w_qkv,
        grad_w_out,
        small_sum[:, expert_count],
        small_sum[:, :expert_count],
        grad_up,
        grad_down,
    )


def solution(mesh):
    placed = (
        P(("expert", "dp"), "ctx", None),
        P(("expert", "dp"), "ctx", None),
        P(("expert", "dp"), "ctx", None),
        P(("expert", "dp"), "ctx", None),
        P(("expert", "dp"), "ctx"),
        P(),
        P(),
        P(),
        P(),
        P(),
        P("expert", None, None),
        P("expert", None, None),
    )
    return jax.shard_map(
        body,
        mesh=mesh,
        in_specs=placed,
        out_specs=(
            P(("expert", "dp"), "ctx", None),
            P(("expert", "dp"), "ctx", None),
            P(),
            P(),
            P(),
            P(),
            P(),
            P("expert", None, ("ctx", "dp")),
            P("expert", ("ctx", "dp"), None),
        ),
        check_vma=False,
    )
```

time: 1520 us -> 565 us (0.37)
  waiting for transfers between devices: 615 us -> 95.6 us
  matrix products: 441 us -> 16.5 us
  Pallas kernels: 0 us -> 269 us
  blocking collectives: 263 us -> 44.9 us
  other arithmetic: 129 us -> 23.7 us
  starting transfers between devices: 5.03 us -> 64.5 us
  local copies, waits for them, and re-layouts: 44.3 us -> 27.4 us
    reduce_scatter x4 -> x2, waiting for transfers between devices: 459 us -> 0.04 us  [body(): lax.psum_scatter(grads.reshape(-1, grads.shape[-1]), 'dp', scatter_dimens...]
    dot_general x29 -> x6, matrix products: 441 us -> 16.5 us  [the longest x5 14.7 us: mm(): return lax.dot_general(left, right, dims, preferred_element_type=F32)]
    pallas_call x0 -> x14, Pallas kernels: none -> 269 us  [the longest x2 79.7 us: run_expert(): pl.pallas_call(functools.partial(expert_kernel, steps=steps, pieces=piece...]
    all_to_all x3 -> x1, blocking collectives: 223 us -> 44.9 us  [exchange(): return lax.all_to_all(value, axes, 0, 0, tiled=True)]
    psum x1 -> x0, waiting for transfers between devices: 80.9 us -> none  [body(): lax.psum((d_gain_attn, d_w_qkv, d_w_out, d_gain_moe, d_w_router), ('exper...]
    convert_element_type x2 -> x10, other arithmetic: 78.8 us -> 6.11 us  [the longest x6 5.12 us: scatter_sum(): return total.astype(BF)]
    ppermute x0 -> x33, waiting for transfers between devices: none -> 55.8 us  [the longest x26 51.4 us: shift(): return lax.ppermute(value, axis, [(i, (i + by) % n) for i in range(n)])]
    psum x1 -> x0, blocking collectives: 40.4 us -> none  [body(): lax.psum((d_gain_attn, d_w_qkv, d_w_out, d_gain_moe, d_w_router), ('exper...]
  transfers between devices with their start and end apart: 8 -> 41, of which waited for: 5 -> 14; matrix products, arithmetic and copies ran while one was open for 24% -> 7% of each run, Pallas kernels for 0% -> 45%
where the time goes in v1:
time: 565 us; the launch traced here: 557 us
  Pallas kernels  269 us (48%)
  waiting for transfers between devices  95.6 us (17%)
  starting transfers between devices  64.5 us (11%)
  blocking collectives  44.9 us (8%)
  local copies, waits for them, and re-layouts  27.4 us (5%)
  other arithmetic  23.7 us (4%)
  matrix products  16.5 us (3%)
  between operations  15.2 us (3%)
    pallas_call x2, Pallas kernels, run_expert(): pl.pallas_call(functools.partial(expert_kernel, steps=steps, pieces=piece...  79.7 us
    pallas_call x2, Pallas kernels, attend_back(): pl.pallas_call(functools.partial(attend_back_kernel, scale=1.0 / math.sqr...  65.2 us
    ppermute x26, waiting for transfers between devices, shift(): return lax.ppermute(value, axis, [(i, (i + by) % n) for i in range(n)])  51.4 us
    pallas_call x1, Pallas kernels, attend(): pl.pallas_call(functools.partial(attend_kernel, scale=1.0 / math.sqrt(wid...  48.2 us
    all_to_all x1, blocking collectives, exchange(): return lax.all_to_all(value, axes, 0, 0, tiled=True)  44.9 us
    all_to_all x6, waiting for transfers between devices, exchange(): return lax.all_to_all(value, axes, 0, 0, tiled=True)  39.8 us
    ppermute x26, starting transfers between devices, shift(): return lax.ppermute(value, axis, [(i, (i + by) % n) for i in range(n)])  35.8 us
    all_to_all x6, starting transfers between devices, exchange(): return lax.all_to_all(value, axes, 0, 0, tiled=True)  27 us
  transfers between devices with their start and end apart: 41, of which 14 were waited for; matrix products, arithmetic and copies ran while one was open for 7% of the time, Pallas kernels for 45%

profile of v1, /device:TPU:0, one launch (start us, length us, event | category | flops | bytes accessed | tf_op | source)
XLA Modules:
  0.0 557.0 jit_solution(7649055055515753586)
XLA Ops:
  13.4 6.7 %seat_rows.3 = bf16[8,256,768]{2,1,0:T(8,128)(2,1)} custom-call(s32[1,1024]{1,0:T(1,128)} %compare_select_fusion.1.t1, s32[1,1024]{1,0:T(1,128)} %compare_select_fusion.t2, bf16[1024,768]{1,0:T(8,128)(2,1)} %bitcast.145), custom_call_target="tpu_custom_call" | custom-call | flops 805306368 | bytes 786432 | tf_op jit(solution)/shard_map/seat_rows/pallas_call | solution.py:435
  22.4 4.0 convolution_convert_fusion.q_ref.k0.v0
  30.0 6.2 %all-to-all-start = ((bf16[8,256,768]{2,1,0:T(8,128)(2,1)}), bf16[8,256,768]{2,1,0:T(8,128)(2,1)}, u32[]{:S(2)}, u32[]{:S(2)}) async-start(bf16[8,256,768]{2,1,0:T(8,128)(2,1)} %seat_rows.3), calls=%async_computation | async-start | bytes 6291456 | tf_op jit(solution)/shard_map/all_to_all | solution.py:568
  38.9 48.2 %attend.1 = (bf16[1024,768]{1,0:T(8,128)(2,1)}, bf16[12,1024,2048]{2,1,0:T(8,128)(2,1)}, f32[1024,768]{1,0:T(8,128)}) custom-call(bf16[1024,2304]{1,0:T(8,128)(2,1)} %copy-done, bf16[1024,2304]{1,0:T(8,128)(2,1)} %copy-done, bf16[1024,1536]{1,0:T(8,128)(2,1)} %copy-done.1, bf16[1024,2304]{1,0:T(8,128)(2,1)} %copy-done, bf16[1024,1536]{1,0:T(8,128)(2,1)} %copy-done.1), custom_call_target="tpu_custom_call" | custom-call | flops 6442450944 | bytes 12582912 | tf_op jit(solution)/shard_map/attend/pallas_call | solution.py:85
  87.1 3.8 fusion.87
  96.9 5.6 %seat_rows.4 = bf16[8,136,768]{2,1,0:T(8,128)(2,1)} custom-call(s32[1,1024]{1,0:T(1,128)} %compare_select_fusion.1.t1, s32[1,1024]{1,0:T(1,128)} %compare_select_fusion.t2, f32[1,1024]{1,0:T(1,128)} %bitcast.175, f32[1,1024]{1,0:T(1,128)} %bitcast.173, bf16[1024,768]{1,0:T(8,128)(2,1)} %copy-done.3), custom_call_target="tpu_custom_call" | custom-call | flops 427819008 | bytes 786432 | tf_op jit(solution)/shard_map/seat_rows/pallas_call | solution.py:435
  102.5 5.4 all-to-all-done.dy_in
  107.8 3.6 all-to-all-start.1
  111.4 5.6 %seat_rows.5 = bf16[8,136,768]{2,1,0:T(8,128)(2,1)} custom-call(s32[1,1024]{1,0:T(1,128)} %compare_select_fusion.1.t1, s32[1,1024]{1,0:T(1,128)} %compare_select_fusion.t2, f32[1,1024]{1,0:T(1,128)} %bitcast.176, f32[1,1024]{1,0:T(1,128)} %bitcast.174, bf16[1024,768]{1,0:T(8,128)(2,1)} %copy-done.3), custom_call_target="tpu_custom_call" | custom-call | flops 427819008 | bytes 786432 | tf_op jit(solution)/shard_map/seat_rows/pallas_call | solution.py:435
  117.0 34.3 %all-to-all-done.1.x_in = bf16[8,136,768]{2,1,0:T(8,128)(2,1)S(1)} async-done(((bf16[8,136,768]{2,1,0:T(8,128)(2,1)}), bf16[8,136,768]{2,1,0:T(8,128)(2,1)S(1)}, u32[]{:S(2)}, u32[]{:S(2)}) %all-to-all-start.1) | async-done | bytes 1671200 | tf_op jit(solution)/shard_map/all_to_all | solution.py:568
  151.3 3.6 all-to-all-start.2
  155.2 39.5 %expert.2 = (bf16[8,128,768]{2,1,0:T(8,128)(2,1)}, bf16[8,136,768]{2,1,0:T(8,128)(2,1)}, bf16[4,2,2,768,384]{4,3,2,1,0:T(8,128)(2,1)}) custom-call(s32[1]{0:T(128)} %bitcast.9.which, bf16[8,136,768]{2,1,0:T(8,128)(2,1)} %copy-done.13, bf16[8,256,768]{2,1,0:T(8,128)(2,1)} %all-to-all-done.dy_in, bf16[4,768,3072]{2,1,0:T(8,128)(2,1)} %up_ref.3, ...), custom_call_target="tpu_custom_call" | custom-call | flops 7247757312 | bytes 4718592 | tf_op jit(solution)/shard_map/expert/pallas_call | solution.py:331
  195.9 4.9 all-to-all-start.3
  201.2 40.2 %expert.3 = (bf16[8,128,768]{2,1,0:T(8,128)(2,1)}, bf16[8,136,768]{2,1,0:T(8,128)(2,1)}, bf16[4,2,2,768,384]{4,3,2,1,0:T(8,128)(2,1)}) custom-call(s32[1]{0:T(128)} %bitcast.12.which, bf16[8,136,768]{2,1,0:T(8,128)(2,1)} %copy-done.12, bf16[8,256,768]{2,1,0:T(8,128)(2,1)} %all-to-all-done.dy_in, bf16[4,768,3072]{2,1,0:T(8,128)(2,1)} %up_ref.3, ...), custom_call_target="tpu_custom_call" | custom-call | flops 7247757312 | bytes 4718592 | tf_op jit(solution)/shard_map/expert/pallas_call | solution.py:331
  243.5 44.9 %all_to_all.35.refs_1_ = bf16[8,136,768]{2,1,0:T(8,128)(2,1)} all-to-all(bf16[8,136,768]{2,1,0:T(8,128)(2,1)S(1)} %copy-done.23), channel_id=1, replica_groups=mesh['expert'=4,'ctx'=2,'dp'=4] {'expert','ctx'}, dimensions={0} | all-to-all | bytes 3342336 | tf_op jit(solution)/shard_map/all_to_all | solution.py:568
  288.4 3.9 all-to-all-start.5
  296.1 17.1 %route_back.1 = (f32[1024,768]{1,0:T(8,128)}, bf16[1024,768]{1,0:T(8,128)(2,1)}, bf16[1024,768]{1,0:T(8,128)(2,1)}, f32[24,768]{1,0:T(8,128)}) custom-call(s32[1024,1]{1,0:T(8,128)} %get-tuple-element.166.t1, s32[1024,1]{1,0:T(8,128)} %get-tuple-element.165.t2, s32[1024,2]{1,0:T(8,128)} %bitcast.139, f32[1024,16]{1,0:T(8,128)} %get-tuple-element.152.probs, ...), custom_call_target="tpu_custom_call" | custom-call | flops 1207959552 | bytes 3932160 | tf_op jit(solution)/shard_map/route_back/pallas_call | solution.py:538
  313.3 42.2 %attend_back.2 = (bf16[1024,512]{1,0:T(8,128)(2,1)}, f32[2,1024,512]{2,1,0:T(8,128)}, bf16[2,1024,512]{2,1,0:T(8,128)(2,1)}) custom-call(bf16[1024,2304]{1,0:T(8,128)(2,1)} %copy-done, bf16[1024,2304]{1,0:T(8,128)(2,1)} %copy-done, bf16[1024,1536]{1,0:T(8,128)(2,1)} %copy-done.1, bf16[1024,2304]{1,0:T(8,128)(2,1)} %copy-done, bf16[1024,1536]{1,0:T(8,128)(2,1)} %copy-done.1, ...), custom_call_target="tpu_custom_call" | custom-call | flops 8589934592 | bytes 8388608 | tf_op jit(solution)/shard_map/attend_back/pallas_call | solution.py:171
  355.7 4.3 collective-permute-done.1.refs_2_
  360.1 10.6 %grad_qkv.2 = (bf16[768,2432]{1,0:T(8,128)(2,1)}, bf16[1024,1536]{1,0:T(8,128)(2,1)}) custom-call(bf16[1024,768]{1,0:T(8,128)(2,1)} %copy-done.10, bf16[1024,512]{1,0:T(8,128)(2,1)} %get-tuple-element.97.refs_0_, f32[2,1024,512]{2,1,0:T(8,128)} %get-tuple-element.98.refs_1_, bf16[2,1024,512]{2,1,0:T(8,128)(2,1)} %collective-permute-done.1.refs_2_, ...), custom_call_target="tpu_custom_call" | custom-call | flops 956301312 | bytes 4980736 | tf_op jit(solution)/shard_map/grad_qkv/pallas_call | solution.py:230
  372.6 4.9 all-to-all-start.6
  385.5 13.2 %collective-permute-done.4 = bf16[96,2432]{1,0:T(8,128)(2,1)S(1)} collective-permute-done((bf16[96,2432]{1,0:T(8,128)(2,1)}, bf16[96,2432]{1,0:T(8,128)(2,1)S(1)}, u32[]{:S(2)}, u32[]{:S(2)}) %collective-permute-start.4) | collective-permute-done | bytes 466976 | tf_op jit(solution)/shard_map/ppermute | solution.py:573
  398.8 9.0 %collective-permute-done.6 = bf16[96,2432]{1,0:T(8,128)(2,1)S(1)} collective-permute-done((bf16[96,2432]{1,0:T(8,128)(2,1)}, bf16[96,2432]{1,0:T(8,128)(2,1)S(1)}, u32[]{:S(2)}, u32[]{:S(2)}) %collective-permute-start.6) | collective-permute-done | bytes 466976 | tf_op jit(solution)/shard_map/ppermute | solution.py:573
  413.3 23.0 %attend_back.3 = (bf16[1024,256]{1,0:T(8,128)(2,1)}, f32[2,1024,256]{2,1,0:T(8,128)}, bf16[2,1024,256]{2,1,0:T(8,128)(2,1)}) custom-call(bf16[1024,2304]{1,0:T(8,128)(2,1)} %copy-done, bf16[1024,2304]{1,0:T(8,128)(2,1)} %copy-done, bf16[1024,1536]{1,0:T(8,128)(2,1)} %copy-done.1, bf16[1024,2304]{1,0:T(8,128)(2,1)} %copy-done, bf16[1024,1536]{1,0:T(8,128)(2,1)} %copy-done.1, ...), custom_call_target="tpu_custom_call" | custom-call | flops 4294967296 | bytes 4194304 | tf_op jit(solution)/shard_map/attend_back/pallas_call | solution.py:171
  443.2 8.2 %collective-permute-done.11 = bf16[24,2432]{1,0:T(8,128)(2,1)S(1)} collective-permute-done((bf16[24,2432]{1,0:T(8,128)(2,1)S(1)}, bf16[24,2432]{1,0:T(8,128)(2,1)S(1)}, u32[]{:S(2)}, u32[]{:S(2)}) %collective-permute-start.11) | collective-permute-done | bytes 116768 | tf_op jit(solution)/shard_map/ppermute | solution.py:573
  457.7 5.1 grad_qkv.3
  465.0 10.0 %collective-permute-done.14 = bf16[4,24,2432]{2,1,0:T(8,128)(2,1)} collective-permute-done((bf16[4,24,2432]{2,1,0:T(8,128)(2,1)}, bf16[4,24,2432]{2,1,0:T(8,128)(2,1)}, u32[]{:S(2)}, u32[]{:S(2)}) %collective-permute-start.14) | collective-permute-done | bytes 466976 | tf_op jit(solution)/shard_map/ppermute | solution.py:573
  488.9 3.7 collective-permute-start.22
  492.9 7.8 %unseat.1 = bf16[1024,768]{1,0:T(8,128)(2,1)} custom-call(s32[1024,1]{1,0:T(8,128)} %get-tuple-element.166.t1, s32[1024,1]{1,0:T(8,128)} %get-tuple-element.165.t2, f32[1024,768]{1,0:T(8,128)} %copy-done.2, bf16[8,128,768]{2,1,0:T(8,128)(2,1)} %copy-done.15, bf16[8,128,768]{2,1,0:T(8,128)(2,1)} %all-to-all-done.6.refs_1_), custom_call_target="tpu_custom_call" | custom-call | flops 805306368 | bytes 1572864 | tf_op jit(solution)/shard_map/unseat/pallas_call | solution.py:478
  518.1 4.7 collective-permute-done.26
  527.2 6.4 %spread.1 = (f32[4,768,384]{2,1,0:T(8,128)}, f32[4,384,768]{2,1,0:T(8,128)}) custom-call(s32[1]{0:T(128)} %bitcast.19.at, bf16[2,2,768,384]{3,2,1,0:T(8,128)(2,1)} %bitcast.147, bf16[2,2,768,384]{3,2,1,0:T(8,128)(2,1)} %bitcast.149, bf16[2,768,384]{2,1,0:T(8,128)(2,1)} %collective-permute-done.31.refs_2_, bf16[2,768,384]{2,1,0:T(8,128)(2,1)} %copy-done.24), custom_call_target="tpu_custom_call" | custom-call | flops 73728 | bytes 7077888 | tf_op jit(solution)/shard_map/spread/pallas_call | solution.py:662
  533.7 11.3 %assemble.1 = (f32[768,2304]{1,0:T(8,128)}, f32[768,768]{1,0:T(8,128)}, f32[768,128]{1,0:T(8,128)}, f32[768,1]{1,0:T(8,128)}) custom-call(s32[3]{0:T(128)} %pad_add_fusion.at, bf16[768,2304]{1,0:T(8,128)(2,1)} %w_ref.1, bf16[4,4,24,2432]{3,2,1,0:T(8,128)(2,1)} %copy-done.11, bf16[4,4,24,768]{3,2,1,0:T(8,128)(2,1)} %copy-done.19, ...), custom_call_target="tpu_custom_call" | custom-call | flops 442368 | bytes 5308416 | tf_op jit(solution)/shard_map/assemble/pallas_call | solution.py:627
  (205 shorter events, 100.1 us)
Async XLA Ops:
  29.5 7.7 %collective-permute-start = (bf16[1024,1536]{1,0:T(8,128)(2,1)}, bf16[1024,1536]{1,0:T(8,128)(2,1)S(1)}, u32[]{:S(2)}, u32[]{:S(2)}) collective-permute-start(bf16[1024,1536]{1,0:T(8,128)(2,1)} %slice.66), channel_id=1, source_target_pairs={{0,4},{4,0},{1,5},{5,1},{2,6},{6,2},{3,7},{7,3},{8,12},{12,8},{9,1... | collective-permute-start | bytes 9437192 | tf_op jit(solution)/shard_map/ppermute | solution.py:564
  30.0 77.8 %all-to-all-start = ((bf16[8,256,768]{2,1,0:T(8,128)(2,1)}), bf16[8,256,768]{2,1,0:T(8,128)(2,1)}, u32[]{:S(2)}, u32[]{:S(2)}) async-start(bf16[8,256,768]{2,1,0:T(8,128)(2,1)} %seat_rows.3), calls=%async_computation | async-start | bytes 6291456 | tf_op jit(solution)/shard_map/all_to_all | solution.py:568
  107.8 43.5 %all-to-all-start.1 = ((bf16[8,136,768]{2,1,0:T(8,128)(2,1)}), bf16[8,136,768]{2,1,0:T(8,128)(2,1)S(1)}, u32[]{:S(2)}, u32[]{:S(2)}) async-start(bf16[8,136,768]{2,1,0:T(8,128)(2,1)} %seat_rows.4), calls=%async_computation.1 | async-start | bytes 3342336 | tf_op jit(solution)/shard_map/all_to_all | solution.py:568
  151.3 43.5 %all-to-all-start.2 = ((bf16[8,136,768]{2,1,0:T(8,128)(2,1)}), bf16[8,136,768]{2,1,0:T(8,128)(2,1)S(1)}, u32[]{:S(2)}, u32[]{:S(2)}) async-start(bf16[8,136,768]{2,1,0:T(8,128)(2,1)} %seat_rows.5), calls=%async_computation.2 | async-start | bytes 3342336 | tf_op jit(solution)/shard_map/all_to_all | solution.py:568
  154.9 281.5 %reduce-scatter.3.cloned.1.call-start = ((), (), s32[]{:S(2)}) async-start(), calls=%async_computation.9 | async-start | bytes 11796480 | tf_op jit(solution)/shard_map/reduce_scatter | solution.py:758
  195.9 45.5 %all-to-all-start.3 = ((bf16[8,136,768]{2,1,0:T(8,128)(2,1)}), bf16[8,136,768]{2,1,0:T(8,128)(2,1)S(1)}, u32[]{:S(2)}, u32[]{:S(2)}) async-start(bf16[8,136,768]{2,1,0:T(8,128)(2,1)} %get-tuple-element.75), calls=%async_computation.3 | async-start | bytes 3342336 | tf_op jit(solution)/shard_map/all_to_all | solution.py:568
  200.8 235.6 %reduce-scatter.5.cloned.1.call-start = ((), (), s32[]{:S(2)}) async-start(), calls=%async_computation.10 | async-start | bytes 11796480 | tf_op jit(solution)/shard_map/reduce_scatter | solution.py:758
  288.4 67.1 %all-to-all-start.5 = ((bf16[8,128,768]{2,1,0:T(8,128)(2,1)}), bf16[8,128,768]{2,1,0:T(8,128)(2,1)S(1)}, u32[]{:S(2)}, u32[]{:S(2)}) async-start(bf16[8,128,768]{2,1,0:T(8,128)(2,1)} %get-tuple-element.86), calls=%async_computation.5 | async-start | bytes 3145728 | tf_op jit(solution)/shard_map/all_to_all | solution.py:568
  372.6 63.7 %all-to-all-start.6 = ((bf16[8,128,768]{2,1,0:T(8,128)(2,1)}), bf16[8,128,768]{2,1,0:T(8,128)(2,1)}, u32[]{:S(2)}, u32[]{:S(2)}) async-start(bf16[8,128,768]{2,1,0:T(8,128)(2,1)} %get-tuple-element.91), calls=%async_computation.6 | async-start | bytes 3145728 | tf_op jit(solution)/shard_map/all_to_all | solution.py:568
  381.1 17.6 %collective-permute-start.4 = (bf16[96,2432]{1,0:T(8,128)(2,1)}, bf16[96,2432]{1,0:T(8,128)(2,1)S(1)}, u32[]{:S(2)}, u32[]{:S(2)}) collective-permute-start(bf16[96,2432]{1,0:T(8,128)(2,1)} %get-tuple-element.159), channel_id=1, source_target_pairs={{0,1},{1,2},{2,3},{3,0},{4,5},{5,6},{6,7},{7,4},{8,9},{9,10},{10,1... | collective-permute-start | bytes 1400840 | tf_op jit(solution)/shard_map/ppermute | solution.py:573
  382.6 25.1 %collective-permute-start.6 = (bf16[96,2432]{1,0:T(8,128)(2,1)}, bf16[96,2432]{1,0:T(8,128)(2,1)S(1)}, u32[]{:S(2)}, u32[]{:S(2)}) collective-permute-start(bf16[96,2432]{1,0:T(8,128)(2,1)} %get-tuple-element.160), channel_id=1, source_target_pairs={{0,3},{1,0},{2,1},{3,2},{4,7},{5,4},{6,5},{7,6},{8,11},{9,8},{10,9... | collective-permute-start | bytes 1400840 | tf_op jit(solution)/shard_map/ppermute | solution.py:573
  384.0 23.7 %collective-permute-start.5 = (bf16[96,2432]{1,0:T(8,128)(2,1)}, bf16[96,2432]{1,0:T(8,128)(2,1)S(1)}, u32[]{:S(2)}, u32[]{:S(2)}) collective-permute-start(bf16[96,2432]{1,0:T(8,128)(2,1)} %get-tuple-element.161), channel_id=1, source_target_pairs={{0,2},{1,3},{2,0},{3,1},{4,6},{5,7},{6,4},{7,5},{8,10},{9,11},{10,... | collective-permute-start | bytes 1400840 | tf_op jit(solution)/shard_map/ppermute | solution.py:573
  408.8 27.6 %collective-permute-start.7 = (bf16[24,2432]{1,0:T(8,128)(2,1)}, bf16[24,2432]{1,0:T(8,128)(2,1)}, u32[]{:S(2)}, u32[]{:S(2)}) collective-permute-start(bf16[24,2432]{1,0:T(8,128)(2,1)} %get-tuple-element.169), channel_id=1, source_target_pairs={{0,8},{8,16},{16,24},{24,0},{1,9},{9,17},{17,25},{25,1},{2,10},{10... | collective-permute-start | bytes 350216 | tf_op jit(solution)/shard_map/ppermute | solution.py:573
  410.3 26.1 %collective-permute-start.9 = (bf16[24,2432]{1,0:T(8,128)(2,1)}, bf16[24,2432]{1,0:T(8,128)(2,1)}, u32[]{:S(2)}, u32[]{:S(2)}) collective-permute-start(bf16[24,2432]{1,0:T(8,128)(2,1)} %get-tuple-element.170), channel_id=1, source_target_pairs={{0,24},{8,0},{16,8},{24,16},{1,25},{9,1},{17,9},{25,17},{2,26},{10... | collective-permute-start | bytes 350216 | tf_op jit(solution)/shard_map/ppermute | solution.py:573
  412.7 23.8 %collective-permute-start.8 = (bf16[24,2432]{1,0:T(8,128)(2,1)}, bf16[24,2432]{1,0:T(8,128)(2,1)}, u32[]{:S(2)}, u32[]{:S(2)}) collective-permute-start(bf16[24,2432]{1,0:T(8,128)(2,1)} %get-tuple-element.171), channel_id=1, source_target_pairs={{0,16},{8,24},{16,0},{24,8},{1,17},{9,25},{17,1},{25,9},{2,18},{10... | collective-permute-start | bytes 350216 | tf_op jit(solution)/shard_map/ppermute | solution.py:573
  436.4 21.3 %collective-permute-start.2 = (bf16[2,1024,256]{2,1,0:T(8,128)(2,1)}, bf16[2,1024,256]{2,1,0:T(8,128)(2,1)}, u32[]{:S(2)}, u32[]{:S(2)}) collective-permute-start(bf16[2,1024,256]{2,1,0:T(8,128)(2,1)} %get-tuple-element.105), channel_id=1, source_target_pairs={{0,4},{4,0},{1,5},{5,1},{2,6},{6,2},{3,7},{7,3},{8,12},{12,8},{9,1... | collective-permute-start | bytes 3145736 | tf_op jit(solution)/shard_map/ppermute | solution.py:564
  439.1 12.3 %collective-permute-start.11 = (bf16[24,2432]{1,0:T(8,128)(2,1)S(1)}, bf16[24,2432]{1,0:T(8,128)(2,1)S(1)}, u32[]{:S(2)}, u32[]{:S(2)}) collective-permute-start(bf16[24,2432]{1,0:T(8,128)(2,1)S(1)} %fusion.67), channel_id=1, source_target_pairs={{0,16},{8,24},{16,0},{24,8},{1,17},{9,25},{17,1},{25,9},{2,18},{10... | collective-permute-start | bytes 350216 | tf_op jit(solution)/shard_map/ppermute | solution.py:573
  440.3 11.1 %collective-permute-start.10 = (bf16[24,2432]{1,0:T(8,128)(2,1)S(1)}, bf16[24,2432]{1,0:T(8,128)(2,1)S(1)}, u32[]{:S(2)}, u32[]{:S(2)}) collective-permute-start(bf16[24,2432]{1,0:T(8,128)(2,1)S(1)} %fusion.67), channel_id=1, source_target_pairs={{0,8},{8,16},{16,24},{24,0},{1,9},{9,17},{17,25},{25,1},{2,10},{10... | collective-permute-start | bytes 350216 | tf_op jit(solution)/shard_map/ppermute | solution.py:573
  452.4 22.6 %collective-permute-start.14 = (bf16[4,24,2432]{2,1,0:T(8,128)(2,1)}, bf16[4,24,2432]{2,1,0:T(8,128)(2,1)}, u32[]{:S(2)}, u32[]{:S(2)}) collective-permute-start(bf16[4,24,2432]{2,1,0:T(8,128)(2,1)} %get-tuple-element.168), channel_id=1, source_target_pairs={{0,2},{1,3},{2,0},{3,1},{4,6},{5,7},{6,4},{7,5},{8,10},{9,11},{10,... | collective-permute-start | bytes 1400840 | tf_op jit(solution)/shard_map/ppermute | solution.py:573
  453.9 21.1 %collective-permute-start.13 = (bf16[4,24,2432]{2,1,0:T(8,128)(2,1)}, bf16[4,24,2432]{2,1,0:T(8,128)(2,1)}, u32[]{:S(2)}, u32[]{:S(2)}) collective-permute-start(bf16[4,24,2432]{2,1,0:T(8,128)(2,1)} %get-tuple-element.168), channel_id=1, source_target_pairs={{0,1},{1,2},{2,3},{3,0},{4,5},{5,6},{6,7},{7,4},{8,9},{9,10},{10,1... | collective-permute-start | bytes 1400840 | tf_op jit(solution)/shard_map/ppermute | solution.py:573
  454.4 21.8 %collective-permute-start.15 = (bf16[4,24,2432]{2,1,0:T(8,128)(2,1)}, bf16[4,24,2432]{2,1,0:T(8,128)(2,1)}, u32[]{:S(2)}, u32[]{:S(2)}) collective-permute-start(bf16[4,24,2432]{2,1,0:T(8,128)(2,1)} %get-tuple-element.168), channel_id=1, source_target_pairs={{0,3},{1,0},{2,1},{3,2},{4,7},{5,4},{6,5},{7,6},{8,11},{9,8},{10,9... | collective-permute-start | bytes 1400840 | tf_op jit(solution)/shard_map/ppermute | solution.py:573
  463.9 14.2 %collective-permute-start.16 = (bf16[384,768]{1,0:T(8,128)(2,1)S(1)}, bf16[384,768]{1,0:T(8,128)(2,1)S(1)}, u32[]{:S(2)}, u32[]{:S(2)}) collective-permute-start(bf16[384,768]{1,0:T(8,128)(2,1)S(1)} %dynamic-slice_bitcast_fusion.3), channel_id=1, source_target_pairs={{0,4},{4,0},{1,5},{5,1},{2,6},{6,2},{3,7},{7,3},{8,12},{12,8},{9,1... | collective-permute-start | bytes 1769480 | tf_op jit(solution)/shard_map/ppermute | solution.py:573
  478.0 55.7 %collective-permute-start.29 = (bf16[4,4,24,2432]{3,2,1,0:T(8,128)(2,1)S(1)}, bf16[4,4,24,2432]{3,2,1,0:T(8,128)(2,1)}, u32[]{:S(2)}, u32[]{:S(2)}) collective-permute-start(bf16[4,4,24,2432]{3,2,1,0:T(8,128)(2,1)S(1)} %pad_maximum_fusion.refs_0_), channel_id=1, source_target_pairs={{0,4},{4,0},{1,5},{5,1},{2,6},{6,2},{3,7},{7,3},{8,12},{12,8},{9,1... | collective-permute-start | bytes 5603336 | tf_op jit(solution)/shard_map/ppermute | solution.py:564
  479.8 8.9 %collective-permute-start.19 = (bf16[96,768]{1,0:T(8,128)(2,1)S(1)}, bf16[96,768]{1,0:T(8,128)(2,1)S(1)}, u32[]{:S(2)}, u32[]{:S(2)}) collective-permute-start(bf16[96,768]{1,0:T(8,128)(2,1)S(1)} %get-tuple-element.163), channel_id=1, source_target_pairs={{0,3},{1,0},{2,1},{3,2},{4,7},{5,4},{6,5},{7,6},{8,11},{9,8},{10,9... | collective-permute-start | bytes 442376 | tf_op jit(solution)/shard_map/ppermute | solution.py:573
  483.9 42.3 %collective-permute-start.32 = (bf16[2,768,384]{2,1,0:T(8,128)(2,1)}, bf16[2,768,384]{2,1,0:T(8,128)(2,1)S(1)}, u32[]{:S(2)}, u32[]{:S(2)}) collective-permute-start(bf16[2,768,384]{2,1,0:T(8,128)(2,1)} %dynamic-slice_bitcast_fusion.1), channel_id=1, source_target_pairs={{0,4},{4,0},{1,5},{5,1},{2,6},{6,2},{3,7},{7,3},{8,12},{12,8},{9,1... | collective-permute-start | bytes 3538952 | tf_op jit(solution)/shard_map/ppermute | solution.py:564
  488.8 11.9 %collective-permute-start.20 = (bf16[24,768]{1,0:T(8,128)(2,1)S(1)}, bf16[24,768]{1,0:T(8,128)(2,1)}, u32[]{:S(2)}, u32[]{:S(2)}) collective-permute-start(bf16[24,768]{1,0:T(8,128)(2,1)S(1)} %get-tuple-element.174), channel_id=1, source_target_pairs={{0,8},{8,16},{16,24},{24,0},{1,9},{9,17},{17,25},{25,1},{2,10},{10... | collective-permute-start | bytes 110600 | tf_op jit(solution)/shard_map/ppermute | solution.py:573
  488.9 11.8 %collective-permute-start.22 = (bf16[24,768]{1,0:T(8,128)(2,1)S(1)}, bf16[24,768]{1,0:T(8,128)(2,1)}, u32[]{:S(2)}, u32[]{:S(2)}) collective-permute-start(bf16[24,768]{1,0:T(8,128)(2,1)S(1)} %get-tuple-element.175), channel_id=1, source_target_pairs={{0,24},{8,0},{16,8},{24,16},{1,25},{9,1},{17,9},{25,17},{2,26},{10... | collective-permute-start | bytes 110600 | tf_op jit(solution)/shard_map/ppermute | solution.py:573
  492.7 8.0 %collective-permute-start.21 = (bf16[24,768]{1,0:T(8,128)(2,1)S(1)}, bf16[24,768]{1,0:T(8,128)(2,1)}, u32[]{:S(2)}, u32[]{:S(2)}) collective-permute-start(bf16[24,768]{1,0:T(8,128)(2,1)S(1)} %get-tuple-element.176), channel_id=1, source_target_pairs={{0,16},{8,24},{16,0},{24,8},{1,17},{9,25},{17,1},{25,9},{2,18},{10... | collective-permute-start | bytes 110600 | tf_op jit(solution)/shard_map/ppermute | solution.py:573
  501.7 7.9 %collective-permute-start.25 = (bf16[24,768]{1,0:T(8,128)(2,1)S(1)}, bf16[24,768]{1,0:T(8,128)(2,1)S(1)}, u32[]{:S(2)}, u32[]{:S(2)}) collective-permute-start(bf16[24,768]{1,0:T(8,128)(2,1)S(1)} %fusion.73), channel_id=1, source_target_pairs={{0,24},{8,0},{16,8},{24,16},{1,25},{9,1},{17,9},{25,17},{2,26},{10... | collective-permute-start | bytes 110600 | tf_op jit(solution)/shard_map/ppermute | solution.py:573
  509.6 16.7 %collective-permute-start.31 = (bf16[2,768,384]{2,1,0:T(8,128)(2,1)S(1)}, bf16[2,768,384]{2,1,0:T(8,128)(2,1)}, u32[]{:S(2)}, u32[]{:S(2)}) collective-permute-start(bf16[2,768,384]{2,1,0:T(8,128)(2,1)S(1)} %copy-done.25), channel_id=1, source_target_pairs={{0,4},{4,0},{1,5},{5,1},{2,6},{6,2},{3,7},{7,3},{8,12},{12,8},{9,1... | collective-permute-start | bytes 3538952 | tf_op jit(solution)/shard_map/ppermute | solution.py:564
  515.1 7.7 %collective-permute-start.26 = (bf16[4,24,768]{2,1,0:T(8,128)(2,1)S(1)}, bf16[4,24,768]{2,1,0:T(8,128)(2,1)S(1)}, u32[]{:S(2)}, u32[]{:S(2)}) collective-permute-start(bf16[4,24,768]{2,1,0:T(8,128)(2,1)S(1)} %get-tuple-element.173), channel_id=1, source_target_pairs={{0,1},{1,2},{2,3},{3,0},{4,5},{5,6},{6,7},{7,4},{8,9},{9,10},{10,1... | collective-permute-start | bytes 442376 | tf_op jit(solution)/shard_map/ppermute | solution.py:573
  523.8 9.9 %collective-permute-start.30 = (bf16[4,4,24,768]{3,2,1,0:T(8,128)(2,1)S(1)}, bf16[4,4,24,768]{3,2,1,0:T(8,128)(2,1)}, u32[]{:S(2)}, u32[]{:S(2)}) collective-permute-start(bf16[4,4,24,768]{3,2,1,0:T(8,128)(2,1)S(1)} %pad_maximum_fusion.1.refs_1_), channel_id=1, source_target_pairs={{0,4},{4,0},{1,5},{5,1},{2,6},{6,2},{3,7},{7,3},{8,12},{12,8},{9,1... | collective-permute-start | bytes 1769480 | tf_op jit(solution)/shard_map/ppermute | solution.py:564
  (46 other events, 277.9 us)
Sparse Core Ops, SparseCore 0:
  194.9 96.2 reduce-scatter.2
  294.3 106.5 reduce-scatter.4

commit v2 on v1

v2 whole, which is shorter than its diff:
```python
import functools
import math

import jax
import jax.numpy as jnp
from jax import lax
from jax.experimental import pallas as pl
from jax.experimental.pallas import tpu as pltpu
from jax.sharding import PartitionSpec as P

HEADS = 12
NORM_EPS = 1e-06
BF = jnp.bfloat16
F32 = jnp.float32
NN = (((1,), (0,)), ((), ()))
NT = (((1,), (1,)), ((), ()))
VMEM_BYTES = 60 << 20
EXTRA = 8
SMALL = 128
SAFE = 40.0


def estimate(flops, moved, slow=0):
    return pl.CostEstimate(flops=flops // 4, bytes_accessed=moved // 4, transcendentals=slow // 4)


def mm(left, right, dims=NN):
    return lax.dot_general(left, right, dims, preferred_element_type=F32)


def norm_forward(values_in, gain_vec):
    centre_mean = jnp.mean(values_in, axis=-1, keepdims=True)
    centred = values_in - centre_mean
    inv_scale = lax.rsqrt(jnp.mean(centred * centred, axis=-1, keepdims=True) + NORM_EPS)
    unit_rows = centred * inv_scale
    return (unit_rows * gain_vec, unit_rows, inv_scale)


def norm_backward(gradient, unit_rows, inv_scale, gain_vec):
    scaled = gradient * gain_vec
    inner_sum = (
        scaled
        - jnp.mean(scaled, axis=-1, keepdims=True)
        - unit_rows * jnp.mean(scaled * unit_rows, axis=-1, keepdims=True)
    )
    return (inner_sum * inv_scale, jnp.sum(gradient * unit_rows, axis=0))


def attend_kernel(q_ref, k0, k1, v0, v1, o_ref, p_ref, li_ref, vext, ksize, *, scale):
    half = k0.shape[0]

    def largest(v):
        return jnp.max(jnp.sum(v * v, axis=1, keepdims=True))

    @pl.when(pl.program_id(1) == 0)
    def _():
        ones = jnp.ones((half, 128), BF)
        vext[0:half, 0:128] = v0[...]
        vext[half:, 0:128] = v1[...]
        vext[0:half, 128:256] = ones
        vext[half:, 128:256] = ones
        ksize[0] = jnp.maximum(largest(k0[...].astype(F32)), largest(k1[...].astype(F32)))

    low = lax.broadcasted_iota(jnp.int32, q_ref.shape, 1) < 64
    q = q_ref[...]
    factor = scale * math.log2(math.e)
    small = largest(q.astype(F32)) * ksize[0] * (factor * factor) < SAFE * SAFE

    def run(shifted):
        outs, sums = [], []
        for h in range(2):
            picked = jnp.where(low if h == 0 else jnp.logical_not(low), q, jnp.zeros_like(q))
            s0 = mm(picked, k0[...], NT) * factor
            s1 = mm(picked, k1[...], NT) * factor
            if shifted:
                peak = jnp.maximum(
                    jnp.max(s0, axis=1, keepdims=True), jnp.max(s1, axis=1, keepdims=True)
                )
                s0 = s0 - peak
                s1 = s1 - peak
            p_ref[h, :, 0:half] = jnp.exp2(s0).astype(BF)
            p_ref[h, :, half:] = jnp.exp2(s1).astype(BF)
            both = mm(p_ref[h], vext[...])
            outs.append(both[:, 0:128])
            sums.append(both[:, 128:256])
        inv = 1.0 / jnp.where(low, sums[0], sums[1])
        o_ref[...] = (jnp.where(low, outs[0], outs[1]) * inv).astype(BF)
        li_ref[...] = inv

    pl.when(small)(lambda: run(False))
    pl.when(jnp.logical_not(small))(lambda: run(True))


def attend(qkv, kv_other, block):
    rows = qkv.shape[0]
    width = qkv.shape[1] // 3
    pairs = width // 128
    tile = pl.BlockSpec((block, 128), lambda h, i: (i, h))
    return pl.pallas_call(
        functools.partial(attend_kernel, scale=1.0 / math.sqrt(width // HEADS)),
        grid=(pairs, rows // block),
        in_specs=[
            tile,
            pl.BlockSpec((rows, 128), lambda h, i: (0, pairs + h)),
            pl.BlockSpec((rows, 128), lambda h, i: (0, h)),
            pl.BlockSpec((rows, 128), lambda h, i: (0, 2 * pairs + h)),
            pl.BlockSpec((rows, 128), lambda h, i: (0, pairs + h)),
        ],
        out_specs=[tile, pl.BlockSpec((2, block, 2 * rows), lambda h, i: (h, i, 0)), tile],
        out_shape=[
            jax.ShapeDtypeStruct((rows, width), BF),
            jax.ShapeDtypeStruct((HEADS, rows, 2 * rows), BF),
            jax.ShapeDtypeStruct((rows, width), F32),
        ],
        scratch_shapes=[pltpu.VMEM((2 * rows, 256), BF), pltpu.SMEM((1,), F32)],
        compiler_params=pltpu.CompilerParams(vmem_limit_bytes=VMEM_BYTES),
        cost_estimate=estimate(rows * width, rows * width),
        name="attend",
    )(qkv, qkv, kv_other, qkv, kv_other)


def attend_back_kernel(
    q_ref, k0, k1, v0, v1, o_ref, g_ref, li_ref, p_ref,
    dq_ref, own_ref, far_ref, vext, kacc, vacc, *, scale, steps,
):
    i = pl.program_id(1)
    half = k0.shape[0]
    lane = lax.broadcasted_iota(jnp.int32, q_ref.shape, 1)
    low = lane < 64

    @pl.when(i == 0)
    def _():
        ones = jnp.where(lax.broadcasted_iota(jnp.int32, (half, 128), 1) < 2, 1.0, 0.0).astype(BF)
        vext[0:half, 0:128] = v0[...]
        vext[half:, 0:128] = v1[...]
        vext[0:half, 128:256] = ones
        vext[half:, 128:256] = ones

    g = g_ref[...].astype(F32) * li_ref[...]
    gb = g.astype(BF)
    go = g * o_ref[...].astype(F32)
    qt = q_ref[...].T
    gt = gb.T
    dqs = []
    for h in range(2):
        mine = low if h == 0 else jnp.logical_not(low)
        delta = -jnp.sum(jnp.where(mine, go, 0.0), axis=1, keepdims=True)
        high = delta.astype(BF).astype(F32)
        extra = jnp.where(lane == 0, high, jnp.where(lane == 1, delta - high, 0.0)).astype(BF)
        gext = jnp.concatenate([jnp.where(mine, gb, jnp.zeros_like(gb)), extra], axis=1)
        p = p_ref[h]
        ds = (p.astype(F32) * mm(gext, vext[...], NT)).astype(BF)
        dqs.append(mm(ds[:, 0:half], k0[...]) + mm(ds[:, half:], k1[...]))
        rows = slice(64 * h, 64 * h + 64)
        dk = mm(qt[rows], ds)
        dv = mm(gt[rows], p)

        @pl.when(i == 0)
        def _():
            kacc[rows] = dk
            vacc[rows] = dv

        @pl.when(i > 0)
        def _():
            kacc[rows] += dk
            vacc[rows] += dv

    dq_ref[...] = (jnp.where(low, dqs[0], dqs[1]) * scale).astype(BF)

    @pl.when(i == steps - 1)
    def _():
        own_ref[0] = kacc[:, 0:half].T * scale
        own_ref[1] = vacc[:, 0:half].T
        far_ref[0] = (kacc[:, half:].T * scale).astype(BF)
        far_ref[1] = vacc[:, half:].T.astype(BF)


def attend_back(qkv, kv_other, mixed, grad, inv_sum, probs, block, first, count):
    rows = qkv.shape[0]
    width = qkv.shape[1] // 3
    pairs = width // 128
    steps = rows // block
    tile = pl.BlockSpec((block, 128), lambda h, i: (i, first + h))
    both = pl.BlockSpec((2, rows, 128), lambda h, i: (0, 0, h))
    return pl.pallas_call(
        functools.partial(attend_back_kernel, scale=1.0 / math.sqrt(width // HEADS), steps=steps),
        grid=(count, steps),
        in_specs=[
            tile,
            pl.BlockSpec((rows, 128), lambda h, i: (0, pairs + first + h)),
            pl.BlockSpec((rows, 128), lambda h, i: (0, first + h)),
            pl.BlockSpec((rows, 128), lambda h, i: (0, 2 * pairs + first + h)),
            pl.BlockSpec((rows, 128), lambda h, i: (0, pairs + first + h)),
            tile,
            tile,
            tile,
            pl.BlockSpec((2, block, 2 * rows), lambda h, i: (first + h, i, 0)),
        ],
        out_specs=[pl.BlockSpec((block, 128), lambda h, i: (i, h)), both, both],
        out_shape=[
            jax.ShapeDtypeStruct((rows, 128 * count), BF),
            jax.ShapeDtypeStruct((2, rows, 128 * count), F32),
            jax.ShapeDtypeStruct((2, rows, 128 * count), BF),
        ],
        scratch_shapes=[
            pltpu.VMEM((2 * rows, 256), BF),
            pltpu.VMEM((128, 2 * rows), F32),
            pltpu.VMEM((128, 2 * rows), F32),
        ],
        compiler_params=pltpu.CompilerParams(vmem_limit_bytes=VMEM_BYTES),
        cost_estimate=estimate(rows * width, rows * width),
        name="attend_back",
    )(qkv, qkv, kv_other, qkv, kv_other, mixed, grad, inv_sum, probs)


def grad_qkv_kernel(core, normed, *refs, count, with_out):
    if count:
        grad_ref, dqkv_ref = refs[-2:]
        cols = dqkv_ref.shape[1]
        wide = cols // 3
        at = 0
        for n in range(count):
            dq, own, far = refs[n], refs[count + n], refs[2 * count + n]
            size = dq.shape[1]
            dqkv_ref[:, at : at + size] = dq[...]
            for m in range(2):
                start = (m + 1) * wide + at
                dqkv_ref[:, start : start + size] = (own[m] + far[m].astype(F32)).astype(BF)
            at += size
        more = refs[3 * count :]
    else:
        dqkv_ref, grad_ref = refs[0], refs[-1]
        cols = dqkv_ref.shape[1]
        more = refs[1:]
    grad_ref[:, 0:cols] = mm(normed[...].T, dqkv_ref[...]).astype(BF)
    if with_out:
        mixed, branch, small = more[:3]
        width = branch.shape[1]
        grad_ref[:, cols : cols + width] = mm(mixed[...].T, branch[...]).astype(BF)
        value = small[...]
        high = value.astype(BF).astype(F32)
        rest = jnp.zeros((SMALL - 2 * value.shape[0], value.shape[1]), F32)
        grad_ref[:, cols + width :] = jnp.concatenate([high, value - high, rest], axis=0).T.astype(BF)


def grad_qkv_half(core, normed, sides, count, more):
    rows, width = normed.shape
    half = width // 2
    cols = sum(side.shape[-1] for side in sides[:count]) * 3 if count else sides[0].shape[1]
    out_cols = cols + (more[1].shape[1] + SMALL if more else 0)
    full = lambda a: pl.BlockSpec(a.shape, lambda i, core: (0,) * a.ndim)
    part = lambda a: pl.BlockSpec((a.shape[0], half), lambda i, core: (0, core[0]))
    out_specs = [pl.BlockSpec((half, out_cols), lambda i, core: (0, 0))]
    out_shape = [jax.ShapeDtypeStruct((half, out_cols), BF)]
    if count:
        out_specs.append(pl.BlockSpec((rows, cols), lambda i, core: (0, 0)))
        out_shape.append(jax.ShapeDtypeStruct((rows, cols), BF))
    return pl.pallas_call(
        functools.partial(grad_qkv_kernel, count=count, with_out=bool(more)),
        grid_spec=pltpu.PrefetchScalarGridSpec(
            num_scalar_prefetch=1,
            grid=(1,),
            in_specs=[part(normed)]
            + [full(side) for side in sides]
            + ([part(more[0]), full(more[1]), part(more[2])] if more else []),
            out_specs=out_specs,
        ),
        out_shape=out_shape,
        compiler_params=pltpu.CompilerParams(vmem_limit_bytes=VMEM_BYTES),
        cost_estimate=estimate(rows * width, rows * width),
        name="grad_qkv",
    )(core.astype(jnp.int32)[None], normed, *sides, *more)


def grad_qkv(normed, dqs, owns, fars, more=()):
    here = lax.axis_index("ctx")
    give, d_qkv = grad_qkv_half(1 - here, normed, (*dqs, *owns, *fars), len(dqs), more)
    other = swap(give)
    (keep,) = grad_qkv_half(here, normed, (d_qkv,), 0, more)
    return [keep, other], d_qkv


GELU_A = math.sqrt(2.0 / math.pi)
GELU_B = 0.044715


def gelu_both(v):
    square = v * v
    t = jnp.tanh(v * (GELU_A + GELU_A * GELU_B * square))
    half = 0.5 + 0.5 * t
    slope = half + (0.5 * v) * (1.0 - t * t) * (GELU_A + 3 * GELU_A * GELU_B * square)
    return v * half, slope


def put_extra(ref, r, row):
    width = ref.shape[2]
    cap = row.shape[1]
    line = lax.broadcasted_iota(jnp.int32, (EXTRA, cap), 0)
    full = jnp.zeros((EXTRA, cap), F32)
    for n, piece in enumerate(three_parts(row)):
        full = jnp.where(line == n, piece.astype(F32), full)
    full = jnp.concatenate([full, jnp.zeros((EXTRA, width - cap), F32)], axis=1)
    ref[r, ref.shape[1] - EXTRA :, :] = full.astype(BF)


def get_extra(ref, r, lanes):
    sent = ref[r, ref.shape[1] - EXTRA :, lanes].astype(F32)
    return sent[0:1] + sent[1:2] + sent[2:3]


def expert_kernel(which, x_in, gate_in, dy_in, *refs, part, parts, steps, first):
    last = part == parts - 1
    if not first:
        refs = refs[1:]
    dg_in = ()
    if last:
        dg_in, refs = refs[: parts - 1], refs[parts - 1 :]
    up_ref, down_ref, out_ref, dx_ref, act_ref, dhid_ref, dp_ref, *refs = refs
    if not last:
        dg_out, refs = refs[0], refs[1:]
    x, gate, out_acc, dx_acc = refs
    f = pl.program_id(0)
    peers, cap = dy_in.shape[0], dy_in.shape[1]

    @pl.when(f == 0)
    def _():
        lanes = slice(part * cap, (part + 1) * cap)
        gates = jnp.concatenate([get_extra(gate_in, r, lanes) for r in range(peers)], axis=0).T
        for r in range(peers):
            at = slice(r * cap, (r + 1) * cap)
            x[at] = x_in[r, 0:cap, :]
            g = gates[:, r : r + 1]
            gate[at] = g
            dp_ref[at] = (dy_in[r].astype(F32) * g).astype(BF)

    up = up_ref[0]
    down = down_ref[0]
    value, slope = gelu_both(mm(x[...], up))
    act_ref[...] = value.astype(BF)
    dhid_ref[...] = (mm(dp_ref[...], down, NT) * slope).astype(BF)

    @pl.when(f == 0)
    def _():
        dx_acc[...] = mm(dhid_ref[...], up, NT)
        out_acc[...] = mm(act_ref[...], down)

    @pl.when(f > 0)
    def _():
        dx_acc[...] += mm(dhid_ref[...], up, NT)
        out_acc[...] += mm(act_ref[...], down)

    @pl.when(f == steps - 1)
    def _():
        sums = []
        for r in range(peers):
            at = slice(r * cap, (r + 1) * cap)
            produced = out_acc[at].astype(BF).astype(F32)
            dx_ref[r, 0:cap, :] = dx_acc[at].astype(BF)
            out_ref[r] = (produced * gate[at]).astype(BF)
            sums.append(jnp.sum(produced * dy_in[r].astype(F32), axis=1, keepdims=True))
        sums = jnp.concatenate(sums, axis=1).T
        if last:
            full = jnp.concatenate([ref[...] for ref in dg_in] + [sums], axis=1)
            for r in range(peers):
                put_extra(dx_ref, r, full[r : r + 1])
        else:
            dg_out[...] = sums


def run_expert(which, part, parts, x, first_x, dy, outs, dgates, w_up, w_down, chunk=768):
    peers, width = x.shape[0], x.shape[2]
    cap = dy.shape[1] // parts
    rows = peers * cap
    hidden = w_up.shape[-1]
    last = part == parts - 1
    full = lambda shape: pl.BlockSpec(shape, lambda f, j: (0,) * len(shape))
    wide = pl.BlockSpec((rows, chunk), lambda f, j: (0, f))
    dx_shape = (peers, cap + (EXTRA if last else 0), width)
    extra_at = (first_x.shape[1] - EXTRA) // EXTRA
    out_specs = [
        pl.BlockSpec((peers, cap, width), lambda f, j: (0, part, 0)),
        full(dx_shape), wide, wide, full((rows, width)),
    ]
    out_shape = [
        jax.ShapeDtypeStruct(dy.shape, BF),
        jax.ShapeDtypeStruct(dx_shape, BF),
        jax.ShapeDtypeStruct((rows, hidden), BF),
        jax.ShapeDtypeStruct((rows, hidden), BF),
        jax.ShapeDtypeStruct((rows, width), BF),
    ]
    if not last:
        out_specs.append(full((peers, cap)))
        out_shape.append(jax.ShapeDtypeStruct((peers, cap), F32))
        dgates = []
    return pl.pallas_call(
        functools.partial(
            expert_kernel, part=part, parts=parts, steps=hidden // chunk, first=outs is None
        ),
        grid_spec=pltpu.PrefetchScalarGridSpec(
            num_scalar_prefetch=1,
            grid=(hidden // chunk,),
            in_specs=[
                full(x.shape),
                pl.BlockSpec((peers, EXTRA, width), lambda f, j: (0, extra_at, 0)),
                pl.BlockSpec((peers, cap, width), lambda f, j: (0, part, 0)),
                *[pl.BlockSpec(memory_space=pl.ANY)] * (outs is not None),
                *[full(d.shape) for d in dgates],
                pl.BlockSpec((1, width, chunk), lambda f, j: (j[0], 0, f)),
                pl.BlockSpec((1, chunk, width), lambda f, j: (j[0], f, 0)),
            ],
            out_specs=out_specs,
            scratch_shapes=[
                pltpu.VMEM((rows, width), BF),
                pltpu.VMEM((rows, 1), F32),
                pltpu.VMEM((rows, width), F32),
                pltpu.VMEM((rows, width), F32),
            ],
        ),
        out_shape=out_shape,
        compiler_params=pltpu.CompilerParams(vmem_limit_bytes=VMEM_BYTES),
        cost_estimate=estimate(8 * rows * width * hidden, 4 * width * hidden, rows * hidden),
        input_output_aliases={} if outs is None else {4: 0},
        name="expert",
    )(which, x, first_x, dy, *([] if outs is None else [outs]), *dgates, w_up, w_down)


def weights_kernel(at, *refs, count, pieces, turned):
    acts, dhids, refs = refs[:count], refs[count : 2 * count], refs[2 * count :]
    if turned:
        xt, dpt, out_ref = refs
    else:
        xs, dps, (out_ref, xt, dpt) = refs[:count], refs[count : 2 * count], refs[2 * count :]

        @pl.when(pl.program_id(0) == 0)
        def _():
            place = 0
            for x, dp in zip(xs, dps):
                rows = dp.shape[0]
                cap = rows // x.shape[0]
                held = jnp.concatenate([x[r, 0:cap, :] for r in range(x.shape[0])], axis=0)
                xt[:, place : place + rows] = held.T
                dpt[:, place : place + rows] = dp[...].T
                place += rows

    def product(left, rights):
        total, place = None, 0
        for right in rights:
            rows = right.shape[0]
            add = mm(left[:, place : place + rows], right[...])
            total = add if total is None else total + add
            place += rows
        return total.astype(BF)

    gup = product(xt, dhids)
    gdown = product(dpt, acts)
    wide = gup.shape[1] // pieces
    for s in range(pieces):
        out_ref[s, 0] = gup[:, s * wide : (s + 1) * wide]
        out_ref[s, 1] = gdown[:, s * wide : (s + 1) * wide]


def weight_grads(core, acts, dhids, sides, turned, n_ctx, n_dp, chunk=768):
    width, hidden = (sides[0].shape[0] if turned else sides[0].shape[2]), acts[0].shape[1]
    rows = sum(a.shape[0] for a in acts)
    half = hidden // n_ctx
    steps = half // chunk
    wide = half // n_dp
    pieces = chunk // wide
    full = lambda shape: pl.BlockSpec(shape, lambda f, at: (0,) * len(shape))
    out_specs = [pl.BlockSpec((pieces, 2, width, wide), lambda f, at: (f, 0, 0, 0))]
    out_shape = [jax.ShapeDtypeStruct((n_dp, 2, width, wide), BF)]
    if not turned:
        out_specs += [full((width, rows))] * 2
        out_shape += [jax.ShapeDtypeStruct((width, rows), BF)] * 2
    made = pl.pallas_call(
        functools.partial(weights_kernel, count=len(acts), pieces=pieces, turned=turned),
        grid_spec=pltpu.PrefetchScalarGridSpec(
            num_scalar_prefetch=1,
            grid=(steps,),
            in_specs=[
                pl.BlockSpec((a.shape[0], chunk), lambda f, at: (0, at[0] * steps + f))
                for a in (*acts, *dhids)
            ]
            + [full(a.shape) for a in sides],
            out_specs=out_specs,
        ),
        out_shape=out_shape,
        compiler_params=pltpu.CompilerParams(vmem_limit_bytes=VMEM_BYTES),
        cost_estimate=estimate(rows * width, rows * width),
        name="weight_grads",
    )(core.astype(jnp.int32)[None], *acts, *dhids, *sides)
    return made[0], made[1:]


def both_weight_grads(group, here, n_ctx, n_dp):
    xs, dps, acts, dhids = zip(*group)
    give, sides = weight_grads(1 - here, acts, dhids, (*xs, *dps), False, n_ctx, n_dp)
    keep, _ = weight_grads(here, acts, dhids, sides, True, n_ctx, n_dp)
    return give, keep


def seats(expert_ids, seat_order, expert_count, capacity, slot_of):
    token_count = expert_ids.shape[0]
    places = jnp.arange(token_count, dtype=jnp.int32)
    earlier = (seat_order[:, None] < seat_order[None, :]) | (
        seat_order[:, None] == seat_order[None, :]
    ) & (places[:, None] < places[None, :])
    earlier = earlier.astype(BF)
    lane_ids = jnp.arange(expert_count, dtype=jnp.int32)
    first_hot = expert_ids[:, 0:1] == lane_ids[None, :]
    second_hot = expert_ids[:, 1:2] == lane_ids[None, :]
    both_hot = jnp.concatenate([first_hot, second_hot], axis=1).astype(BF)
    ahead = jnp.einsum("st,se->te", earlier, both_hot, preferred_element_type=F32)
    ahead_first = ahead[:, :expert_count]
    ahead_second = ahead[:, expert_count:] + jnp.sum(first_hot.astype(F32), axis=0)[None, :]
    rank_first = jnp.sum(jnp.where(first_hot, ahead_first, 0.0), axis=-1)
    rank_second = jnp.sum(jnp.where(second_hot, ahead_second, 0.0), axis=-1)

    def slot(picked, rank):
        at = rank.astype(jnp.int32)
        return jnp.where(at < capacity, slot_of(picked, at), -1)

    return (
        slot(expert_ids[:, 0], rank_first),
        slot(expert_ids[:, 1], rank_second),
        first_hot,
        second_hot,
    )


def three_parts(v):
    high = v.astype(BF)
    rest = v - high.astype(F32)
    mid = rest.astype(BF)
    return high, mid, (rest - mid.astype(F32)).astype(BF)


def seat_rows_kernel(t1, t2, *refs, chosen, parts, cap):
    *gate_refs, rows_ref, out_ref = refs
    peers = out_ref.shape[0]
    tokens = t1.shape[1]
    group = min(peers, max(1, 256 // cap))

    def hot_of(t, part, r):
        ids = lax.broadcasted_iota(jnp.int32, (group * cap, tokens), 0) + (part * peers + r) * cap
        return ids == t[...]

    for n, part in enumerate(chosen):
        for r in range(0, peers, group):
            hot = hot_of(t1, part, r) | hot_of(t2, part, r)
            got = mm(jnp.where(hot, 1.0, 0.0).astype(BF), rows_ref[...]).astype(BF)
            for m in range(group):
                out_ref[r + m, n * cap : (n + 1) * cap, :] = got[m * cap : (m + 1) * cap]
    if gate_refs:
        lefts = [jnp.concatenate(three_parts(g[...]), axis=0) for g in gate_refs]
        for r in range(0, peers, group):
            got = []
            for part in range(parts):
                both = sum(
                    mm(left, jnp.where(hot_of(t, part, r), 1.0, 0.0).astype(BF), NT)
                    for left, t in zip(lefts, (t1, t2))
                )
                got.append(jnp.sum(both, axis=0, keepdims=True))
            for m in range(group):
                put_extra(
                    out_ref, r + m, jnp.concatenate([g[:, m * cap : (m + 1) * cap] for g in got], axis=1)
                )


def seat_rows(t1, t2, rows, gates, chosen, parts, peers, cap):
    tokens, width = rows.shape
    per_peer = len(chosen) * cap + (EXTRA if gates else 0)
    return pl.pallas_call(
        functools.partial(seat_rows_kernel, chosen=chosen, parts=parts, cap=cap),
        out_shape=jax.ShapeDtypeStruct((peers, per_peer, width), BF),
        compiler_params=pltpu.CompilerParams(vmem_limit_bytes=VMEM_BYTES),
        cost_estimate=estimate(2 * peers * per_peer * tokens * width, 4 * tokens * width),
        name="seat_rows",
    )(t1[None], t2[None], *[g[None] for g in gates], rows)


def rows_back(t1, t2, back, extra, split=1):
    tokens = t1.shape[0]
    total, place = None, 0
    firsts = jnp.zeros((tokens, 1), F32)
    seconds = firsts
    peers = back[0].shape[0]
    parts = [(ref, 0, back[0].shape[1]) for ref in back]
    if split > 1:
        cap = back[0].shape[1] // split
        parts = [(back[0], n * cap, cap) for n in range(split)]
    for part, (ref, start, cap) in enumerate(parts):
        group = min(peers, max(1, 512 // cap))
        for b in range(0, peers, group):
            ids = lax.broadcasted_iota(jnp.int32, (tokens, group * cap), 1) + place
            place += group * cap
            first = ids == t1
            second = ids == t2
            hot = jnp.where(first | second, 1.0, 0.0).astype(BF)
            add = mm(hot, jnp.concatenate([ref[b + n, start : start + cap, :] for n in range(group)], axis=0))
            total = add if total is None else total + add
            if extra:
                lanes = slice(part * cap, (part + 1) * cap)
                dg = jnp.concatenate([get_extra(back[-1], b + n, lanes) for n in range(group)], axis=1)
                firsts += jnp.sum(jnp.where(first, dg, 0.0), axis=1, keepdims=True)
                seconds += jnp.sum(jnp.where(second, dg, 0.0), axis=1, keepdims=True)
    return total, firsts, seconds


def unseat_kernel(t1, t2, base, back, out_ref, *, split):
    total, _, _ = rows_back(t1[...], t2[...], [back], False, split)
    out_ref[...] = (base[...] + total).astype(BF)


def unseat(t1, t2, base, back, split, block=256):
    tokens, width = base.shape
    col = pl.BlockSpec((block, 1), lambda i: (i, 0))
    rows = pl.BlockSpec((block, width), lambda i: (i, 0))
    return pl.pallas_call(
        functools.partial(unseat_kernel, split=split),
        grid=(tokens // block,),
        in_specs=[col, col, rows, pl.BlockSpec(back.shape, lambda i: (0, 0, 0))],
        out_specs=rows,
        out_shape=jax.ShapeDtypeStruct((tokens, width), BF),
        compiler_params=pltpu.CompilerParams(vmem_limit_bytes=VMEM_BYTES),
        cost_estimate=estimate(tokens * width, tokens * width),
        name="unseat",
    )(t1[:, None], t2[:, None], base, back)


def route_back_kernel(
    t1, t2, ids, probs, dy, middle, gain, w_router, w_out, *refs,
):
    dmiddle_ref, dbranch_ref, dmixed_ref, small_ref = refs[-4:]
    total, dg1, dg2 = rows_back(t1[...], t2[...], refs[:-4], True)
    p = probs[...]
    experts = p.shape[1]
    lane = lax.broadcasted_iota(jnp.int32, p.shape, 1)
    d_gates = jnp.where(lane == ids[:, 0:1], dg1, 0.0) + jnp.where(lane == ids[:, 1:2], dg2, 0.0)
    d_logits = p * (d_gates - jnp.sum(p * d_gates, axis=1, keepdims=True))
    d_routed = total
    for piece in three_parts(d_logits):
        d_routed = d_routed + mm(piece, w_router[...], NT)
    v = middle[...]
    centred = v - jnp.mean(v, axis=1, keepdims=True)
    inv = lax.rsqrt(jnp.mean(centred * centred, axis=1, keepdims=True) + NORM_EPS)
    unit = centred * inv
    routed = (unit * gain[...]).astype(BF)
    scaled = d_routed * gain[...]
    d_norm = inv * (
        scaled
        - jnp.mean(scaled, axis=1, keepdims=True)
        - unit * jnp.mean(scaled * unit, axis=1, keepdims=True)
    )
    d_middle = dy[...].astype(F32) + d_norm
    d_branch = d_middle.astype(BF)
    dmiddle_ref[...] = d_middle
    dbranch_ref[...] = d_branch
    dmixed_ref[...] = mm(d_branch, w_out[...], NT).astype(BF)
    to_router = 0.0
    for piece in three_parts(d_logits.T):
        to_router = to_router + mm(piece, routed)
    to_gain = jnp.sum(d_routed * unit, axis=0, keepdims=True)

    @pl.when(pl.program_id(0) == 0)
    def _():
        small_ref[...] = jnp.zeros_like(small_ref)

    small_ref[0:experts, :] += to_router
    small_ref[experts : experts + 1, :] += to_gain


def route_back(t1, t2, ids, probs, dy, middle, gain, w_router, w_out, parts, block=256):
    tokens, width = dy.shape
    experts = probs.shape[1]
    line = lambda cols: pl.BlockSpec((block, cols), lambda i: (i, 0))
    full = lambda a: pl.BlockSpec(a.shape, lambda i: (0,) * a.ndim)
    gain = gain[None]
    return pl.pallas_call(
        route_back_kernel,
        grid=(tokens // block,),
        in_specs=[
            line(1), line(1), line(2), line(experts), line(width), line(width),
            full(gain), full(w_router), full(w_out),
        ]
        + [full(part) for part in parts],
        out_specs=[
            line(width), line(width), line(width),
            pl.BlockSpec((experts + 8, width), lambda i: (0, 0)),
        ],
        out_shape=[
            jax.ShapeDtypeStruct((tokens, width), F32),
            jax.ShapeDtypeStruct((tokens, width), BF),
            jax.ShapeDtypeStruct((tokens, width), BF),
            jax.ShapeDtypeStruct((experts + 8, width), F32),
        ],
        compiler_params=pltpu.CompilerParams(vmem_limit_bytes=VMEM_BYTES),
        cost_estimate=estimate(tokens * width, tokens * width),
        name="route_back",
    )(t1[:, None], t2[:, None], ids, probs, dy, middle, gain, w_router, w_out, *parts)


def swap(value):
    n = lax.axis_size("ctx")
    return lax.ppermute(value, "ctx", [(i, (i + 1) % n) for i in range(n)])


def exchange(value, axes):
    return lax.all_to_all(value, axes, 0, 0, tiled=True)


def shift(value, axis, by):
    n = lax.axis_size(axis)
    return lax.ppermute(value, axis, [(i, (i + by) % n) for i in range(n)])


def scatter_begin(value, axis):
    n = lax.axis_size(axis)
    me = lax.axis_index(axis)
    x = value.reshape(n, value.shape[0] // n, value.shape[1])
    pick = lambda at: lax.dynamic_index_in_dim(x, at, 0, keepdims=False)
    return [pick(me)] + [shift(pick(lax.rem(me + s, n)), axis, s) for s in range(1, n)]


def add_up(pieces):
    total = pieces[0].astype(F32)
    for piece in pieces[1:]:
        total = total + piece.astype(F32)
    return total.astype(BF)


def gather_back(x, axis):
    n = lax.axis_size(axis)
    return [x] + [shift(x, axis, s) for s in range(1, n)]


def assemble_kernel(at, w_ref, *refs, groups, spans):
    ins, outs = refs[: 2 * groups], refs[2 * groups :]
    me = at[2]
    owners, rows = ins[0].shape[1], ins[0].shape[2]

    def write(held):
        for z in range(owners):
            back = lax.rem(me + owners - z, owners)
            for ref, span in zip(held, spans):
                piece = ref[0, back].astype(F32)
                for src, which, dst, size in span:
                    outs[which][z * rows : (z + 1) * rows, dst : dst + size] = piece[:, src : src + size]

    is_mine = pl.program_id(0) == at[0]
    pl.when(is_mine)(lambda: write(ins[:groups]))
    pl.when(jnp.logical_not(is_mine))(lambda: write(ins[groups:]))
    outs[-1][...] = jnp.sum(outs[0][...] * w_ref[...].astype(F32), axis=1, keepdims=True)


def assemble(sums, spans, widths, w_qkv):
    n_dp, owners, rows, _ = sums[0][0].shape
    n_ctx = lax.axis_size("ctx")
    block = owners * rows
    height = n_ctx * n_dp * block
    at = jnp.stack([lax.axis_index(axis) for axis in ("ctx", "dp", "expert")]).astype(jnp.int32)

    def back(mine):
        def place(c, d, at):
            edge = jnp.where(c == 0, 0, n_dp - 1)
            return ((at[1] + n_dp - jnp.where((c == at[0]) == mine, d, edge)) % n_dp, 0, 0, 0)

        return place

    line = lambda cols: pl.BlockSpec((block, cols), lambda c, d, at: (c * n_dp + d, 0))
    widths = [*widths, 1]
    return pl.pallas_call(
        functools.partial(assemble_kernel, groups=len(sums), spans=spans),
        grid_spec=pltpu.PrefetchScalarGridSpec(
            num_scalar_prefetch=1,
            grid=(n_ctx, n_dp),
            in_specs=[line(w_qkv.shape[1])]
            + [pl.BlockSpec((1,) + mine.shape[1:], back(True)) for mine, _ in sums]
            + [pl.BlockSpec((1,) + mine.shape[1:], back(False)) for mine, _ in sums],
            out_specs=[line(cols) for cols in widths],
        ),
        out_shape=[jax.ShapeDtypeStruct((height, cols), F32) for cols in widths],
        compiler_params=pltpu.CompilerParams(vmem_limit_bytes=VMEM_BYTES),
        cost_estimate=estimate(height * 2304, 12 * height * 2304),
        name="assemble",
    )(at, w_qkv, *[mine for mine, _ in sums], *[other for _, other in sums])


def spread_kernel(at, *refs):
    *ins, up_ref, down_ref = refs
    j = pl.program_id(0)
    for s, src in enumerate(ins):

        @pl.when(lax.rem(at[0] + len(ins) - s, len(ins)) == j)
        def _():
            up_ref[0] = src[0].astype(F32)
            down_ref[0] = src[1].astype(F32).T


def spread(pieces, place):
    count = len(pieces)
    _, width, cols = pieces[0].shape
    return pl.pallas_call(
        spread_kernel,
        grid_spec=pltpu.PrefetchScalarGridSpec(
            num_scalar_prefetch=1,
            grid=(count,),
            in_specs=[pl.BlockSpec((2, width, cols), lambda j, at: (0, 0, 0))] * count,
            out_specs=[
                pl.BlockSpec((1, width, cols), lambda j, at: (j, 0, 0)),
                pl.BlockSpec((1, cols, width), lambda j, at: (j, 0, 0)),
            ],
        ),
        out_shape=[
            jax.ShapeDtypeStruct((count, width, cols), F32),
            jax.ShapeDtypeStruct((count, cols, width), F32),
        ],
        compiler_params=pltpu.CompilerParams(vmem_limit_bytes=VMEM_BYTES),
        cost_estimate=estimate(width * cols, 12 * count * width * cols),
        name="spread",
    )(place.astype(jnp.int32)[None], *pieces)


def after(value, *others):
    return lax.optimization_barrier((value, others))[0]


def body(
    tokens,
    cotangent,
    router_noise,
    expert_ids,
    seat_order,
    gain_attn,
    w_qkv,
    w_out,
    gain_moe,
    w_router,
    w_up,
    w_down,
):
    image_count, half_len, width = tokens.shape
    rows = image_count * half_len
    expert_count = router_noise.shape[-1]
    n_owner = lax.axis_size("expert")
    n_ctx = lax.axis_size("ctx")
    n_dp = lax.axis_size("dp")
    here = lax.axis_index("ctx")
    my_dp = lax.axis_index("dp")
    held = w_up.shape[0]
    capacity = (2 * rows + expert_count - 1) // expert_count
    one_each = held == n_dp
    if one_each:
        parts, peers, axes = 2, n_owner * n_dp, ("expert", "dp")
        cap = capacity // parts
        slot_of = lambda e, at: (at // cap * peers + e) * cap + at % cap
        which = [my_dp] * parts
    else:
        parts, peers, axes = held // n_ctx, n_owner * n_ctx, ("expert", "ctx")
        cap = capacity
        slot_of = lambda e, at: ((e % parts) * peers + e // parts) * cap + at
        which = [here * parts + part for part in range(parts)]

    t1, t2, first_hot, second_hot = seats(
        expert_ids.reshape(rows, 2), seat_order.reshape(rows), expert_count, capacity, slot_of
    )
    dy_b = cotangent.reshape(rows, width)
    every = tuple(range(parts))
    dy_slots = seat_rows(t1, t2, dy_b, (), every, parts, peers, cap)
    dy_got = exchange(dy_slots, axes)

    tokens_f = after(tokens, dy_slots).reshape(rows, width).astype(F32)
    normed_a, unit_a, inv_a = norm_forward(tokens_f, gain_attn)
    normed_ab = normed_a.astype(BF)
    qkv_b = mm(normed_ab, w_qkv).astype(BF)
    kv_other = swap(qkv_b[:, width:])
    mixed_b, probs, inv_sum = attend(qkv_b, kv_other, rows)

    middle = tokens_f + mm(mixed_b, w_out)
    normed_m, _, _ = norm_forward(middle, gain_moe)
    routed_b = normed_m.astype(BF)
    logits = mm(routed_b, w_router) + router_noise.reshape(rows, expert_count)
    gate_probs = jax.nn.softmax(logits, axis=-1)
    gate_first = jnp.sum(jnp.where(first_hot, gate_probs, 0.0), axis=-1)
    gate_second = jnp.sum(jnp.where(second_hot, gate_probs, 0.0), axis=-1)

    sent = [
        seat_rows(
            t1, t2, routed_b, () if part else (gate_first, gate_second), (part,), parts, peers, cap
        )
        for part in every
    ]
    sent[0], dy_got = lax.optimization_barrier((sent[0], dy_got))
    x_got = [exchange(sent[0], axes)]
    outs, dx_back, dgates, kept = None, [], [], []
    for part in every:
        last = part == parts - 1
        x = x_got[part]
        if not last:
            x, following = lax.optimization_barrier((x, sent[part + 1]))
            x_got.append(exchange(following, axes))
        outs, dx, act, dhid, dp, *dg = run_expert(
            which[part].astype(jnp.int32)[None], part, parts, x, x_got[0], dy_got, outs, dgates, w_up, w_down
        )
        dgates += dg
        if not last:
            dx, x_got[-1] = lax.optimization_barrier((dx, x_got[-1]))
        if dx_back:
            dx, dx_back[-1], act = lax.optimization_barrier((dx, dx_back[-1], act))
        dx_back.append(exchange(dx, axes))
        kept.append((x_got[part], dp, act, dhid))
    if one_each:
        give, keep = both_weight_grads(kept, here, n_ctx, n_dp)
        dx_back, give, keep = lax.optimization_barrier((dx_back, give, keep))
        other = swap(give)
    else:
        mine, far = [], []
        for group in kept:
            give, keep = (
                lax.psum_scatter(
                    g.reshape(-1, g.shape[-1]), "dp", scatter_dimension=0, tiled=True
                ).reshape(g.shape[1:])
                for g in both_weight_grads([group], here, n_ctx, n_dp)
            )
            mine.append(keep)
            far.append(swap(give))
        pieces = [
            jnp.where(here == n // parts, mine[n % parts], far[n % parts]) for n in reversed(range(held))
        ]
    outs, dx_back = lax.optimization_barrier((outs, dx_back))
    returned = exchange(outs, axes)
    if one_each:
        blocks = []
        for n in range(n_dp):
            pick = lambda v: lax.dynamic_index_in_dim(v, lax.rem(my_dp + n, n_dp), 0, keepdims=False)
            blocks.append(add_up([pick(keep), pick(other)]))
        dx_back, blocks = lax.optimization_barrier((dx_back, blocks))
        pieces = [block if n == 0 else shift(block, "dp", n) for n, block in enumerate(blocks)]

    d_middle, d_branch_b, d_mixed_b, small = route_back(
        t1, t2, expert_ids.reshape(rows, 2), gate_probs, dy_b, middle, gain_moe, w_router, w_out, dx_back
    )

    pairs = width // 128
    calls = [(first, pairs // 3) for first in range(0, pairs, pairs // 3)]

    def call(n, grad):
        return attend_back(qkv_b, kv_other, mixed_b, grad, inv_sum, probs, rows, *calls[n])

    dq0, own0, far0 = call(0, d_mixed_b)
    dq1, own1, far1 = call(1, after(d_mixed_b, dq0))
    fars = [swap(far0), swap(far1)]
    result = unseat(t1, t2, after(middle, dq1), returned, parts)
    fars, pieces, result = lax.optimization_barrier((fars, pieces, result))
    grad_a, d_qkv_a = grad_qkv(
        normed_ab, [dq0, dq1], [own0, own1], fars, (mixed_b, d_branch_b, small)
    )
    sum_a = add_up(grad_a)
    d_mixed_b, sum_a = lax.optimization_barrier((d_mixed_b, sum_a))
    got_a = scatter_begin(sum_a, "dp")
    dq2, own2, far2 = call(2, d_mixed_b)
    got_a, dq2, own2, far2 = lax.optimization_barrier((got_a, dq2, own2, far2))
    got_a = scatter_begin(add_up(got_a), "expert")
    far2 = swap(far2)
    got_b, d_qkv_b = grad_qkv(normed_ab, [dq2], [own2], [far2])
    got_a, got_b[0] = lax.optimization_barrier((got_a, got_b[0]))
    got_a = gather_back(add_up(got_a), "expert")
    got_b = scatter_begin(add_up(got_b), "dp")
    got_a, got_b[0] = lax.optimization_barrier((got_a, got_b[0]))
    got_a = gather_back(jnp.stack(got_a), "dp")
    got_b, got_a[0] = lax.optimization_barrier((got_b, got_a[0]))
    got_b = scatter_begin(add_up(got_b), "expert")
    grad_up, grad_down = spread(after(pieces, got_a[0]), my_dp if one_each else jnp.int32(held - 1))
    got_b, grad_up = lax.optimization_barrier((got_b, grad_up))
    got_b = gather_back(add_up(got_b), "expert")
    got_b = gather_back(jnp.stack(got_b), "dp")
    got_a, got_b[0] = lax.optimization_barrier((got_a, got_b[0]))
    all_a = jnp.stack(got_a)
    all_a = (all_a, swap(all_a))

    d_normed_a = 0.0
    for first, d_qkv in ((0, d_qkv_a), (calls[2][0], after(d_qkv_b, all_a[0]))):
        start, wide = 128 * first, d_qkv.shape[1] // 3
        columns = [w_qkv[:, m * width + start : m * width + start + wide] for m in range(3)]
        d_normed_a = d_normed_a + mm(d_qkv, jnp.concatenate(columns, axis=1), NT)
    d_tokens_norm, _ = norm_backward(d_normed_a, unit_a, inv_a, gain_attn)
    d_tokens = d_middle + d_tokens_norm
    d_tokens, got_b = lax.optimization_barrier((d_tokens, got_b))

    all_b = jnp.stack(got_b)
    all_b = (all_b, swap(all_b))
    cols_a, cols_b, start_b = d_qkv_a.shape[1], d_qkv_b.shape[1], 128 * calls[2][0]
    spans = [
        [(m * cols_a // 3, 0, m * width, cols_a // 3) for m in range(3)]
        + [(cols_a, 1, 0, width), (cols_a + width, 2, 0, SMALL)],
        [(m * cols_b // 3, 0, m * width + start_b, cols_b // 3) for m in range(3)],
    ]
    grad_w_qkv, grad_w_out, small_sum, gain_sum = assemble(
        [all_a, all_b], spans, (3 * width, width, SMALL), w_qkv
    )
    n_small = small.shape[0]
    small_sum = small_sum[:, :n_small] + small_sum[:, n_small : 2 * n_small]
    return (
        result.reshape(image_count, half_len, width),
        d_tokens.reshape(image_count, half_len, width),
        gain_sum[:, 0] / gain_attn,
        grad_w_qkv,
        grad_w_out,
        small_sum[:, expert_count],
        small_sum[:, :expert_count],
        grad_up,
        grad_down,
    )


def solution(mesh):
    placed = (
        P(("expert", "dp"), "ctx", None),
        P(("expert", "dp"), "ctx", None),
        P(("expert", "dp"), "ctx", None),
        P(("expert", "dp"), "ctx", None),
        P(("expert", "dp"), "ctx"),
        P(),
        P(),
        P(),
        P(),
        P(),
        P("expert", None, None),
        P("expert", None, None),
    )
    return jax.shard_map(
        body,
        mesh=mesh,
        in_specs=placed,
        out_specs=(
            P(("expert", "dp"), "ctx", None),
            P(("expert", "dp"), "ctx", None),
            P(),
            P(),
            P(),
            P(),
            P(),
            P("expert", None, ("ctx", "dp")),
            P("expert", ("ctx", "dp"), None),
        ),
        check_vma=False,
    )
```

time: 565 us -> 523 us (0.926)
  blocking collectives: 44.9 us -> 0 us
  starting transfers between devices: 64.5 us -> 93.7 us
  waiting for transfers between devices: 95.6 us -> 78.3 us
  between operations: 15.2 us -> 1.6 us
  Pallas kernels: 269 us -> 279 us
  local copies, waits for them, and re-layouts: 27.4 us -> 18.7 us
    all_to_all x1 -> x0, blocking collectives: 44.9 us -> none  [exchange(): return lax.all_to_all(value, axes, 0, 0, tiled=True)]
    all_to_all x6, starting transfers between devices: 27 us -> 52 us  [exchange(): return lax.all_to_all(value, axes, 0, 0, tiled=True)]
    ppermute x26 -> x27, waiting for transfers between devices: 51.4 us -> 29.8 us  [shift(): return lax.ppermute(value, axis, [(i, (i + by) % n) for i in range(n)])]
    pallas_call x9 -> x13, Pallas kernels: 127 us -> 148 us  [the longest x2 58.7 us: run_expert(): pl.pallas_call(functools.partial(expert_kernel, part=part, parts=parts, s...]
    pallas_call x1, Pallas kernels: 48.2 us -> 40.9 us  [attend(): pl.pallas_call(functools.partial(attend_kernel, scale=1.0 / math.sqrt(wid...]
    squeeze x8 -> x4, local copies, waits for them, and re-layouts: 7.1 us -> 0.89 us  [scatter_begin(): pick = lambda at: lax.dynamic_index_in_dim(x, at, 0, keepdims=False)]
    convert_element_type x6 -> x7, other arithmetic: 5.12 us -> 11.1 us  [add_up(): return total.astype(BF)]
    ppermute x26 -> x27, starting transfers between devices: 35.8 us -> 40.8 us  [shift(): return lax.ppermute(value, axis, [(i, (i + by) % n) for i in range(n)])]
  transfers between devices with their start and end apart: 41 -> 42, of which waited for: 14 -> 16; matrix products, arithmetic and copies ran while one was open for 7% -> 8% of each run, Pallas kernels for 45% -> 50%
where the time goes in v2:
time: 523 us; the launch traced here: 515 us
  Pallas kernels  279 us (53%)
  starting transfers between devices  93.7 us (18%)
  waiting for transfers between devices  78.3 us (15%)
  other arithmetic  28.5 us (5%)
  local copies, waits for them, and re-layouts  18.7 us (4%)
  matrix products  14.8 us (3%)
    pallas_call x3, Pallas kernels, attend_back(): pl.pallas_call(functools.partial(attend_back_kernel, scale=1.0 / math.sqr...  63 us
    pallas_call x2, Pallas kernels, run_expert(): pl.pallas_call(functools.partial(expert_kernel, part=part, parts=parts, s...  58.7 us
    all_to_all x6, starting transfers between devices, exchange(): return lax.all_to_all(value, axes, 0, 0, tiled=True)  52 us
    all_to_all x6, waiting for transfers between devices, exchange(): return lax.all_to_all(value, axes, 0, 0, tiled=True)  42.2 us
    pallas_call x1, Pallas kernels, attend(): pl.pallas_call(functools.partial(attend_kernel, scale=1.0 / math.sqrt(wid...  40.9 us
    ppermute x27, starting transfers between devices, shift(): return lax.ppermute(value, axis, [(i, (i + by) % n) for i in range(n)])  40.8 us
    pallas_call x2, Pallas kernels, weight_grads(): pl.pallas_call(functools.partial(weights_kernel, count=len(acts), pieces=...  36.3 us
    ppermute x27, waiting for transfers between devices, shift(): return lax.ppermute(value, axis, [(i, (i + by) % n) for i in range(n)])  29.8 us
  transfers between devices with their start and end apart: 42, of which 16 were waited for; matrix products, arithmetic and copies ran while one was open for 8% of the time, Pallas kernels for 50%

profile of v2, /device:TPU:0, one launch (start us, length us, event | category | flops | bytes accessed | tf_op | source)
XLA Modules:
  0.0 514.5 jit_solution(12121961370822104944)
XLA Ops:
  6.9 6.5 %seat_rows.3 = bf16[16,128,768]{2,1,0:T(8,128)(2,1)} custom-call(s32[1,1024]{1,0:T(1,128)} %compare_select_fusion.1.t1, s32[1,1024]{1,0:T(1,128)} %compare_select_fusion.t2, bf16[1024,768]{1,0:T(8,128)(2,1)} %bitcast.120), custom_call_target="tpu_custom_call" | custom-call | flops 805306368 | bytes 786432 | tf_op jit(solution)/shard_map/seat_rows/pallas_call | solution.py:573
  13.4 8.5 %all-to-all-start = ((bf16[16,128,768]{2,1,0:T(8,128)(2,1)}), bf16[16,128,768]{2,1,0:T(8,128)(2,1)}, u32[]{:S(2)}, u32[]{:S(2)}) async-start(bf16[16,128,768]{2,1,0:T(8,128)(2,1)} %seat_rows.3), calls=%async_computation | async-start | bytes 6291456 | tf_op jit(solution)/shard_map/all_to_all | solution.py:709
  32.4 4.9 collective-permute-done.k1.v1
  38.9 40.9 %attend.1 = (bf16[1024,768]{1,0:T(8,128)(2,1)}, bf16[12,1024,2048]{2,1,0:T(8,128)(2,1)}, f32[1024,768]{1,0:T(8,128)}) custom-call(bf16[1024,2304]{1,0:T(8,128)(2,1)} %copy-done, bf16[1024,2304]{1,0:T(8,128)(2,1)} %copy-done, bf16[1024,1536]{1,0:T(8,128)(2,1)} %copy-done.1, bf16[1024,2304]{1,0:T(8,128)(2,1)} %copy-done, bf16[1024,1536]{1,0:T(8,128)(2,1)} %copy-done.1), custom_call_target="tpu_custom_call" | custom-call | flops 196608 | bytes 196608 | tf_op jit(solution)/shard_map/attend/pallas_call | solution.py:99
  89.1 6.7 %seat_rows.4 = bf16[16,72,768]{2,1,0:T(8,128)(2,1)} custom-call(s32[1,1024]{1,0:T(1,128)} %compare_select_fusion.1.t1, s32[1,1024]{1,0:T(1,128)} %compare_select_fusion.t2, f32[1,1024]{1,0:T(1,128)} %bitcast.149, f32[1,1024]{1,0:T(1,128)} %bitcast.148, bf16[1024,768]{1,0:T(8,128)(2,1)} %copy-done.5), custom_call_target="tpu_custom_call" | custom-call | flops 452984832 | bytes 786432 | tf_op jit(solution)/shard_map/seat_rows/pallas_call | solution.py:573
  95.8 11.0 %all-to-all-start.1 = ((bf16[16,72,768]{2,1,0:T(8,128)(2,1)}), bf16[16,72,768]{2,1,0:T(8,128)(2,1)S(1)}, u32[]{:S(2)}, u32[]{:S(2)}) async-start(bf16[16,72,768]{2,1,0:T(8,128)(2,1)} %seat_rows.4), calls=%async_computation.1 | async-start | bytes 3538944 | tf_op jit(solution)/shard_map/all_to_all | solution.py:709
  106.8 4.4 seat_rows.5
  111.2 33.2 %all-to-all-done.1.x_in.gate_in.refs_4_ = bf16[16,72,768]{2,1,0:T(8,128)(2,1)S(1)} async-done(((bf16[16,72,768]{2,1,0:T(8,128)(2,1)}), bf16[16,72,768]{2,1,0:T(8,128)(2,1)S(1)}, u32[]{:S(2)}, u32[]{:S(2)}) %all-to-all-start.1) | async-done | bytes 1769504 | tf_op jit(solution)/shard_map/all_to_all | solution.py:709
  144.4 9.0 %all-to-all-start.2 = ((bf16[16,64,768]{2,1,0:T(8,128)(2,1)}), bf16[16,64,768]{2,1,0:T(8,128)(2,1)S(1)}, u32[]{:S(2)}, u32[]{:S(2)}) async-start(bf16[16,64,768]{2,1,0:T(8,128)(2,1)} %seat_rows.5), calls=%async_computation.2 | async-start | bytes 3145728 | tf_op jit(solution)/shard_map/all_to_all | solution.py:709
  153.4 29.2 %expert.2 = (bf16[16,128,768]{2,1,0:T(8,128)(2,1)}, bf16[16,64,768]{2,1,0:T(8,128)(2,1)}, bf16[1024,3072]{1,0:T(8,128)(2,1)}, bf16[1024,3072]{1,0:T(8,128)(2,1)}...) custom-call(s32[1]{0:T(128)} %bitcast.9.which.at, bf16[16,72,768]{2,1,0:T(8,128)(2,1)} %copy-done.3, ...), custom_call_target="tpu_custom_call" | custom-call | flops 4831838208 | bytes 2359296 | tf_op jit(solution)/shard_map/expert/pallas_call | solution.py:395
  182.7 4.3 all-to-all-done.2.x_in.refs_5_
  186.9 7.6 %all-to-all-start.3 = ((bf16[16,64,768]{2,1,0:T(8,128)(2,1)}), bf16[16,64,768]{2,1,0:T(8,128)(2,1)S(1)}, u32[]{:S(2)}, u32[]{:S(2)}) async-start(bf16[16,64,768]{2,1,0:T(8,128)(2,1)} %get-tuple-element.137), calls=%async_computation.3 | async-start | bytes 3145728 | tf_op jit(solution)/shard_map/all_to_all | solution.py:709
  194.5 29.5 %expert.3 = (bf16[16,128,768]{2,1,0:T(8,128)(2,1)}, bf16[16,72,768]{2,1,0:T(8,128)(2,1)}, bf16[1024,3072]{1,0:T(8,128)(2,1)}, bf16[1024,3072]{1,0:T(8,128)(2,1)}, bf16[1024,768]{1,0:T(8,128)(2,1)}) custom-call(s32[1]{0:T(128)} %bitcast.9.which.at, bf16[16,64,768]{2,1,0:T(8,128)(2,1)} %copy-done.10, ...), custom_call_target="tpu_custom_call", output_to_operand_aliasing={{0}: (4, {})} | custom-call | flops 4831838208 | bytes 2359296 | tf_op jit(solution)/shard_map/expert/pallas_call | solution.py:395
  224.0 4.1 all-to-all-done.3.refs_0_
  228.0 7.8 %all-to-all-start.4 = ((bf16[16,72,768]{2,1,0:T(8,128)(2,1)}), bf16[16,72,768]{2,1,0:T(8,128)(2,1)S(1)}, u32[]{:S(2)}, u32[]{:S(2)}) async-start(bf16[16,72,768]{2,1,0:T(8,128)(2,1)} %get-tuple-element.140), calls=%async_computation.4 | async-start | bytes 3538944 | tf_op jit(solution)/shard_map/all_to_all | solution.py:709
  235.8 19.5 %weight_grads.2 = (bf16[4,2,768,384]{3,2,1,0:T(8,128)(2,1)}, bf16[768,2048]{1,0:T(8,128)(2,1)}, bf16[768,2048]{1,0:T(8,128)(2,1)}) custom-call(s32[1]{0:T(128)} %bitcast.12.at.core, bf16[1024,3072]{1,0:T(8,128)(2,1)} %get-tuple-element.141.refs_0_, bf16[1024,3072]{1,0:T(8,128)(2,1)} %get-tuple-element.142.refs_1_, ...), custom_call_target="tpu_custom_call" | custom-call | flops 393216 | bytes 393216 | tf_op jit(solution)/shard_map/weight_grads/pallas_call | solution.py:475
  255.4 16.7 %weight_grads.3 = bf16[4,2,768,384]{3,2,1,0:T(8,128)(2,1)} custom-call(s32[1]{0:T(128)} %bitcast.13.at.core, bf16[1024,3072]{1,0:T(8,128)(2,1)} %get-tuple-element.141.refs_0_, bf16[1024,3072]{1,0:T(8,128)(2,1)} %get-tuple-element.142.refs_1_, bf16[1024,3072]{1,0:T(8,128)(2,1)} %get-tuple-element.143.refs_2_, bf16[1024,3072]{1,0:T(8,128)(2,1)} %get-tuple-element.144.refs_3_, ...), custom_call_target="tpu_custom_call" | custom-call | flops 393216 | bytes 393216 | tf_op jit(solution)/shard_map/weight_grads/pallas_call | solution.py:475
  273.9 8.2 %all-to-all-start.5 = ((bf16[16,128,768]{2,1,0:T(8,128)(2,1)}), bf16[16,128,768]{2,1,0:T(8,128)(2,1)}, u32[]{:S(2)}, u32[]{:S(2)}) async-start(bf16[16,128,768]{2,1,0:T(8,128)(2,1)} %get-tuple-element.171), calls=%async_computation.5 | async-start | bytes 6291456 | tf_op jit(solution)/shard_map/all_to_all | solution.py:709
  282.7 6.8 %fusion.30 = (bf16[2,768,384]{2,1,0:T(8,128)(2,1)}, bf16[2,768,384]{2,1,0:T(8,128)(2,1)}, bf16[2,768,384]{2,1,0:T(8,128)(2,1)}, bf16[2,768,384]{2,1,0:T(8,128)(2,1)}) fusion(bf16[4,2,768,384]{3,2,1,0:T(8,128)(2,1)} %collective-permute-done.1, s32[]{:T(128)S(6)} %select_n.189, bf16[4,2,768,384]{3,2,1,0:T(8,128)(2,1)} %weight_grads.3, s32[]{:T(128)S(6)} %select_n.188, ...), kind=kLoop, calls=%fused_computation.41 | loop fusion | flops 9437184 | bytes 14155792 | tf_op jit(solution)/shard_map/convert_element_type | solution.py:729
  297.6 17.3 %route_back.1 = (f32[1024,768]{1,0:T(8,128)}, bf16[1024,768]{1,0:T(8,128)(2,1)}, bf16[1024,768]{1,0:T(8,128)(2,1)}, f32[24,768]{1,0:T(8,128)}) custom-call(s32[1024,1]{1,0:T(8,128)} %get-tuple-element.296.t1, s32[1024,1]{1,0:T(8,128)} %get-tuple-element.295.t2, s32[1024,2]{1,0:T(8,128)} %bitcast.117, f32[1024,16]{1,0:T(8,128)} %get-tuple-element.276.probs, ...), custom_call_target="tpu_custom_call" | custom-call | flops 196608 | bytes 196608 | tf_op jit(solution)/shard_map/route_back/pallas_call | solution.py:679
  314.9 21.0 %attend_back.3 = (bf16[1024,256]{1,0:T(8,128)(2,1)}, f32[2,1024,256]{2,1,0:T(8,128)}, bf16[2,1024,256]{2,1,0:T(8,128)(2,1)}) custom-call(bf16[1024,2304]{1,0:T(8,128)(2,1)} %copy-done, bf16[1024,2304]{1,0:T(8,128)(2,1)} %copy-done, bf16[1024,1536]{1,0:T(8,128)(2,1)} %copy-done.1, bf16[1024,2304]{1,0:T(8,128)(2,1)} %copy-done, bf16[1024,1536]{1,0:T(8,128)(2,1)} %copy-done.1, ...), custom_call_target="tpu_custom_call" | custom-call | flops 196608 | bytes 196608 | tf_op jit(solution)/shard_map/attend_back/pallas_call | solution.py:185
  335.9 21.1 %attend_back.4 = (bf16[1024,256]{1,0:T(8,128)(2,1)}, f32[2,1024,256]{2,1,0:T(8,128)}, bf16[2,1024,256]{2,1,0:T(8,128)(2,1)}) custom-call(bf16[1024,2304]{1,0:T(8,128)(2,1)} %copy-done, bf16[1024,2304]{1,0:T(8,128)(2,1)} %copy-done, bf16[1024,1536]{1,0:T(8,128)(2,1)} %copy-done.1, bf16[1024,2304]{1,0:T(8,128)(2,1)} %copy-done, bf16[1024,1536]{1,0:T(8,128)(2,1)} %copy-done.1, ...), custom_call_target="tpu_custom_call" | custom-call | flops 196608 | bytes 196608 | tf_op jit(solution)/shard_map/attend_back/pallas_call | solution.py:185
  357.5 7.8 %unseat.1 = bf16[1024,768]{1,0:T(8,128)(2,1)} custom-call(s32[1024,1]{1,0:T(8,128)} %get-tuple-element.296.t1, s32[1024,1]{1,0:T(8,128)} %get-tuple-element.295.t2, f32[1024,768]{1,0:T(8,128)} %copy-done.2, bf16[16,128,768]{2,1,0:T(8,128)(2,1)} %all-to-all-done.5.back), custom_call_target="tpu_custom_call" | custom-call | flops 196608 | bytes 196608 | tf_op jit(solution)/shard_map/unseat/pallas_call | solution.py:619
  368.1 7.4 %collective-permute-done.6.refs_3_ = bf16[2,768,384]{2,1,0:T(8,128)(2,1)} collective-permute-done((bf16[2,768,384]{2,1,0:T(8,128)(2,1)}, bf16[2,768,384]{2,1,0:T(8,128)(2,1)}, u32[]{:S(2)}, u32[]{:S(2)}) %collective-permute-start.6) | collective-permute-done | bytes 1179680 | tf_op jit(solution)/shard_map/ppermute | solution.py:714
  375.5 7.7 %grad_qkv.4 = (bf16[384,2432]{1,0:T(8,128)(2,1)}, bf16[1024,1536]{1,0:T(8,128)(2,1)}) custom-call(s32[1]{0:T(128)} %bitcast.12.at.core, bf16[1024,768]{1,0:T(8,128)(2,1)} %copy-done.4, bf16[1024,256]{1,0:T(8,128)(2,1)} %get-tuple-element.162.refs_0_, bf16[1024,256]{1,0:T(8,128)(2,1)} %get-tuple-element.169.refs_1_, ...), custom_call_target="tpu_custom_call" | custom-call | flops 196608 | bytes 196608 | tf_op jit(solution)/shard_map/grad_qkv/pallas_call | solution.py:258
  383.2 6.1 %grad_qkv.5 = bf16[384,2432]{1,0:T(8,128)(2,1)} custom-call(s32[1]{0:T(128)} %bitcast.13.at.core, bf16[1024,768]{1,0:T(8,128)(2,1)} %copy-done.4, bf16[1024,1536]{1,0:T(8,128)(2,1)} %get-tuple-element.180.refs_0_, bf16[1024,768]{1,0:T(8,128)(2,1)} %get-tuple-element.126.o_ref.refs_6_.refs_1_, bf16[1024,768]{1,0:T(8,128)(2,1)} %get-tuple-element.178.refs_7_.refs_2_, ...), custom_call_target="tpu_custom_call" | custom-call | flops 196608 | bytes 196608 | tf_op jit(solution)/shard_map/grad_qkv/pallas_call | solution.py:258
  397.5 20.9 %attend_back.5 = (bf16[1024,256]{1,0:T(8,128)(2,1)}, f32[2,1024,256]{2,1,0:T(8,128)}, bf16[2,1024,256]{2,1,0:T(8,128)(2,1)}) custom-call(bf16[1024,2304]{1,0:T(8,128)(2,1)} %copy-done, bf16[1024,2304]{1,0:T(8,128)(2,1)} %copy-done, bf16[1024,1536]{1,0:T(8,128)(2,1)} %copy-done.1, bf16[1024,2304]{1,0:T(8,128)(2,1)} %copy-done, bf16[1024,1536]{1,0:T(8,128)(2,1)} %copy-done.1, ...), custom_call_target="tpu_custom_call" | custom-call | flops 196608 | bytes 196608 | tf_op jit(solution)/shard_map/attend_back/pallas_call | solution.py:185
  418.8 4.1 collective-permute-start.12
  426.4 4.1 grad_qkv.6
  441.9 4.6 collective-permute-done.16
  463.9 6.5 %spread.1 = (f32[4,768,384]{2,1,0:T(8,128)}, f32[4,384,768]{2,1,0:T(8,128)}) custom-call(s32[1]{0:T(128)} %bitcast.9.which.at, bf16[2,768,384]{2,1,0:T(8,128)(2,1)} %get-tuple-element.215.refs_0_, bf16[2,768,384]{2,1,0:T(8,128)(2,1)} %copy-done.21, bf16[2,768,384]{2,1,0:T(8,128)(2,1)} %copy-done.22, bf16[2,768,384]{2,1,0:T(8,128)(2,1)} %collective-permute-done.6.refs_3_), custom_call_target="tpu_custom_call" | custom-call | flops 73728 | bytes 3538944 | tf_op jit(solution)/shard_map/spread/pallas_call | solution.py:803
  499.8 9.8 %assemble.1 = (f32[768,2304]{1,0:T(8,128)}, f32[768,768]{1,0:T(8,128)}, f32[768,128]{1,0:T(8,128)}, f32[768,1]{1,0:T(8,128)}) custom-call(s32[3]{0:T(128)} %pad_add_fusion.at, bf16[768,2304]{1,0:T(8,128)(2,1)} %w_ref.1, bf16[4,4,24,2432]{3,2,1,0:T(8,128)(2,1)} %copy-done.13, bf16[4,4,24,768]{3,2,1,0:T(8,128)(2,1)} %copy-done.18, ...), custom_call_target="tpu_custom_call" | custom-call | flops 442368 | bytes 5308416 | tf_op jit(solution)/shard_map/assemble/pallas_call | solution.py:772
  (204 shorter events, 116.0 us)
Async XLA Ops:
  13.4 82.4 %all-to-all-start = ((bf16[16,128,768]{2,1,0:T(8,128)(2,1)}), bf16[16,128,768]{2,1,0:T(8,128)(2,1)}, u32[]{:S(2)}, u32[]{:S(2)}) async-start(bf16[16,128,768]{2,1,0:T(8,128)(2,1)} %seat_rows.3), calls=%async_computation | async-start | bytes 6291456 | tf_op jit(solution)/shard_map/all_to_all | solution.py:709
  95.8 48.7 %all-to-all-start.1 = ((bf16[16,72,768]{2,1,0:T(8,128)(2,1)}), bf16[16,72,768]{2,1,0:T(8,128)(2,1)S(1)}, u32[]{:S(2)}, u32[]{:S(2)}) async-start(bf16[16,72,768]{2,1,0:T(8,128)(2,1)} %seat_rows.4), calls=%async_computation.1 | async-start | bytes 3538944 | tf_op jit(solution)/shard_map/all_to_all | solution.py:709
  144.4 42.5 %all-to-all-start.2 = ((bf16[16,64,768]{2,1,0:T(8,128)(2,1)}), bf16[16,64,768]{2,1,0:T(8,128)(2,1)S(1)}, u32[]{:S(2)}, u32[]{:S(2)}) async-start(bf16[16,64,768]{2,1,0:T(8,128)(2,1)} %seat_rows.5), calls=%async_computation.2 | async-start | bytes 3145728 | tf_op jit(solution)/shard_map/all_to_all | solution.py:709
  186.9 41.1 %all-to-all-start.3 = ((bf16[16,64,768]{2,1,0:T(8,128)(2,1)}), bf16[16,64,768]{2,1,0:T(8,128)(2,1)S(1)}, u32[]{:S(2)}, u32[]{:S(2)}) async-start(bf16[16,64,768]{2,1,0:T(8,128)(2,1)} %get-tuple-element.137), calls=%async_computation.3 | async-start | bytes 3145728 | tf_op jit(solution)/shard_map/all_to_all | solution.py:709
  228.0 44.7 %all-to-all-start.4 = ((bf16[16,72,768]{2,1,0:T(8,128)(2,1)}), bf16[16,72,768]{2,1,0:T(8,128)(2,1)S(1)}, u32[]{:S(2)}, u32[]{:S(2)}) async-start(bf16[16,72,768]{2,1,0:T(8,128)(2,1)} %get-tuple-element.140), calls=%async_computation.4 | async-start | bytes 3538944 | tf_op jit(solution)/shard_map/all_to_all | solution.py:709
  272.7 10.0 %collective-permute-start.1 = (bf16[4,2,768,384]{3,2,1,0:T(8,128)(2,1)}, bf16[4,2,768,384]{3,2,1,0:T(8,128)(2,1)}, u32[]{:S(2)}, u32[]{:S(2)}) collective-permute-start(bf16[4,2,768,384]{3,2,1,0:T(8,128)(2,1)} %get-tuple-element.155), channel_id=1, source_target_pairs={{0,4},{4,0},{1,5},{5,1},{2,6},{6,2},{3,7},{7,3},{8,12},{12,8},{9,1... | collective-permute-start | bytes 14155784 | tf_op jit(solution)/shard_map/ppermute | solution.py:705
  273.9 83.6 %all-to-all-start.5 = ((bf16[16,128,768]{2,1,0:T(8,128)(2,1)}), bf16[16,128,768]{2,1,0:T(8,128)(2,1)}, u32[]{:S(2)}, u32[]{:S(2)}) async-start(bf16[16,128,768]{2,1,0:T(8,128)(2,1)} %get-tuple-element.171), calls=%async_computation.5 | async-start | bytes 6291456 | tf_op jit(solution)/shard_map/all_to_all | solution.py:709
  289.5 75.9 %collective-permute-start.4 = (bf16[2,768,384]{2,1,0:T(8,128)(2,1)}, bf16[2,768,384]{2,1,0:T(8,128)(2,1)S(1)}, u32[]{:S(2)}, u32[]{:S(2)}) collective-permute-start(bf16[2,768,384]{2,1,0:T(8,128)(2,1)} %get-tuple-element.166), channel_id=1, source_target_pairs={{0,1},{1,2},{2,3},{3,0},{4,5},{5,6},{6,7},{7,4},{8,9},{9,10},{10,1... | collective-permute-start | bytes 3538952 | tf_op jit(solution)/shard_map/ppermute | solution.py:714
  291.3 76.8 %collective-permute-start.5 = (bf16[2,768,384]{2,1,0:T(8,128)(2,1)}, bf16[2,768,384]{2,1,0:T(8,128)(2,1)S(1)}, u32[]{:S(2)}, u32[]{:S(2)}) collective-permute-start(bf16[2,768,384]{2,1,0:T(8,128)(2,1)} %get-tuple-element.167), channel_id=1, source_target_pairs={{0,2},{1,3},{2,0},{3,1},{4,6},{5,7},{6,4},{7,5},{8,10},{9,11},{10,... | collective-permute-start | bytes 3538952 | tf_op jit(solution)/shard_map/ppermute | solution.py:714
  292.8 82.7 %collective-permute-start.6 = (bf16[2,768,384]{2,1,0:T(8,128)(2,1)}, bf16[2,768,384]{2,1,0:T(8,128)(2,1)}, u32[]{:S(2)}, u32[]{:S(2)}) collective-permute-start(bf16[2,768,384]{2,1,0:T(8,128)(2,1)} %get-tuple-element.168), channel_id=1, source_target_pairs={{0,3},{1,0},{2,1},{3,2},{4,7},{5,4},{6,5},{7,6},{8,11},{9,8},{10,9... | collective-permute-start | bytes 3538952 | tf_op jit(solution)/shard_map/ppermute | solution.py:714
  357.0 8.3 %collective-permute-start.3 = (bf16[2,1024,256]{2,1,0:T(8,128)(2,1)}, bf16[2,1024,256]{2,1,0:T(8,128)(2,1)S(1)}, u32[]{:S(2)}, u32[]{:S(2)}) collective-permute-start(bf16[2,1024,256]{2,1,0:T(8,128)(2,1)} %get-tuple-element.164), channel_id=1, source_target_pairs={{0,4},{4,0},{1,5},{5,1},{2,6},{6,2},{3,7},{7,3},{8,12},{12,8},{9,1... | collective-permute-start | bytes 3145736 | tf_op jit(solution)/shard_map/ppermute | solution.py:705
  357.0 8.3 %collective-permute-start.2 = (bf16[2,1024,256]{2,1,0:T(8,128)(2,1)}, bf16[2,1024,256]{2,1,0:T(8,128)(2,1)}, u32[]{:S(2)}, u32[]{:S(2)}) collective-permute-start(bf16[2,1024,256]{2,1,0:T(8,128)(2,1)} %get-tuple-element.161), channel_id=1, source_target_pairs={{0,4},{4,0},{1,5},{5,1},{2,6},{6,2},{3,7},{7,3},{8,12},{12,8},{9,1... | collective-permute-start | bytes 3145736 | tf_op jit(solution)/shard_map/ppermute | solution.py:705
  391.4 27.0 %collective-permute-start.10 = (bf16[96,2432]{1,0:T(8,128)(2,1)S(1)}, bf16[96,2432]{1,0:T(8,128)(2,1)S(1)}, u32[]{:S(2)}, u32[]{:S(2)}) collective-permute-start(bf16[96,2432]{1,0:T(8,128)(2,1)S(1)} %get-tuple-element.287), channel_id=1, source_target_pairs={{0,3},{1,0},{2,1},{3,2},{4,7},{5,4},{6,5},{7,6},{8,11},{9,8},{10,9... | collective-permute-start | bytes 1400840 | tf_op jit(solution)/shard_map/ppermute | solution.py:714
  394.4 23.9 %collective-permute-start.8 = (bf16[96,2432]{1,0:T(8,128)(2,1)S(1)}, bf16[96,2432]{1,0:T(8,128)(2,1)S(1)}, u32[]{:S(2)}, u32[]{:S(2)}) collective-permute-start(bf16[96,2432]{1,0:T(8,128)(2,1)S(1)} %get-tuple-element.289), channel_id=1, source_target_pairs={{0,1},{1,2},{2,3},{3,0},{4,5},{5,6},{6,7},{7,4},{8,9},{9,10},{10,1... | collective-permute-start | bytes 1400840 | tf_op jit(solution)/shard_map/ppermute | solution.py:714
  394.4 23.9 %collective-permute-start.9 = (bf16[96,2432]{1,0:T(8,128)(2,1)S(1)}, bf16[96,2432]{1,0:T(8,128)(2,1)S(1)}, u32[]{:S(2)}, u32[]{:S(2)}) collective-permute-start(bf16[96,2432]{1,0:T(8,128)(2,1)S(1)} %get-tuple-element.288), channel_id=1, source_target_pairs={{0,2},{1,3},{2,0},{3,1},{4,6},{5,7},{6,4},{7,5},{8,10},{9,11},{10,... | collective-permute-start | bytes 1400840 | tf_op jit(solution)/shard_map/ppermute | solution.py:714
  418.8 15.0 %collective-permute-start.12 = (bf16[24,2432]{1,0:T(8,128)(2,1)S(1)}, bf16[24,2432]{1,0:T(8,128)(2,1)S(1)}, u32[]{:S(2)}, u32[]{:S(2)}) collective-permute-start(bf16[24,2432]{1,0:T(8,128)(2,1)S(1)} %get-tuple-element.299), channel_id=1, source_target_pairs={{0,8},{8,16},{16,24},{24,0},{1,9},{9,17},{17,25},{25,1},{2,10},{10... | collective-permute-start | bytes 350216 | tf_op jit(solution)/shard_map/ppermute | solution.py:714
  422.9 10.9 %collective-permute-start.13 = (bf16[24,2432]{1,0:T(8,128)(2,1)S(1)}, bf16[24,2432]{1,0:T(8,128)(2,1)S(1)}, u32[]{:S(2)}, u32[]{:S(2)}) collective-permute-start(bf16[24,2432]{1,0:T(8,128)(2,1)S(1)} %get-tuple-element.298), channel_id=1, source_target_pairs={{0,16},{8,24},{16,0},{24,8},{1,17},{9,25},{17,1},{25,9},{2,18},{10... | collective-permute-start | bytes 350216 | tf_op jit(solution)/shard_map/ppermute | solution.py:714
  422.9 10.9 %collective-permute-start.14 = (bf16[24,2432]{1,0:T(8,128)(2,1)S(1)}, bf16[24,2432]{1,0:T(8,128)(2,1)S(1)}, u32[]{:S(2)}, u32[]{:S(2)}) collective-permute-start(bf16[24,2432]{1,0:T(8,128)(2,1)S(1)} %get-tuple-element.297), channel_id=1, source_target_pairs={{0,24},{8,0},{16,8},{24,16},{1,25},{9,1},{17,9},{25,17},{2,26},{10... | collective-permute-start | bytes 350216 | tf_op jit(solution)/shard_map/ppermute | solution.py:714
  434.0 7.9 %collective-permute-start.15 = (bf16[24,2432]{1,0:T(8,128)(2,1)S(1)}, bf16[24,2432]{1,0:T(8,128)(2,1)S(1)}, u32[]{:S(2)}, u32[]{:S(2)}) collective-permute-start(bf16[24,2432]{1,0:T(8,128)(2,1)S(1)} %add_convert_fusion.8), channel_id=1, source_target_pairs={{0,8},{8,16},{16,24},{24,0},{1,9},{9,17},{17,25},{25,1},{2,10},{10... | collective-permute-start | bytes 350216 | tf_op jit(solution)/shard_map/ppermute | solution.py:714
  434.7 11.8 %collective-permute-start.16 = (bf16[24,2432]{1,0:T(8,128)(2,1)S(1)}, bf16[24,2432]{1,0:T(8,128)(2,1)S(1)}, u32[]{:S(2)}, u32[]{:S(2)}) collective-permute-start(bf16[24,2432]{1,0:T(8,128)(2,1)S(1)} %add_convert_fusion.8), channel_id=1, source_target_pairs={{0,16},{8,24},{16,0},{24,8},{1,17},{9,25},{17,1},{25,9},{2,18},{10... | collective-permute-start | bytes 350216 | tf_op jit(solution)/shard_map/ppermute | solution.py:714
  437.4 9.1 %collective-permute-start.17 = (bf16[24,2432]{1,0:T(8,128)(2,1)S(1)}, bf16[24,2432]{1,0:T(8,128)(2,1)S(1)}, u32[]{:S(2)}, u32[]{:S(2)}) collective-permute-start(bf16[24,2432]{1,0:T(8,128)(2,1)S(1)} %add_convert_fusion.8), channel_id=1, source_target_pairs={{0,24},{8,0},{16,8},{24,16},{1,25},{9,1},{17,9},{25,17},{2,26},{10... | collective-permute-start | bytes 350216 | tf_op jit(solution)/shard_map/ppermute | solution.py:714
  447.4 7.9 %collective-permute-start.21 = (bf16[96,768]{1,0:T(8,128)(2,1)S(1)}, bf16[96,768]{1,0:T(8,128)(2,1)S(1)}, u32[]{:S(2)}, u32[]{:S(2)}) collective-permute-start(bf16[96,768]{1,0:T(8,128)(2,1)S(1)} %get-tuple-element.291), channel_id=1, source_target_pairs={{0,3},{1,0},{2,1},{3,2},{4,7},{5,4},{6,5},{7,6},{8,11},{9,8},{10,9... | collective-permute-start | bytes 442376 | tf_op jit(solution)/shard_map/ppermute | solution.py:714
  456.1 14.3 %collective-permute-start.25 = (bf16[24,768]{1,0:T(8,128)(2,1)}, bf16[24,768]{1,0:T(8,128)(2,1)}, u32[]{:S(2)}, u32[]{:S(2)}) collective-permute-start(bf16[24,768]{1,0:T(8,128)(2,1)} %get-tuple-element.303), channel_id=1, source_target_pairs={{0,8},{8,16},{16,24},{24,0},{1,9},{9,17},{17,25},{25,1},{2,10},{10... | collective-permute-start | bytes 110600 | tf_op jit(solution)/shard_map/ppermute | solution.py:714
  459.1 12.3 %collective-permute-start.26 = (bf16[24,768]{1,0:T(8,128)(2,1)S(1)}, bf16[24,768]{1,0:T(8,128)(2,1)}, u32[]{:S(2)}, u32[]{:S(2)}) collective-permute-start(bf16[24,768]{1,0:T(8,128)(2,1)S(1)} %get-tuple-element.302), channel_id=1, source_target_pairs={{0,16},{8,24},{16,0},{24,8},{1,17},{9,25},{17,1},{25,9},{2,18},{10... | collective-permute-start | bytes 110600 | tf_op jit(solution)/shard_map/ppermute | solution.py:714
  459.1 12.3 %collective-permute-start.27 = (bf16[24,768]{1,0:T(8,128)(2,1)S(1)}, bf16[24,768]{1,0:T(8,128)(2,1)}, u32[]{:S(2)}, u32[]{:S(2)}) collective-permute-start(bf16[24,768]{1,0:T(8,128)(2,1)S(1)} %get-tuple-element.301), channel_id=1, source_target_pairs={{0,24},{8,0},{16,8},{24,16},{1,25},{9,1},{17,9},{25,17},{2,26},{10... | collective-permute-start | bytes 110600 | tf_op jit(solution)/shard_map/ppermute | solution.py:714
  461.5 23.1 %collective-permute-start.22 = (bf16[4,24,2432]{2,1,0:T(8,128)(2,1)S(1)}, bf16[4,24,2432]{2,1,0:T(8,128)(2,1)}, u32[]{:S(2)}, u32[]{:S(2)}) collective-permute-start(bf16[4,24,2432]{2,1,0:T(8,128)(2,1)S(1)} %pad_maximum_fusion.2), channel_id=1, source_target_pairs={{0,1},{1,2},{2,3},{3,0},{4,5},{5,6},{6,7},{7,4},{8,9},{9,10},{10,1... | collective-permute-start | bytes 1400840 | tf_op jit(solution)/shard_map/ppermute | solution.py:714
  463.2 23.5 %collective-permute-start.23 = (bf16[4,24,2432]{2,1,0:T(8,128)(2,1)S(1)}, bf16[4,24,2432]{2,1,0:T(8,128)(2,1)}, u32[]{:S(2)}, u32[]{:S(2)}) collective-permute-start(bf16[4,24,2432]{2,1,0:T(8,128)(2,1)S(1)} %pad_maximum_fusion.2), channel_id=1, source_target_pairs={{0,2},{1,3},{2,0},{3,1},{4,6},{5,7},{6,4},{7,5},{8,10},{9,11},{10,... | collective-permute-start | bytes 1400840 | tf_op jit(solution)/shard_map/ppermute | solution.py:714
  470.4 16.4 %collective-permute-start.24 = (bf16[4,24,2432]{2,1,0:T(8,128)(2,1)S(1)}, bf16[4,24,2432]{2,1,0:T(8,128)(2,1)S(1)}, u32[]{:S(2)}, u32[]{:S(2)}) collective-permute-start(bf16[4,24,2432]{2,1,0:T(8,128)(2,1)S(1)} %pad_maximum_fusion.2), channel_id=1, source_target_pairs={{0,3},{1,0},{2,1},{3,2},{4,7},{5,4},{6,5},{7,6},{8,11},{9,8},{10,9... | collective-permute-start | bytes 1400840 | tf_op jit(solution)/shard_map/ppermute | solution.py:714
  482.5 14.3 %collective-permute-start.31 = (bf16[4,24,768]{2,1,0:T(8,128)(2,1)S(1)}, bf16[4,24,768]{2,1,0:T(8,128)(2,1)S(1)}, u32[]{:S(2)}, u32[]{:S(2)}) collective-permute-start(bf16[4,24,768]{2,1,0:T(8,128)(2,1)S(1)} %pad_maximum_fusion.3), channel_id=1, source_target_pairs={{0,1},{1,2},{2,3},{3,0},{4,5},{5,6},{6,7},{7,4},{8,9},{9,10},{10,1... | collective-permute-start | bytes 442376 | tf_op jit(solution)/shard_map/ppermute | solution.py:714
  483.2 13.5 %collective-permute-start.32 = (bf16[4,24,768]{2,1,0:T(8,128)(2,1)S(1)}, bf16[4,24,768]{2,1,0:T(8,128)(2,1)S(1)}, u32[]{:S(2)}, u32[]{:S(2)}) collective-permute-start(bf16[4,24,768]{2,1,0:T(8,128)(2,1)S(1)} %pad_maximum_fusion.3), channel_id=1, source_target_pairs={{0,2},{1,3},{2,0},{3,1},{4,6},{5,7},{6,4},{7,5},{8,10},{9,11},{10,... | collective-permute-start | bytes 442376 | tf_op jit(solution)/shard_map/ppermute | solution.py:714
  484.6 12.2 %collective-permute-start.33 = (bf16[4,24,768]{2,1,0:T(8,128)(2,1)S(1)}, bf16[4,24,768]{2,1,0:T(8,128)(2,1)S(1)}, u32[]{:S(2)}, u32[]{:S(2)}) collective-permute-start(bf16[4,24,768]{2,1,0:T(8,128)(2,1)S(1)} %pad_maximum_fusion.3), channel_id=1, source_target_pairs={{0,3},{1,0},{2,1},{3,2},{4,7},{5,4},{6,5},{7,6},{8,11},{9,8},{10,9... | collective-permute-start | bytes 442376 | tf_op jit(solution)/shard_map/ppermute | solution.py:714
  488.2 10.8 %collective-permute-start.34 = (bf16[4,4,24,2432]{3,2,1,0:T(8,128)(2,1)S(1)}, bf16[4,4,24,2432]{3,2,1,0:T(8,128)(2,1)}, u32[]{:S(2)}, u32[]{:S(2)}) collective-permute-start(bf16[4,4,24,2432]{3,2,1,0:T(8,128)(2,1)S(1)} %pad_maximum_fusion.refs_0_), channel_id=1, source_target_pairs={{0,4},{4,0},{1,5},{5,1},{2,6},{6,2},{3,7},{7,3},{8,12},{12,8},{9,1... | collective-permute-start | bytes 5603336 | tf_op jit(solution)/shard_map/ppermute | solution.py:705
  (46 other events, 246.9 us)

commit v3 on v2

--- a/solution.py
+++ b/solution.py
@@ -46,11 +46,43 @@
     return (inner_sum * inv_scale, jnp.sum(gradient * unit_rows, axis=0))
 
 
+def project_kernel(x_ref, gain, w_ref, normed_ref, q_ref, kv_ref):
+    width = x_ref.shape[1]
+    normed = norm_forward(x_ref[...].astype(F32), gain[...])[0].astype(BF)
+    normed_ref[...] = normed
+    out = mm(normed, w_ref[...]).astype(BF)
+    q_ref[...] = out[:, 0:width]
+    kv_ref[...] = out[:, width:]
+
+
+def project(x, gain, w_qkv, block=256):
+    rows, width = x.shape
+    line = lambda cols: pl.BlockSpec((block, cols), lambda i: (i, 0))
+    return pl.pallas_call(
+        project_kernel,
+        grid=(rows // block,),
+        in_specs=[
+            line(width),
+            pl.BlockSpec((1, width), lambda i: (0, 0)),
+            pl.BlockSpec(w_qkv.shape, lambda i: (0, 0)),
+        ],
+        out_specs=[line(width), line(width), line(2 * width)],
+        out_shape=[jax.ShapeDtypeStruct((rows, n * width), BF) for n in (1, 1, 2)],
+        compiler_params=pltpu.CompilerParams(vmem_limit_bytes=VMEM_BYTES),
+        cost_estimate=estimate(6 * rows * width * width, 20 * rows * width),
+        name="project",
+    )(x, gain[None], w_qkv)
+
+
 def attend_kernel(q_ref, k0, k1, v0, v1, o_ref, p_ref, li_ref, vext, ksize, *, scale):
     half = k0.shape[0]
 
     def largest(v):
-        return jnp.max(jnp.sum(v * v, axis=1, keepdims=True))
+        same = lax.broadcasted_iota(jnp.int32, (128, 128), 0) // 64 == (
+            lax.broadcasted_iota(jnp.int32, (128, 128), 1) // 64
+        )
+        squares = (v.astype(F32) * v.astype(F32)).astype(BF)
+        return 1.01 * jnp.max(mm(squares, same.astype(BF)), axis=0, keepdims=True)
 
     @pl.when(pl.program_id(1) == 0)
     def _():
@@ -59,12 +91,12 @@
         vext[half:, 0:128] = v1[...]
         vext[0:half, 128:256] = ones
         vext[half:, 128:256] = ones
-        ksize[0] = jnp.maximum(largest(k0[...].astype(F32)), largest(k1[...].astype(F32)))
+        ksize[...] = jnp.maximum(largest(k0[...]), largest(k1[...]))
 
     low = lax.broadcasted_iota(jnp.int32, q_ref.shape, 1) < 64
     q = q_ref[...]
     factor = scale * math.log2(math.e)
-    small = largest(q.astype(F32)) * ksize[0] * (factor * factor) < SAFE * SAFE
+    small = jnp.max(largest(q) * ksize[...]) * (factor * factor) < SAFE * SAFE
 
     def run(shifted):
         outs, sums = [], []
@@ -91,9 +123,8 @@
     pl.when(jnp.logical_not(small))(lambda: run(True))
 
 
-def attend(qkv, kv_other, block):
-    rows = qkv.shape[0]
-    width = qkv.shape[1] // 3
+def attend(q, kv, kv_other, block):
+    rows, width = q.shape
     pairs = width // 128
     tile = pl.BlockSpec((block, 128), lambda h, i: (i, h))
     return pl.pallas_call(
@@ -101,9 +132,9 @@
         grid=(pairs, rows // block),
         in_specs=[
             tile,
+            pl.BlockSpec((rows, 128), lambda h, i: (0, h)),
+            pl.BlockSpec((rows, 128), lambda h, i: (0, h)),
             pl.BlockSpec((rows, 128), lambda h, i: (0, pairs + h)),
-            pl.BlockSpec((rows, 128), lambda h, i: (0, h)),
-            pl.BlockSpec((rows, 128), lambda h, i: (0, 2 * pairs + h)),
             pl.BlockSpec((rows, 128), lambda h, i: (0, pairs + h)),
         ],
         out_specs=[tile, pl.BlockSpec((2, block, 2 * rows), lambda h, i: (h, i, 0)), tile],
@@ -112,11 +143,11 @@
             jax.ShapeDtypeStruct((HEADS, rows, 2 * rows), BF),
             jax.ShapeDtypeStruct((rows, width), F32),
         ],
-        scratch_shapes=[pltpu.VMEM((2 * rows, 256), BF), pltpu.SMEM((1,), F32)],
+        scratch_shapes=[pltpu.VMEM((2 * rows, 256), BF), pltpu.VMEM((1, 128), F32)],
         compiler_params=pltpu.CompilerParams(vmem_limit_bytes=VMEM_BYTES),
         cost_estimate=estimate(rows * width, rows * width),
         name="attend",
-    )(qkv, qkv, kv_other, qkv, kv_other)
+    )(q, kv, kv_other, kv, kv_other)
 
 
 def attend_back_kernel(
@@ -175,9 +206,8 @@
         far_ref[1] = vacc[:, half:].T.astype(BF)
 
 
-def attend_back(qkv, kv_other, mixed, grad, inv_sum, probs, block, first, count):
-    rows = qkv.shape[0]
-    width = qkv.shape[1] // 3
+def attend_back(q, kv, kv_other, mixed, grad, inv_sum, probs, block, first, count):
+    rows, width = q.shape
     pairs = width // 128
     steps = rows // block
     tile = pl.BlockSpec((block, 128), lambda h, i: (i, first + h))
@@ -187,9 +217,9 @@
         grid=(count, steps),
         in_specs=[
             tile,
+            pl.BlockSpec((rows, 128), lambda h, i: (0, first + h)),
+            pl.BlockSpec((rows, 128), lambda h, i: (0, first + h)),
             pl.BlockSpec((rows, 128), lambda h, i: (0, pairs + first + h)),
-            pl.BlockSpec((rows, 128), lambda h, i: (0, first + h)),
-            pl.BlockSpec((rows, 128), lambda h, i: (0, 2 * pairs + first + h)),
             pl.BlockSpec((rows, 128), lambda h, i: (0, pairs + first + h)),
             tile,
             tile,
@@ -210,7 +240,7 @@
         compiler_params=pltpu.CompilerParams(vmem_limit_bytes=VMEM_BYTES),
         cost_estimate=estimate(rows * width, rows * width),
         name="attend_back",
-    )(qkv, qkv, kv_other, qkv, kv_other, mixed, grad, inv_sum, probs)
+    )(q, kv, kv_other, kv, kv_other, mixed, grad, inv_sum, probs)
 
 
 def grad_qkv_kernel(core, normed, *refs, count, with_out):
@@ -243,9 +273,8 @@
         grad_ref[:, cols + width :] = jnp.concatenate([high, value - high, rest], axis=0).T.astype(BF)
 
 
-def grad_qkv_half(core, normed, sides, count, more):
+def grad_qkv_part(core, normed, sides, count, more, half):
     rows, width = normed.shape
-    half = width // 2
     cols = sum(side.shape[-1] for side in sides[:count]) * 3 if count else sides[0].shape[1]
     out_cols = cols + (more[1].shape[1] + SMALL if more else 0)
     full = lambda a: pl.BlockSpec(a.shape, lambda i, core: (0,) * a.ndim)
@@ -273,10 +302,15 @@
 
 
 def grad_qkv(normed, dqs, owns, fars, more=()):
+    return grad_qkv_part(jnp.int32(0), normed, (*dqs, *owns, *fars), len(dqs), more, normed.shape[1])
+
+
+def grad_qkv_halves(normed, dqs, owns, fars):
     here = lax.axis_index("ctx")
-    give, d_qkv = grad_qkv_half(1 - here, normed, (*dqs, *owns, *fars), len(dqs), more)
+    half = normed.shape[1] // 2
+    give, d_qkv = grad_qkv_part(1 - here, normed, (*dqs, *owns, *fars), len(dqs), (), half)
     other = swap(give)
-    (keep,) = grad_qkv_half(here, normed, (d_qkv,), 0, more)
+    (keep,) = grad_qkv_part(here, normed, (d_qkv,), 0, (), half)
     return [keep, other], d_qkv
 
 
@@ -607,17 +641,19 @@
     return total, firsts, seconds
 
 
-def unseat_kernel(t1, t2, base, back, out_ref, *, split):
-    total, _, _ = rows_back(t1[...], t2[...], [back], False, split)
-    out_ref[...] = (base[...] + total).astype(BF)
-
-
-def unseat(t1, t2, base, back, split, block=256):
+def unseat_kernel(t1, t2, base, back, out_ref, *, split, sub):
+    for r in range(0, t1.shape[0], sub):
+        at = slice(r, r + sub)
+        total, _, _ = rows_back(t1[at], t2[at], [back], False, split)
+        out_ref[at] = (base[at] + total).astype(BF)
+
+
+def unseat(t1, t2, base, back, split, block=512, sub=512):
     tokens, width = base.shape
     col = pl.BlockSpec((block, 1), lambda i: (i, 0))
     rows = pl.BlockSpec((block, width), lambda i: (i, 0))
     return pl.pallas_call(
-        functools.partial(unseat_kernel, split=split),
+        functools.partial(unseat_kernel, split=split, sub=sub),
         grid=(tokens // block,),
         in_specs=[col, col, rows, pl.BlockSpec(back.shape, lambda i: (0, 0, 0))],
         out_specs=rows,
@@ -625,42 +661,40 @@
         compiler_params=pltpu.CompilerParams(vmem_limit_bytes=VMEM_BYTES),
         cost_estimate=estimate(tokens * width, tokens * width),
         name="unseat",
-    )(t1[:, None], t2[:, None], base, back)
+    )(t1, t2, base, back)
 
 
 def route_back_kernel(
-    t1, t2, ids, probs, dy, middle, gain, w_router, w_out, *refs,
+    t1, t2, ids, probs, dy, middle, gain, w_router, w_out, *refs, sub
 ):
     dmiddle_ref, dbranch_ref, dmixed_ref, small_ref = refs[-4:]
-    total, dg1, dg2 = rows_back(t1[...], t2[...], refs[:-4], True)
-    p = probs[...]
-    experts = p.shape[1]
-    lane = lax.broadcasted_iota(jnp.int32, p.shape, 1)
-    d_gates = jnp.where(lane == ids[:, 0:1], dg1, 0.0) + jnp.where(lane == ids[:, 1:2], dg2, 0.0)
-    d_logits = p * (d_gates - jnp.sum(p * d_gates, axis=1, keepdims=True))
-    d_routed = total
-    for piece in three_parts(d_logits):
-        d_routed = d_routed + mm(piece, w_router[...], NT)
-    v = middle[...]
-    centred = v - jnp.mean(v, axis=1, keepdims=True)
-    inv = lax.rsqrt(jnp.mean(centred * centred, axis=1, keepdims=True) + NORM_EPS)
-    unit = centred * inv
-    routed = (unit * gain[...]).astype(BF)
-    scaled = d_routed * gain[...]
-    d_norm = inv * (
-        scaled
-        - jnp.mean(scaled, axis=1, keepdims=True)
-        - unit * jnp.mean(scaled * unit, axis=1, keepdims=True)
-    )
-    d_middle = dy[...].astype(F32) + d_norm
-    d_branch = d_middle.astype(BF)
-    dmiddle_ref[...] = d_middle
-    dbranch_ref[...] = d_branch
-    dmixed_ref[...] = mm(d_branch, w_out[...], NT).astype(BF)
-    to_router = 0.0
-    for piece in three_parts(d_logits.T):
-        to_router = to_router + mm(piece, routed)
-    to_gain = jnp.sum(d_routed * unit, axis=0, keepdims=True)
+    experts = probs.shape[1]
+    to_router, to_gain = 0.0, 0.0
+    for r in range(0, t1.shape[0], sub):
+        at = slice(r, r + sub)
+        d_routed, dg1, dg2 = rows_back(t1[at], t2[at], refs[:-4], True)
+        p = probs[at]
+        lane = lax.broadcasted_iota(jnp.int32, p.shape, 1)
+        d_gates = jnp.where(lane == ids[at, 0:1], dg1, 0.0) + jnp.where(lane == ids[at, 1:2], dg2, 0.0)
+        d_logits = p * (d_gates - jnp.sum(p * d_gates, axis=1, keepdims=True))
+        for piece in three_parts(d_logits):
+            d_routed = d_routed + mm(piece, w_router[...], NT)
+        normed, unit, inv = norm_forward(middle[at], gain[...])
+        routed = normed.astype(BF)
+        scaled = d_routed * gain[...]
+        d_norm = inv * (
+            scaled
+            - jnp.mean(scaled, axis=1, keepdims=True)
+            - unit * jnp.mean(scaled * unit, axis=1, keepdims=True)
+        )
+        d_middle = dy[at].astype(F32) + d_norm
+        d_branch = d_middle.astype(BF)
+        dmiddle_ref[at] = d_middle
+        dbranch_ref[at] = d_branch
+        dmixed_ref[at] = mm(d_branch, w_out[...], NT).astype(BF)
+        for piece in three_parts(d_logits.T):
+            to_router = to_router + mm(piece, routed)
+        to_gain = to_gain + jnp.sum(d_routed * unit, axis=0, keepdims=True)
 
     @pl.when(pl.program_id(0) == 0)
     def _():
@@ -670,14 +704,14 @@
     small_ref[experts : experts + 1, :] += to_gain
 
 
-def route_back(t1, t2, ids, probs, dy, middle, gain, w_router, w_out, parts, block=256):
+def route_back(t1, t2, ids, probs, dy, middle, gain, w_router, w_out, parts, block=512, sub=256):
     tokens, width = dy.shape
     experts = probs.shape[1]
     line = lambda cols: pl.BlockSpec((block, cols), lambda i: (i, 0))
     full = lambda a: pl.BlockSpec(a.shape, lambda i: (0,) * a.ndim)
     gain = gain[None]
     return pl.pallas_call(
-        route_back_kernel,
+        functools.partial(route_back_kernel, sub=sub),
         grid=(tokens // block,),
         in_specs=[
             line(1), line(1), line(2), line(experts), line(width), line(width),
@@ -697,7 +731,7 @@
         compiler_params=pltpu.CompilerParams(vmem_limit_bytes=VMEM_BYTES),
         cost_estimate=estimate(tokens * width, tokens * width),
         name="route_back",
-    )(t1[:, None], t2[:, None], ids, probs, dy, middle, gain, w_router, w_out, *parts)
+    )(t1, t2, ids, probs, dy, middle, gain, w_router, w_out, *parts)
 
 
 def swap(value):
@@ -869,14 +903,12 @@
     dy_slots = seat_rows(t1, t2, dy_b, (), every, parts, peers, cap)
     dy_got = exchange(dy_slots, axes)
 
-    tokens_f = after(tokens, dy_slots).reshape(rows, width).astype(F32)
-    normed_a, unit_a, inv_a = norm_forward(tokens_f, gain_attn)
-    normed_ab = normed_a.astype(BF)
-    qkv_b = mm(normed_ab, w_qkv).astype(BF)
-    kv_other = swap(qkv_b[:, width:])
-    mixed_b, probs, inv_sum = attend(qkv_b, kv_other, rows)
-
-    middle = tokens_f + mm(mixed_b, w_out)
+    tokens_b = after(tokens, dy_slots).reshape(rows, width)
+    normed_ab, q_b, kv_b = project(tokens_b, gain_attn, w_qkv)
+    kv_other = swap(kv_b)
+    mixed_b, probs, inv_sum = attend(q_b, kv_b, kv_other, rows)
+
+    middle = tokens_b.astype(F32) + mm(mixed_b, w_out)
     normed_m, _, _ = norm_forward(middle, gain_moe)
     routed_b = normed_m.astype(BF)
     logits = mm(routed_b, w_router) + router_noise.reshape(rows, expert_count)
@@ -893,11 +925,12 @@
     sent[0], dy_got = lax.optimization_barrier((sent[0], dy_got))
     x_got = [exchange(sent[0], axes)]
     outs, dx_back, dgates, kept = None, [], [], []
+    t1c, t2c = t1[:, None], t2[:, None]
     for part in every:
         last = part == parts - 1
         x = x_got[part]
         if not last:
-            x, following = lax.optimization_barrier((x, sent[part + 1]))
+            x, following, t1c, t2c = lax.optimization_barrier((x, sent[part + 1], t1c, t2c))
             x_got.append(exchange(following, axes))
         outs, dx, act, dhid, dp, *dg = run_expert(
             which[part].astype(jnp.int32)[None], part, parts, x, x_got[0], dy_got, outs, dgates, w_up, w_down
@@ -938,31 +971,32 @@
         pieces = [block if n == 0 else shift(block, "dp", n) for n, block in enumerate(blocks)]
 
     d_middle, d_branch_b, d_mixed_b, small = route_back(
-        t1, t2, expert_ids.reshape(rows, 2), gate_probs, dy_b, middle, gain_moe, w_router, w_out, dx_back
+        t1c, t2c, expert_ids.reshape(rows, 2), gate_probs, dy_b, middle, gain_moe, w_router, w_out, dx_back
     )
 
     pairs = width // 128
     calls = [(first, pairs // 3) for first in range(0, pairs, pairs // 3)]
 
     def call(n, grad):
-        return attend_back(qkv_b, kv_other, mixed_b, grad, inv_sum, probs, rows, *calls[n])
+        return attend_back(q_b, kv_b, kv_other, mixed_b, grad, inv_sum, probs, rows, *calls[n])
 
     dq0, own0, far0 = call(0, d_mixed_b)
     dq1, own1, far1 = call(1, after(d_mixed_b, dq0))
     fars = [swap(far0), swap(far1)]
-    result = unseat(t1, t2, after(middle, dq1), returned, parts)
-    fars, pieces, result = lax.optimization_barrier((fars, pieces, result))
+    result = unseat(t1c, t2c, after(middle, dq1), returned, parts)
+    fars, result = lax.optimization_barrier((fars, result))
     grad_a, d_qkv_a = grad_qkv(
         normed_ab, [dq0, dq1], [own0, own1], fars, (mixed_b, d_branch_b, small)
     )
-    sum_a = add_up(grad_a)
+    grad_a, pieces = lax.optimization_barrier((grad_a, pieces))
+    sum_a = add_up(scatter_begin(grad_a, "ctx"))
     d_mixed_b, sum_a = lax.optimization_barrier((d_mixed_b, sum_a))
     got_a = scatter_begin(sum_a, "dp")
     dq2, own2, far2 = call(2, d_mixed_b)
     got_a, dq2, own2, far2 = lax.optimization_barrier((got_a, dq2, own2, far2))
     got_a = scatter_begin(add_up(got_a), "expert")
     far2 = swap(far2)
-    got_b, d_qkv_b = grad_qkv(normed_ab, [dq2], [own2], [far2])
+    got_b, d_qkv_b = grad_qkv_halves(normed_ab, [dq2], [own2], [far2])
     got_a, got_b[0] = lax.optimization_barrier((got_a, got_b[0]))
     got_a = gather_back(add_up(got_a), "expert")
     got_b = scatter_begin(add_up(got_b), "dp")
@@ -983,8 +1017,8 @@
         start, wide = 128 * first, d_qkv.shape[1] // 3
         columns = [w_qkv[:, m * width + start : m * width + start + wide] for m in range(3)]
         d_normed_a = d_normed_a + mm(d_qkv, jnp.concatenate(columns, axis=1), NT)
-    d_tokens_norm, _ = norm_backward(d_normed_a, unit_a, inv_a, gain_attn)
-    d_tokens = d_middle + d_tokens_norm
+    _, unit_a, inv_a = norm_forward(tokens_b.astype(F32), gain_attn)
+    d_tokens = d_middle + norm_backward(d_normed_a, unit_a, inv_a, gain_attn)[0]
     d_tokens, got_b = lax.optimization_barrier((d_tokens, got_b))
 
     all_b = jnp.stack(got_b)

time: 523 us -> 511 us (0.977)
  waiting for transfers between devices: 78.3 us -> 69.9 us
  local copies, waits for them, and re-layouts: 18.7 us -> 24.3 us
    ppermute x27 -> x28, waiting for transfers between devices: 29.8 us -> 23.8 us  [shift(): return lax.ppermute(value, axis, [(i, (i + by) % n) for i in range(n)])]
    dot_general x5 -> x4, matrix products: 13 us -> 9.1 us  [mm(): return lax.dot_general(left, right, dims, preferred_element_type=F32)]
    unnamed x76 -> x70, local copies, waits for them, and re-layouts: 12.7 us -> 15.3 us
    ppermute x27 -> x28, starting transfers between devices: 40.8 us -> 40.5 us  [shift(): return lax.ppermute(value, axis, [(i, (i + by) % n) for i in range(n)])]
  transfers between devices with their start and end apart: 42 -> 42, of which waited for: 16 -> 16; matrix products, arithmetic and copies ran while one was open for 8% -> 7% of each run, Pallas kernels for 50% -> 52%
where the time goes in v3:
time: 511 us; the launch traced here: 504 us
  Pallas kernels  279 us (55%)
  starting transfers between devices  89.3 us (17%)
  waiting for transfers between devices  69.9 us (14%)
  other arithmetic  28.4 us (6%)
  local copies, waits for them, and re-layouts  24.3 us (5%)
  matrix products  10.9 us (2%)
    pallas_call x3, Pallas kernels, attend_back(): pl.pallas_call(functools.partial(attend_back_kernel, scale=1.0 / math.sqr...  62.9 us
    pallas_call x2, Pallas kernels, run_expert(): pl.pallas_call(functools.partial(expert_kernel, part=part, parts=parts, s...  58.6 us
    all_to_all x6, starting transfers between devices, exchange(): return lax.all_to_all(value, axes, 0, 0, tiled=True)  48 us
    ppermute x28, starting transfers between devices, shift(): return lax.ppermute(value, axis, [(i, (i + by) % n) for i in range(n)])  40.5 us
    all_to_all x6, waiting for transfers between devices, exchange(): return lax.all_to_all(value, axes, 0, 0, tiled=True)  39.9 us
    pallas_call x1, Pallas kernels, attend(): pl.pallas_call(functools.partial(attend_kernel, scale=1.0 / math.sqrt(wid...  37.6 us
    pallas_call x2, Pallas kernels, weight_grads(): pl.pallas_call(functools.partial(weights_kernel, count=len(acts), pieces=...  36.2 us
    ppermute x28, waiting for transfers between devices, shift(): return lax.ppermute(value, axis, [(i, (i + by) % n) for i in range(n)])  23.8 us
  transfers between devices with their start and end apart: 42, of which 16 were waited for; matrix products, arithmetic and copies ran while one was open for 7% of the time, Pallas kernels for 52%

profile of v3, /device:TPU:0, one launch (start us, length us, event | category | flops | bytes accessed | tf_op | source)
XLA Modules:
  0.0 503.7 jit_solution(15143986446298443561)
XLA Ops:
  6.9 6.5 %seat_rows.3 = bf16[16,128,768]{2,1,0:T(8,128)(2,1)} custom-call(s32[1,1024]{1,0:T(1,128)} %compare_select_fusion.1.t1, s32[1,1024]{1,0:T(1,128)} %compare_select_fusion.t2, bf16[1024,768]{1,0:T(8,128)(2,1)} %bitcast.103), custom_call_target="tpu_custom_call" | custom-call | flops 805306368 | bytes 786432 | tf_op jit(solution)/shard_map/seat_rows/pallas_call | solution.py:607
  13.4 8.5 %all-to-all-start = ((bf16[16,128,768]{2,1,0:T(8,128)(2,1)}), bf16[16,128,768]{2,1,0:T(8,128)(2,1)}, u32[]{:S(2)}, u32[]{:S(2)}) async-start(bf16[16,128,768]{2,1,0:T(8,128)(2,1)} %seat_rows.3), calls=%async_computation | async-start | bytes 6291456 | tf_op jit(solution)/shard_map/all_to_all | solution.py:743
  22.5 8.3 %project.1 = (bf16[1024,768]{1,0:T(8,128)(2,1)}, bf16[1024,768]{1,0:T(8,128)(2,1)}, bf16[1024,1536]{1,0:T(8,128)(2,1)}) custom-call(bf16[1024,768]{1,0:T(8,128)(2,1)} %bitcast.98, f32[1,768]{1,0:T(1,128)} %broadcast_in_dim.25.gain, bf16[768,2304]{1,0:T(8,128)(2,1)} %w_ref.3), custom_call_target="tpu_custom_call" | custom-call | flops 905969664 | bytes 3932160 | tf_op jit(solution)/shard_map/project/pallas_call | solution.py:61
  31.8 4.9 collective-permute-done.k1.v1
  38.4 37.6 %attend.1 = (bf16[1024,768]{1,0:T(8,128)(2,1)}, bf16[12,1024,2048]{2,1,0:T(8,128)(2,1)}, f32[1024,768]{1,0:T(8,128)}) custom-call(bf16[1024,768]{1,0:T(8,128)(2,1)} %get-tuple-element.132.q_ref, bf16[1024,1536]{1,0:T(8,128)(2,1)} %get-tuple-element.133.k0.v0, bf16[1024,1536]{1,0:T(8,128)(2,1)} %copy-done, bf16[1024,1536]{1,0:T(8,128)(2,1)} %get-tuple-element.133.k0.v0, ...), custom_call_target="tpu_custom_call" | custom-call | flops 196608 | bytes 196608 | tf_op jit(solution)/shard_map/attend/pallas_call | solution.py:130
  76.0 3.8 fusion.69
  85.7 6.7 %seat_rows.4 = bf16[16,72,768]{2,1,0:T(8,128)(2,1)} custom-call(s32[1,1024]{1,0:T(1,128)} %compare_select_fusion.1.t1, s32[1,1024]{1,0:T(1,128)} %compare_select_fusion.t2, f32[1,1024]{1,0:T(1,128)} %bitcast.136, f32[1,1024]{1,0:T(1,128)} %bitcast.135, bf16[1024,768]{1,0:T(8,128)(2,1)} %copy-done.4), custom_call_target="tpu_custom_call" | custom-call | flops 452984832 | bytes 786432 | tf_op jit(solution)/shard_map/seat_rows/pallas_call | solution.py:607
  92.4 7.0 %all-to-all-start.1 = ((bf16[16,72,768]{2,1,0:T(8,128)(2,1)}), bf16[16,72,768]{2,1,0:T(8,128)(2,1)S(1)}, u32[]{:S(2)}, u32[]{:S(2)}) async-start(bf16[16,72,768]{2,1,0:T(8,128)(2,1)} %seat_rows.4), calls=%async_computation.1 | async-start | bytes 3538944 | tf_op jit(solution)/shard_map/all_to_all | solution.py:743
  101.8 4.4 seat_rows.5
  106.2 30.8 %all-to-all-done.1.x_in.gate_in.refs_4_ = bf16[16,72,768]{2,1,0:T(8,128)(2,1)S(1)} async-done(((bf16[16,72,768]{2,1,0:T(8,128)(2,1)}), bf16[16,72,768]{2,1,0:T(8,128)(2,1)S(1)}, u32[]{:S(2)}, u32[]{:S(2)}) %all-to-all-start.1) | async-done | bytes 1769504 | tf_op jit(solution)/shard_map/all_to_all | solution.py:743
  137.0 9.0 %all-to-all-start.2 = ((bf16[16,64,768]{2,1,0:T(8,128)(2,1)}), bf16[16,64,768]{2,1,0:T(8,128)(2,1)S(1)}, u32[]{:S(2)}, u32[]{:S(2)}) async-start(bf16[16,64,768]{2,1,0:T(8,128)(2,1)} %seat_rows.5), calls=%async_computation.2 | async-start | bytes 3145728 | tf_op jit(solution)/shard_map/all_to_all | solution.py:743
  146.0 29.3 %expert.2 = (bf16[16,128,768]{2,1,0:T(8,128)(2,1)}, bf16[16,64,768]{2,1,0:T(8,128)(2,1)}, bf16[1024,3072]{1,0:T(8,128)(2,1)}, bf16[1024,3072]{1,0:T(8,128)(2,1)}...) custom-call(s32[1]{0:T(128)} %bitcast.11.which.at, bf16[16,72,768]{2,1,0:T(8,128)(2,1)} %copy-done.2, ...), custom_call_target="tpu_custom_call" | custom-call | flops 4831838208 | bytes 2359296 | tf_op jit(solution)/shard_map/expert/pallas_call | solution.py:429
  175.3 4.2 all-to-all-done.2.x_in.refs_5_
  179.5 7.6 %all-to-all-start.3 = ((bf16[16,64,768]{2,1,0:T(8,128)(2,1)}), bf16[16,64,768]{2,1,0:T(8,128)(2,1)S(1)}, u32[]{:S(2)}, u32[]{:S(2)}) async-start(bf16[16,64,768]{2,1,0:T(8,128)(2,1)} %get-tuple-element.147), calls=%async_computation.3 | async-start | bytes 3145728 | tf_op jit(solution)/shard_map/all_to_all | solution.py:743
  187.1 29.3 %expert.3 = (bf16[16,128,768]{2,1,0:T(8,128)(2,1)}, bf16[16,72,768]{2,1,0:T(8,128)(2,1)}, bf16[1024,3072]{1,0:T(8,128)(2,1)}, bf16[1024,3072]{1,0:T(8,128)(2,1)}, bf16[1024,768]{1,0:T(8,128)(2,1)}) custom-call(s32[1]{0:T(128)} %bitcast.11.which.at, bf16[16,64,768]{2,1,0:T(8,128)(2,1)} %copy-done.8, ...), custom_call_target="tpu_custom_call", output_to_operand_aliasing={{0}: (4, {})} | custom-call | flops 4831838208 | bytes 2359296 | tf_op jit(solution)/shard_map/expert/pallas_call | solution.py:429
  216.5 4.2 all-to-all-done.3.refs_0_
  221.9 7.8 %all-to-all-start.4 = ((bf16[16,72,768]{2,1,0:T(8,128)(2,1)}), bf16[16,72,768]{2,1,0:T(8,128)(2,1)S(1)}, u32[]{:S(2)}, u32[]{:S(2)}) async-start(bf16[16,72,768]{2,1,0:T(8,128)(2,1)} %get-tuple-element.150), calls=%async_computation.4 | async-start | bytes 3538944 | tf_op jit(solution)/shard_map/all_to_all | solution.py:743
  229.7 19.5 %weight_grads.2 = (bf16[4,2,768,384]{3,2,1,0:T(8,128)(2,1)}, bf16[768,2048]{1,0:T(8,128)(2,1)}, bf16[768,2048]{1,0:T(8,128)(2,1)}) custom-call(s32[1]{0:T(128)} %bitcast.12.at.core, bf16[1024,3072]{1,0:T(8,128)(2,1)} %get-tuple-element.151.refs_0_, bf16[1024,3072]{1,0:T(8,128)(2,1)} %get-tuple-element.152.refs_1_, ...), custom_call_target="tpu_custom_call" | custom-call | flops 393216 | bytes 393216 | tf_op jit(solution)/shard_map/weight_grads/pallas_call | solution.py:509
  249.2 16.7 %weight_grads.3 = bf16[4,2,768,384]{3,2,1,0:T(8,128)(2,1)} custom-call(s32[1]{0:T(128)} %bitcast.13.at.core, bf16[1024,3072]{1,0:T(8,128)(2,1)} %get-tuple-element.151.refs_0_, bf16[1024,3072]{1,0:T(8,128)(2,1)} %get-tuple-element.152.refs_1_, bf16[1024,3072]{1,0:T(8,128)(2,1)} %get-tuple-element.153.refs_2_, bf16[1024,3072]{1,0:T(8,128)(2,1)} %get-tuple-element.154.refs_3_, ...), custom_call_target="tpu_custom_call" | custom-call | flops 393216 | bytes 393216 | tf_op jit(solution)/shard_map/weight_grads/pallas_call | solution.py:509
  267.8 8.2 %all-to-all-start.5 = ((bf16[16,128,768]{2,1,0:T(8,128)(2,1)}), bf16[16,128,768]{2,1,0:T(8,128)(2,1)S(1)}, u32[]{:S(2)}, u32[]{:S(2)}) async-start(bf16[16,128,768]{2,1,0:T(8,128)(2,1)} %get-tuple-element.177), calls=%async_computation.5 | async-start | bytes 6291456 | tf_op jit(solution)/shard_map/all_to_all | solution.py:743
  276.0 6.7 %fusion.27 = (bf16[2,768,384]{2,1,0:T(8,128)(2,1)}, bf16[2,768,384]{2,1,0:T(8,128)(2,1)}, bf16[2,768,384]{2,1,0:T(8,128)(2,1)}, bf16[2,768,384]{2,1,0:T(8,128)(2,1)}) fusion(bf16[4,2,768,384]{3,2,1,0:T(8,128)(2,1)} %collective-permute-done.1, s32[]{:T(128)S(6)} %select_n.196, bf16[4,2,768,384]{3,2,1,0:T(8,128)(2,1)} %weight_grads.3, s32[]{:T(128)S(6)} %select_n.195, ...), kind=kLoop, calls=%fused_computation.39 | loop fusion | flops 9437184 | bytes 14155792 | tf_op jit(solution)/shard_map/convert_element_type | solution.py:763
  289.0 16.5 %route_back.1 = (f32[1024,768]{1,0:T(8,128)}, bf16[1024,768]{1,0:T(8,128)(2,1)}, bf16[1024,768]{1,0:T(8,128)(2,1)}, f32[24,768]{1,0:T(8,128)}) custom-call(s32[1024,1]{1,0:T(8,128)} %get-tuple-element.136.t1, s32[1024,1]{1,0:T(8,128)} %get-tuple-element.137.t2, s32[1024,2]{1,0:T(8,128)} %bitcast.100, f32[1024,16]{1,0:T(8,128)} %get-tuple-element.288.probs, ...), custom_call_target="tpu_custom_call" | custom-call | flops 196608 | bytes 196608 | tf_op jit(solution)/shard_map/route_back/pallas_call | solution.py:713
  305.4 20.9 %attend_back.3 = (bf16[1024,256]{1,0:T(8,128)(2,1)}, f32[2,1024,256]{2,1,0:T(8,128)}, bf16[2,1024,256]{2,1,0:T(8,128)(2,1)}) custom-call(bf16[1024,768]{1,0:T(8,128)(2,1)} %get-tuple-element.132.q_ref, bf16[1024,1536]{1,0:T(8,128)(2,1)} %get-tuple-element.133.k0.v0, bf16[1024,1536]{1,0:T(8,128)(2,1)} %copy-done, ...), custom_call_target="tpu_custom_call" | custom-call | flops 196608 | bytes 196608 | tf_op jit(solution)/shard_map/attend_back/pallas_call | solution.py:215
  326.3 21.1 %attend_back.4 = (bf16[1024,256]{1,0:T(8,128)(2,1)}, f32[2,1024,256]{2,1,0:T(8,128)}, bf16[2,1024,256]{2,1,0:T(8,128)(2,1)}) custom-call(bf16[1024,768]{1,0:T(8,128)(2,1)} %get-tuple-element.132.q_ref, bf16[1024,1536]{1,0:T(8,128)(2,1)} %get-tuple-element.133.k0.v0, bf16[1024,1536]{1,0:T(8,128)(2,1)} %copy-done, ...), custom_call_target="tpu_custom_call" | custom-call | flops 196608 | bytes 196608 | tf_op jit(solution)/shard_map/attend_back/pallas_call | solution.py:215
  349.7 7.9 %unseat.1 = bf16[1024,768]{1,0:T(8,128)(2,1)} custom-call(s32[1024,1]{1,0:T(8,128)} %get-tuple-element.136.t1, s32[1024,1]{1,0:T(8,128)} %get-tuple-element.137.t2, f32[1024,768]{1,0:T(8,128)} %copy-done.1, bf16[16,128,768]{2,1,0:T(8,128)(2,1)} %copy-done.9), custom_call_target="tpu_custom_call" | custom-call | flops 196608 | bytes 196608 | tf_op jit(solution)/shard_map/unseat/pallas_call | solution.py:655
  357.6 10.2 %grad_qkv.3 = (bf16[768,2432]{1,0:T(8,128)(2,1)}, bf16[1024,1536]{1,0:T(8,128)(2,1)}) custom-call(s32[1]{0:T(128)} %constant.165.clone.1.core, bf16[1024,768]{1,0:T(8,128)(2,1)} %get-tuple-element.180.normed, bf16[1024,256]{1,0:T(8,128)(2,1)} %get-tuple-element.172.refs_0_, bf16[1024,256]{1,0:T(8,128)(2,1)} %get-tuple-element.175.refs_1_, ...), custom_call_target="tpu_custom_call" | custom-call | flops 196608 | bytes 196608 | tf_op jit(solution)/shard_map/grad_qkv/pallas_call | solution.py:287
  372.2 4.0 collective-permute-done.7
  386.6 20.9 %attend_back.5 = (bf16[1024,256]{1,0:T(8,128)(2,1)}, f32[2,1024,256]{2,1,0:T(8,128)}, bf16[2,1024,256]{2,1,0:T(8,128)(2,1)}) custom-call(bf16[1024,768]{1,0:T(8,128)(2,1)} %get-tuple-element.132.q_ref, bf16[1024,1536]{1,0:T(8,128)(2,1)} %get-tuple-element.133.k0.v0, bf16[1024,1536]{1,0:T(8,128)(2,1)} %copy-done, ...), custom_call_target="tpu_custom_call" | custom-call | flops 196608 | bytes 196608 | tf_op jit(solution)/shard_map/attend_back/pallas_call | solution.py:215
  415.5 4.1 grad_qkv.4
  431.1 4.6 collective-permute-done.16
  453.4 6.5 %spread.1 = (f32[4,768,384]{2,1,0:T(8,128)}, f32[4,384,768]{2,1,0:T(8,128)}) custom-call(s32[1]{0:T(128)} %bitcast.11.which.at, bf16[2,768,384]{2,1,0:T(8,128)(2,1)} %get-tuple-element.227.refs_0_, bf16[2,768,384]{2,1,0:T(8,128)(2,1)} %collective-permute-done.4.refs_1_, bf16[2,768,384]{2,1,0:T(8,128)(2,1)} %collective-permute-done.5.refs_2_, ...), custom_call_target="tpu_custom_call" | custom-call | flops 73728 | bytes 3538944 | tf_op jit(solution)/shard_map/spread/pallas_call | solution.py:837
  488.9 9.8 %assemble.1 = (f32[768,2304]{1,0:T(8,128)}, f32[768,768]{1,0:T(8,128)}, f32[768,128]{1,0:T(8,128)}, f32[768,1]{1,0:T(8,128)}) custom-call(s32[3]{0:T(128)} %pad_add_fusion.at, bf16[768,2304]{1,0:T(8,128)(2,1)} %w_ref.3, bf16[4,4,24,2432]{3,2,1,0:T(8,128)(2,1)} %copy-done.10, bf16[4,4,24,768]{3,2,1,0:T(8,128)(2,1)} %copy-done.14, ...), custom_call_target="tpu_custom_call" | custom-call | flops 442368 | bytes 5308416 | tf_op jit(solution)/shard_map/assemble/pallas_call | solution.py:806
  (197 shorter events, 114.8 us)
Async XLA Ops:
  13.4 79.0 %all-to-all-start = ((bf16[16,128,768]{2,1,0:T(8,128)(2,1)}), bf16[16,128,768]{2,1,0:T(8,128)(2,1)}, u32[]{:S(2)}, u32[]{:S(2)}) async-start(bf16[16,128,768]{2,1,0:T(8,128)(2,1)} %seat_rows.3), calls=%async_computation | async-start | bytes 6291456 | tf_op jit(solution)/shard_map/all_to_all | solution.py:743
  92.4 44.6 %all-to-all-start.1 = ((bf16[16,72,768]{2,1,0:T(8,128)(2,1)}), bf16[16,72,768]{2,1,0:T(8,128)(2,1)S(1)}, u32[]{:S(2)}, u32[]{:S(2)}) async-start(bf16[16,72,768]{2,1,0:T(8,128)(2,1)} %seat_rows.4), calls=%async_computation.1 | async-start | bytes 3538944 | tf_op jit(solution)/shard_map/all_to_all | solution.py:743
  137.0 42.5 %all-to-all-start.2 = ((bf16[16,64,768]{2,1,0:T(8,128)(2,1)}), bf16[16,64,768]{2,1,0:T(8,128)(2,1)S(1)}, u32[]{:S(2)}, u32[]{:S(2)}) async-start(bf16[16,64,768]{2,1,0:T(8,128)(2,1)} %seat_rows.5), calls=%async_computation.2 | async-start | bytes 3145728 | tf_op jit(solution)/shard_map/all_to_all | solution.py:743
  179.5 41.1 %all-to-all-start.3 = ((bf16[16,64,768]{2,1,0:T(8,128)(2,1)}), bf16[16,64,768]{2,1,0:T(8,128)(2,1)S(1)}, u32[]{:S(2)}, u32[]{:S(2)}) async-start(bf16[16,64,768]{2,1,0:T(8,128)(2,1)} %get-tuple-element.147), calls=%async_computation.3 | async-start | bytes 3145728 | tf_op jit(solution)/shard_map/all_to_all | solution.py:743
  221.9 44.7 %all-to-all-start.4 = ((bf16[16,72,768]{2,1,0:T(8,128)(2,1)}), bf16[16,72,768]{2,1,0:T(8,128)(2,1)S(1)}, u32[]{:S(2)}, u32[]{:S(2)}) async-start(bf16[16,72,768]{2,1,0:T(8,128)(2,1)} %get-tuple-element.150), calls=%async_computation.4 | async-start | bytes 3538944 | tf_op jit(solution)/shard_map/all_to_all | solution.py:743
  266.6 9.4 %collective-permute-start.1 = (bf16[4,2,768,384]{3,2,1,0:T(8,128)(2,1)}, bf16[4,2,768,384]{3,2,1,0:T(8,128)(2,1)}, u32[]{:S(2)}, u32[]{:S(2)}) collective-permute-start(bf16[4,2,768,384]{3,2,1,0:T(8,128)(2,1)} %get-tuple-element.165), channel_id=1, source_target_pairs={{0,4},{4,0},{1,5},{5,1},{2,6},{6,2},{3,7},{7,3},{8,12},{12,8},{9,1... | collective-permute-start | bytes 14155784 | tf_op jit(solution)/shard_map/ppermute | solution.py:739
  267.8 80.2 %all-to-all-start.5 = ((bf16[16,128,768]{2,1,0:T(8,128)(2,1)}), bf16[16,128,768]{2,1,0:T(8,128)(2,1)S(1)}, u32[]{:S(2)}, u32[]{:S(2)}) async-start(bf16[16,128,768]{2,1,0:T(8,128)(2,1)} %get-tuple-element.177), calls=%async_computation.5 | async-start | bytes 6291456 | tf_op jit(solution)/shard_map/all_to_all | solution.py:743
  282.7 85.0 %collective-permute-start.4 = (bf16[2,768,384]{2,1,0:T(8,128)(2,1)}, bf16[2,768,384]{2,1,0:T(8,128)(2,1)}, u32[]{:S(2)}, u32[]{:S(2)}) collective-permute-start(bf16[2,768,384]{2,1,0:T(8,128)(2,1)} %get-tuple-element.190), channel_id=1, source_target_pairs={{0,1},{1,2},{2,3},{3,0},{4,5},{5,6},{6,7},{7,4},{8,9},{9,10},{10,1... | collective-permute-start | bytes 3538952 | tf_op jit(solution)/shard_map/ppermute | solution.py:748
  284.6 83.2 %collective-permute-start.5 = (bf16[2,768,384]{2,1,0:T(8,128)(2,1)}, bf16[2,768,384]{2,1,0:T(8,128)(2,1)}, u32[]{:S(2)}, u32[]{:S(2)}) collective-permute-start(bf16[2,768,384]{2,1,0:T(8,128)(2,1)} %get-tuple-element.191), channel_id=1, source_target_pairs={{0,2},{1,3},{2,0},{3,1},{4,6},{5,7},{6,4},{7,5},{8,10},{9,11},{10,... | collective-permute-start | bytes 3538952 | tf_op jit(solution)/shard_map/ppermute | solution.py:748
  286.1 83.2 %collective-permute-start.6 = (bf16[2,768,384]{2,1,0:T(8,128)(2,1)}, bf16[2,768,384]{2,1,0:T(8,128)(2,1)}, u32[]{:S(2)}, u32[]{:S(2)}) collective-permute-start(bf16[2,768,384]{2,1,0:T(8,128)(2,1)} %get-tuple-element.192), channel_id=1, source_target_pairs={{0,3},{1,0},{2,1},{3,2},{4,7},{5,4},{6,5},{7,6},{8,11},{9,8},{10,9... | collective-permute-start | bytes 3538952 | tf_op jit(solution)/shard_map/ppermute | solution.py:748
  347.5 10.0 %collective-permute-start.3 = (bf16[2,1024,256]{2,1,0:T(8,128)(2,1)}, bf16[2,1024,256]{2,1,0:T(8,128)(2,1)}, u32[]{:S(2)}, u32[]{:S(2)}) collective-permute-start(bf16[2,1024,256]{2,1,0:T(8,128)(2,1)} %get-tuple-element.174), channel_id=1, source_target_pairs={{0,4},{4,0},{1,5},{5,1},{2,6},{6,2},{3,7},{7,3},{8,12},{12,8},{9,1... | collective-permute-start | bytes 3145736 | tf_op jit(solution)/shard_map/ppermute | solution.py:739
  347.5 10.1 %collective-permute-start.2 = (bf16[2,1024,256]{2,1,0:T(8,128)(2,1)}, bf16[2,1024,256]{2,1,0:T(8,128)(2,1)}, u32[]{:S(2)}, u32[]{:S(2)}) collective-permute-start(bf16[2,1024,256]{2,1,0:T(8,128)(2,1)} %get-tuple-element.171), channel_id=1, source_target_pairs={{0,4},{4,0},{1,5},{5,1},{2,6},{6,2},{3,7},{7,3},{8,12},{12,8},{9,1... | collective-permute-start | bytes 3145736 | tf_op jit(solution)/shard_map/ppermute | solution.py:739
  378.4 29.1 %collective-permute-start.10 = (bf16[96,2432]{1,0:T(8,128)(2,1)S(1)}, bf16[96,2432]{1,0:T(8,128)(2,1)S(1)}, u32[]{:S(2)}, u32[]{:S(2)}) collective-permute-start(bf16[96,2432]{1,0:T(8,128)(2,1)S(1)} %get-tuple-element.299), channel_id=1, source_target_pairs={{0,3},{1,0},{2,1},{3,2},{4,7},{5,4},{6,5},{7,6},{8,11},{9,8},{10,9... | collective-permute-start | bytes 1400840 | tf_op jit(solution)/shard_map/ppermute | solution.py:748
  381.0 26.4 %collective-permute-start.8 = (bf16[96,2432]{1,0:T(8,128)(2,1)S(1)}, bf16[96,2432]{1,0:T(8,128)(2,1)}, u32[]{:S(2)}, u32[]{:S(2)}) collective-permute-start(bf16[96,2432]{1,0:T(8,128)(2,1)S(1)} %get-tuple-element.301), channel_id=1, source_target_pairs={{0,1},{1,2},{2,3},{3,0},{4,5},{5,6},{6,7},{7,4},{8,9},{9,10},{10,1... | collective-permute-start | bytes 1400840 | tf_op jit(solution)/shard_map/ppermute | solution.py:748
  381.0 26.4 %collective-permute-start.9 = (bf16[96,2432]{1,0:T(8,128)(2,1)S(1)}, bf16[96,2432]{1,0:T(8,128)(2,1)}, u32[]{:S(2)}, u32[]{:S(2)}) collective-permute-start(bf16[96,2432]{1,0:T(8,128)(2,1)S(1)} %get-tuple-element.300), channel_id=1, source_target_pairs={{0,2},{1,3},{2,0},{3,1},{4,6},{5,7},{6,4},{7,5},{8,10},{9,11},{10,... | collective-permute-start | bytes 1400840 | tf_op jit(solution)/shard_map/ppermute | solution.py:748
  409.1 13.8 %collective-permute-start.12 = (bf16[24,2432]{1,0:T(8,128)(2,1)S(1)}, bf16[24,2432]{1,0:T(8,128)(2,1)S(1)}, u32[]{:S(2)}, u32[]{:S(2)}) collective-permute-start(bf16[24,2432]{1,0:T(8,128)(2,1)S(1)} %get-tuple-element.311), channel_id=1, source_target_pairs={{0,8},{8,16},{16,24},{24,0},{1,9},{9,17},{17,25},{25,1},{2,10},{10... | collective-permute-start | bytes 350216 | tf_op jit(solution)/shard_map/ppermute | solution.py:748
  411.7 11.3 %collective-permute-start.13 = (bf16[24,2432]{1,0:T(8,128)(2,1)S(1)}, bf16[24,2432]{1,0:T(8,128)(2,1)S(1)}, u32[]{:S(2)}, u32[]{:S(2)}) collective-permute-start(bf16[24,2432]{1,0:T(8,128)(2,1)S(1)} %get-tuple-element.310), channel_id=1, source_target_pairs={{0,16},{8,24},{16,0},{24,8},{1,17},{9,25},{17,1},{25,9},{2,18},{10... | collective-permute-start | bytes 350216 | tf_op jit(solution)/shard_map/ppermute | solution.py:748
  411.7 11.3 %collective-permute-start.14 = (bf16[24,2432]{1,0:T(8,128)(2,1)S(1)}, bf16[24,2432]{1,0:T(8,128)(2,1)S(1)}, u32[]{:S(2)}, u32[]{:S(2)}) collective-permute-start(bf16[24,2432]{1,0:T(8,128)(2,1)S(1)} %get-tuple-element.309), channel_id=1, source_target_pairs={{0,24},{8,0},{16,8},{24,16},{1,25},{9,1},{17,9},{25,17},{2,26},{10... | collective-permute-start | bytes 350216 | tf_op jit(solution)/shard_map/ppermute | solution.py:748
  423.1 8.0 %collective-permute-start.15 = (bf16[24,2432]{1,0:T(8,128)(2,1)S(1)}, bf16[24,2432]{1,0:T(8,128)(2,1)S(1)}, u32[]{:S(2)}, u32[]{:S(2)}) collective-permute-start(bf16[24,2432]{1,0:T(8,128)(2,1)S(1)} %add_convert_fusion.7), channel_id=1, source_target_pairs={{0,8},{8,16},{16,24},{24,0},{1,9},{9,17},{17,25},{25,1},{2,10},{10... | collective-permute-start | bytes 350216 | tf_op jit(solution)/shard_map/ppermute | solution.py:748
  424.7 10.9 %collective-permute-start.16 = (bf16[24,2432]{1,0:T(8,128)(2,1)S(1)}, bf16[24,2432]{1,0:T(8,128)(2,1)S(1)}, u32[]{:S(2)}, u32[]{:S(2)}) collective-permute-start(bf16[24,2432]{1,0:T(8,128)(2,1)S(1)} %add_convert_fusion.7), channel_id=1, source_target_pairs={{0,16},{8,24},{16,0},{24,8},{1,17},{9,25},{17,1},{25,9},{2,18},{10... | collective-permute-start | bytes 350216 | tf_op jit(solution)/shard_map/ppermute | solution.py:748
  426.0 9.7 %collective-permute-start.17 = (bf16[24,2432]{1,0:T(8,128)(2,1)S(1)}, bf16[24,2432]{1,0:T(8,128)(2,1)S(1)}, u32[]{:S(2)}, u32[]{:S(2)}) collective-permute-start(bf16[24,2432]{1,0:T(8,128)(2,1)S(1)} %add_convert_fusion.7), channel_id=1, source_target_pairs={{0,24},{8,0},{16,8},{24,16},{1,25},{9,1},{17,9},{25,17},{2,26},{10... | collective-permute-start | bytes 350216 | tf_op jit(solution)/shard_map/ppermute | solution.py:748
  435.6 7.6 %collective-permute-start.19 = (bf16[96,768]{1,0:T(8,128)(2,1)S(1)}, bf16[96,768]{1,0:T(8,128)(2,1)S(1)}, u32[]{:S(2)}, u32[]{:S(2)}) collective-permute-start(bf16[96,768]{1,0:T(8,128)(2,1)S(1)} %get-tuple-element.305), channel_id=1, source_target_pairs={{0,1},{1,2},{2,3},{3,0},{4,5},{5,6},{6,7},{7,4},{8,9},{9,10},{10,1... | collective-permute-start | bytes 442376 | tf_op jit(solution)/shard_map/ppermute | solution.py:748
  444.9 14.9 %collective-permute-start.25 = (bf16[24,768]{1,0:T(8,128)(2,1)S(1)}, bf16[24,768]{1,0:T(8,128)(2,1)S(1)}, u32[]{:S(2)}, u32[]{:S(2)}) collective-permute-start(bf16[24,768]{1,0:T(8,128)(2,1)S(1)} %get-tuple-element.315), channel_id=1, source_target_pairs={{0,8},{8,16},{16,24},{24,0},{1,9},{9,17},{17,25},{25,1},{2,10},{10... | collective-permute-start | bytes 110600 | tf_op jit(solution)/shard_map/ppermute | solution.py:748
  448.1 13.0 %collective-permute-start.26 = (bf16[24,768]{1,0:T(8,128)(2,1)S(1)}, bf16[24,768]{1,0:T(8,128)(2,1)S(1)}, u32[]{:S(2)}, u32[]{:S(2)}) collective-permute-start(bf16[24,768]{1,0:T(8,128)(2,1)S(1)} %get-tuple-element.314), channel_id=1, source_target_pairs={{0,16},{8,24},{16,0},{24,8},{1,17},{9,25},{17,1},{25,9},{2,18},{10... | collective-permute-start | bytes 110600 | tf_op jit(solution)/shard_map/ppermute | solution.py:748
  449.2 11.9 %collective-permute-start.27 = (bf16[24,768]{1,0:T(8,128)(2,1)S(1)}, bf16[24,768]{1,0:T(8,128)(2,1)S(1)}, u32[]{:S(2)}, u32[]{:S(2)}) collective-permute-start(bf16[24,768]{1,0:T(8,128)(2,1)S(1)} %get-tuple-element.313), channel_id=1, source_target_pairs={{0,24},{8,0},{16,8},{24,16},{1,25},{9,1},{17,9},{25,17},{2,26},{10... | collective-permute-start | bytes 110600 | tf_op jit(solution)/shard_map/ppermute | solution.py:748
  450.5 22.1 %collective-permute-start.22 = (bf16[4,24,2432]{2,1,0:T(8,128)(2,1)S(1)}, bf16[4,24,2432]{2,1,0:T(8,128)(2,1)S(1)}, u32[]{:S(2)}, u32[]{:S(2)}) collective-permute-start(bf16[4,24,2432]{2,1,0:T(8,128)(2,1)S(1)} %pad_maximum_fusion.2), channel_id=1, source_target_pairs={{0,1},{1,2},{2,3},{3,0},{4,5},{5,6},{6,7},{7,4},{8,9},{9,10},{10,1... | collective-permute-start | bytes 1400840 | tf_op jit(solution)/shard_map/ppermute | solution.py:748
  452.2 22.5 %collective-permute-start.23 = (bf16[4,24,2432]{2,1,0:T(8,128)(2,1)S(1)}, bf16[4,24,2432]{2,1,0:T(8,128)(2,1)S(1)}, u32[]{:S(2)}, u32[]{:S(2)}) collective-permute-start(bf16[4,24,2432]{2,1,0:T(8,128)(2,1)S(1)} %pad_maximum_fusion.2), channel_id=1, source_target_pairs={{0,2},{1,3},{2,0},{3,1},{4,6},{5,7},{6,4},{7,5},{8,10},{9,11},{10,... | collective-permute-start | bytes 1400840 | tf_op jit(solution)/shard_map/ppermute | solution.py:748
  459.9 14.8 %collective-permute-start.24 = (bf16[4,24,2432]{2,1,0:T(8,128)(2,1)S(1)}, bf16[4,24,2432]{2,1,0:T(8,128)(2,1)S(1)}, u32[]{:S(2)}, u32[]{:S(2)}) collective-permute-start(bf16[4,24,2432]{2,1,0:T(8,128)(2,1)S(1)} %pad_maximum_fusion.2), channel_id=1, source_target_pairs={{0,3},{1,0},{2,1},{3,2},{4,7},{5,4},{6,5},{7,6},{8,11},{9,8},{10,9... | collective-permute-start | bytes 1400840 | tf_op jit(solution)/shard_map/ppermute | solution.py:748
  471.1 14.8 %collective-permute-start.31 = (bf16[4,24,768]{2,1,0:T(8,128)(2,1)S(1)}, bf16[4,24,768]{2,1,0:T(8,128)(2,1)S(1)}, u32[]{:S(2)}, u32[]{:S(2)}) collective-permute-start(bf16[4,24,768]{2,1,0:T(8,128)(2,1)S(1)} %pad_maximum_fusion.3), channel_id=1, source_target_pairs={{0,1},{1,2},{2,3},{3,0},{4,5},{5,6},{6,7},{7,4},{8,9},{9,10},{10,1... | collective-permute-start | bytes 442376 | tf_op jit(solution)/shard_map/ppermute | solution.py:748
  471.9 14.0 %collective-permute-start.32 = (bf16[4,24,768]{2,1,0:T(8,128)(2,1)S(1)}, bf16[4,24,768]{2,1,0:T(8,128)(2,1)S(1)}, u32[]{:S(2)}, u32[]{:S(2)}) collective-permute-start(bf16[4,24,768]{2,1,0:T(8,128)(2,1)S(1)} %pad_maximum_fusion.3), channel_id=1, source_target_pairs={{0,2},{1,3},{2,0},{3,1},{4,6},{5,7},{6,4},{7,5},{8,10},{9,11},{10,... | collective-permute-start | bytes 442376 | tf_op jit(solution)/shard_map/ppermute | solution.py:748
  472.6 13.3 %collective-permute-start.33 = (bf16[4,24,768]{2,1,0:T(8,128)(2,1)S(1)}, bf16[4,24,768]{2,1,0:T(8,128)(2,1)S(1)}, u32[]{:S(2)}, u32[]{:S(2)}) collective-permute-start(bf16[4,24,768]{2,1,0:T(8,128)(2,1)S(1)} %pad_maximum_fusion.3), channel_id=1, source_target_pairs={{0,3},{1,0},{2,1},{3,2},{4,7},{5,4},{6,5},{7,6},{8,11},{9,8},{10,9... | collective-permute-start | bytes 442376 | tf_op jit(solution)/shard_map/ppermute | solution.py:748
  476.9 11.2 %collective-permute-start.34 = (bf16[4,4,24,2432]{3,2,1,0:T(8,128)(2,1)S(1)}, bf16[4,4,24,2432]{3,2,1,0:T(8,128)(2,1)}, u32[]{:S(2)}, u32[]{:S(2)}) collective-permute-start(bf16[4,4,24,2432]{3,2,1,0:T(8,128)(2,1)S(1)} %pad_maximum_fusion.refs_0_), channel_id=1, source_target_pairs={{0,4},{4,0},{1,5},{5,1},{2,6},{6,2},{3,7},{7,3},{8,12},{12,8},{9,1... | collective-permute-start | bytes 5603336 | tf_op jit(solution)/shard_map/ppermute | solution.py:739
  (43 other events, 205.1 us)

commit v4 on v3

--- a/solution.py
+++ b/solution.py
@@ -200,8 +200,8 @@
 
     @pl.when(i == steps - 1)
     def _():
-        own_ref[0] = kacc[:, 0:half].T * scale
-        own_ref[1] = vacc[:, 0:half].T
+        own_ref[0] = (kacc[:, 0:half].T * scale).astype(BF)
+        own_ref[1] = vacc[:, 0:half].T.astype(BF)
         far_ref[0] = (kacc[:, half:].T * scale).astype(BF)
         far_ref[1] = vacc[:, half:].T.astype(BF)
 
@@ -229,7 +229,7 @@
         out_specs=[pl.BlockSpec((block, 128), lambda h, i: (i, h)), both, both],
         out_shape=[
             jax.ShapeDtypeStruct((rows, 128 * count), BF),
-            jax.ShapeDtypeStruct((2, rows, 128 * count), F32),
+            jax.ShapeDtypeStruct((2, rows, 128 * count), BF),
             jax.ShapeDtypeStruct((2, rows, 128 * count), BF),
         ],
         scratch_shapes=[
@@ -255,7 +255,7 @@
             dqkv_ref[:, at : at + size] = dq[...]
             for m in range(2):
                 start = (m + 1) * wide + at
-                dqkv_ref[:, start : start + size] = (own[m] + far[m].astype(F32)).astype(BF)
+                dqkv_ref[:, start : start + size] = (own[m].astype(F32) + far[m].astype(F32)).astype(BF)
             at += size
         more = refs[3 * count :]
     else:
@@ -967,7 +967,7 @@
         for n in range(n_dp):
             pick = lambda v: lax.dynamic_index_in_dim(v, lax.rem(my_dp + n, n_dp), 0, keepdims=False)
             blocks.append(add_up([pick(keep), pick(other)]))
-        dx_back, blocks = lax.optimization_barrier((dx_back, blocks))
+        dx_back, blocks[1:] = lax.optimization_barrier((dx_back, blocks[1:]))
         pieces = [block if n == 0 else shift(block, "dp", n) for n, block in enumerate(blocks)]
 
     d_middle, d_branch_b, d_mixed_b, small = route_back(

time: 511 us -> 511 us (level)
  transfers between devices with their start and end apart: 42 -> 42, of which waited for: 16 -> 15; matrix products, arithmetic and copies ran while one was open for 7% -> 7% of each run, Pallas kernels for 52% -> 52%
where the time goes in v4:
time: 511 us; the launch traced here: 504 us
  Pallas kernels  278 us (54%)
  starting transfers between devices  89.8 us (18%)
  waiting for transfers between devices  70.5 us (14%)
  other arithmetic  28.3 us (6%)
  local copies, waits for them, and re-layouts  24.4 us (5%)
  matrix products  10.9 us (2%)
    pallas_call x3, Pallas kernels, attend_back(): pl.pallas_call(functools.partial(attend_back_kernel, scale=1.0 / math.sqr...  62.5 us
    pallas_call x2, Pallas kernels, run_expert(): pl.pallas_call(functools.partial(expert_kernel, part=part, parts=parts, s...  58.6 us
    all_to_all x6, starting transfers between devices, exchange(): return lax.all_to_all(value, axes, 0, 0, tiled=True)  48 us
    ppermute x28, starting transfers between devices, shift(): return lax.ppermute(value, axis, [(i, (i + by) % n) for i in range(n)])  41.1 us
    all_to_all x6, waiting for transfers between devices, exchange(): return lax.all_to_all(value, axes, 0, 0, tiled=True)  39.9 us
    pallas_call x1, Pallas kernels, attend(): pl.pallas_call(functools.partial(attend_kernel, scale=1.0 / math.sqrt(wid...  37.6 us
    pallas_call x2, Pallas kernels, weight_grads(): pl.pallas_call(functools.partial(weights_kernel, count=len(acts), pieces=...  36.2 us
    ppermute x28, waiting for transfers between devices, shift(): return lax.ppermute(value, axis, [(i, (i + by) % n) for i in range(n)])  24.3 us
  transfers between devices with their start and end apart: 42, of which 15 were waited for; matrix products, arithmetic and copies ran while one was open for 7% of the time, Pallas kernels for 52%

profile of v4, /device:TPU:0, one launch (start us, length us, event | category | flops | bytes accessed | tf_op | source)
XLA Modules:
  0.0 503.5 jit_solution(12752788063486533493)
XLA Ops:
  6.9 6.5 %seat_rows.3 = bf16[16,128,768]{2,1,0:T(8,128)(2,1)} custom-call(s32[1,1024]{1,0:T(1,128)} %compare_select_fusion.1.t1, s32[1,1024]{1,0:T(1,128)} %compare_select_fusion.t2, bf16[1024,768]{1,0:T(8,128)(2,1)} %bitcast.103), custom_call_target="tpu_custom_call" | custom-call | flops 805306368 | bytes 786432 | tf_op jit(solution)/shard_map/seat_rows/pallas_call | solution.py:607
  13.4 8.5 %all-to-all-start = ((bf16[16,128,768]{2,1,0:T(8,128)(2,1)}), bf16[16,128,768]{2,1,0:T(8,128)(2,1)}, u32[]{:S(2)}, u32[]{:S(2)}) async-start(bf16[16,128,768]{2,1,0:T(8,128)(2,1)} %seat_rows.3), calls=%async_computation | async-start | bytes 6291456 | tf_op jit(solution)/shard_map/all_to_all | solution.py:743
  22.5 8.3 %project.1 = (bf16[1024,768]{1,0:T(8,128)(2,1)}, bf16[1024,768]{1,0:T(8,128)(2,1)}, bf16[1024,1536]{1,0:T(8,128)(2,1)}) custom-call(bf16[1024,768]{1,0:T(8,128)(2,1)} %bitcast.98, f32[1,768]{1,0:T(1,128)} %broadcast_in_dim.25.gain, bf16[768,2304]{1,0:T(8,128)(2,1)} %w_ref.3), custom_call_target="tpu_custom_call" | custom-call | flops 905969664 | bytes 3932160 | tf_op jit(solution)/shard_map/project/pallas_call | solution.py:61
  31.8 4.9 collective-permute-done.k1.v1
  38.4 37.6 %attend.1 = (bf16[1024,768]{1,0:T(8,128)(2,1)}, bf16[12,1024,2048]{2,1,0:T(8,128)(2,1)}, f32[1024,768]{1,0:T(8,128)}) custom-call(bf16[1024,768]{1,0:T(8,128)(2,1)} %get-tuple-element.131.q_ref, bf16[1024,1536]{1,0:T(8,128)(2,1)} %get-tuple-element.132.k0.v0, bf16[1024,1536]{1,0:T(8,128)(2,1)} %copy-done, bf16[1024,1536]{1,0:T(8,128)(2,1)} %get-tuple-element.132.k0.v0, ...), custom_call_target="tpu_custom_call" | custom-call | flops 196608 | bytes 196608 | tf_op jit(solution)/shard_map/attend/pallas_call | solution.py:130
  76.0 3.8 fusion.69
  85.7 6.7 %seat_rows.4 = bf16[16,72,768]{2,1,0:T(8,128)(2,1)} custom-call(s32[1,1024]{1,0:T(1,128)} %compare_select_fusion.1.t1, s32[1,1024]{1,0:T(1,128)} %compare_select_fusion.t2, f32[1,1024]{1,0:T(1,128)} %bitcast.136, f32[1,1024]{1,0:T(1,128)} %bitcast.135, bf16[1024,768]{1,0:T(8,128)(2,1)} %copy-done.4), custom_call_target="tpu_custom_call" | custom-call | flops 452984832 | bytes 786432 | tf_op jit(solution)/shard_map/seat_rows/pallas_call | solution.py:607
  92.4 7.0 %all-to-all-start.1 = ((bf16[16,72,768]{2,1,0:T(8,128)(2,1)}), bf16[16,72,768]{2,1,0:T(8,128)(2,1)S(1)}, u32[]{:S(2)}, u32[]{:S(2)}) async-start(bf16[16,72,768]{2,1,0:T(8,128)(2,1)} %seat_rows.4), calls=%async_computation.1 | async-start | bytes 3538944 | tf_op jit(solution)/shard_map/all_to_all | solution.py:743
  101.8 4.4 seat_rows.5
  106.2 30.8 %all-to-all-done.1.x_in.gate_in.refs_4_ = bf16[16,72,768]{2,1,0:T(8,128)(2,1)S(1)} async-done(((bf16[16,72,768]{2,1,0:T(8,128)(2,1)}), bf16[16,72,768]{2,1,0:T(8,128)(2,1)S(1)}, u32[]{:S(2)}, u32[]{:S(2)}) %all-to-all-start.1) | async-done | bytes 1769504 | tf_op jit(solution)/shard_map/all_to_all | solution.py:743
  137.0 9.0 %all-to-all-start.2 = ((bf16[16,64,768]{2,1,0:T(8,128)(2,1)}), bf16[16,64,768]{2,1,0:T(8,128)(2,1)S(1)}, u32[]{:S(2)}, u32[]{:S(2)}) async-start(bf16[16,64,768]{2,1,0:T(8,128)(2,1)} %seat_rows.5), calls=%async_computation.2 | async-start | bytes 3145728 | tf_op jit(solution)/shard_map/all_to_all | solution.py:743
  146.0 29.3 %expert.2 = (bf16[16,128,768]{2,1,0:T(8,128)(2,1)}, bf16[16,64,768]{2,1,0:T(8,128)(2,1)}, bf16[1024,3072]{1,0:T(8,128)(2,1)}, bf16[1024,3072]{1,0:T(8,128)(2,1)}...) custom-call(s32[1]{0:T(128)} %bitcast.11.which.at, bf16[16,72,768]{2,1,0:T(8,128)(2,1)} %copy-done.2, ...), custom_call_target="tpu_custom_call" | custom-call | flops 4831838208 | bytes 2359296 | tf_op jit(solution)/shard_map/expert/pallas_call | solution.py:429
  175.3 4.2 all-to-all-done.2.x_in.refs_5_
  179.5 7.6 %all-to-all-start.3 = ((bf16[16,64,768]{2,1,0:T(8,128)(2,1)}), bf16[16,64,768]{2,1,0:T(8,128)(2,1)S(1)}, u32[]{:S(2)}, u32[]{:S(2)}) async-start(bf16[16,64,768]{2,1,0:T(8,128)(2,1)} %get-tuple-element.146), calls=%async_computation.3 | async-start | bytes 3145728 | tf_op jit(solution)/shard_map/all_to_all | solution.py:743
  187.1 29.3 %expert.3 = (bf16[16,128,768]{2,1,0:T(8,128)(2,1)}, bf16[16,72,768]{2,1,0:T(8,128)(2,1)}, bf16[1024,3072]{1,0:T(8,128)(2,1)}, bf16[1024,3072]{1,0:T(8,128)(2,1)}, bf16[1024,768]{1,0:T(8,128)(2,1)}) custom-call(s32[1]{0:T(128)} %bitcast.11.which.at, bf16[16,64,768]{2,1,0:T(8,128)(2,1)} %copy-done.8, ...), custom_call_target="tpu_custom_call", output_to_operand_aliasing={{0}: (4, {})} | custom-call | flops 4831838208 | bytes 2359296 | tf_op jit(solution)/shard_map/expert/pallas_call | solution.py:429
  216.5 4.2 all-to-all-done.3.refs_0_
  221.9 7.8 %all-to-all-start.4 = ((bf16[16,72,768]{2,1,0:T(8,128)(2,1)}), bf16[16,72,768]{2,1,0:T(8,128)(2,1)S(1)}, u32[]{:S(2)}, u32[]{:S(2)}) async-start(bf16[16,72,768]{2,1,0:T(8,128)(2,1)} %get-tuple-element.149), calls=%async_computation.4 | async-start | bytes 3538944 | tf_op jit(solution)/shard_map/all_to_all | solution.py:743
  229.7 19.5 %weight_grads.2 = (bf16[4,2,768,384]{3,2,1,0:T(8,128)(2,1)}, bf16[768,2048]{1,0:T(8,128)(2,1)}, bf16[768,2048]{1,0:T(8,128)(2,1)}) custom-call(s32[1]{0:T(128)} %bitcast.12.at.core, bf16[1024,3072]{1,0:T(8,128)(2,1)} %get-tuple-element.150.refs_0_, bf16[1024,3072]{1,0:T(8,128)(2,1)} %get-tuple-element.151.refs_1_, ...), custom_call_target="tpu_custom_call" | custom-call | flops 393216 | bytes 393216 | tf_op jit(solution)/shard_map/weight_grads/pallas_call | solution.py:509
  249.2 16.7 %weight_grads.3 = bf16[4,2,768,384]{3,2,1,0:T(8,128)(2,1)} custom-call(s32[1]{0:T(128)} %bitcast.13.at.core, bf16[1024,3072]{1,0:T(8,128)(2,1)} %get-tuple-element.150.refs_0_, bf16[1024,3072]{1,0:T(8,128)(2,1)} %get-tuple-element.151.refs_1_, bf16[1024,3072]{1,0:T(8,128)(2,1)} %get-tuple-element.152.refs_2_, bf16[1024,3072]{1,0:T(8,128)(2,1)} %get-tuple-element.153.refs_3_, ...), custom_call_target="tpu_custom_call" | custom-call | flops 393216 | bytes 393216 | tf_op jit(solution)/shard_map/weight_grads/pallas_call | solution.py:509
  267.8 8.2 %all-to-all-start.5 = ((bf16[16,128,768]{2,1,0:T(8,128)(2,1)}), bf16[16,128,768]{2,1,0:T(8,128)(2,1)S(1)}, u32[]{:S(2)}, u32[]{:S(2)}) async-start(bf16[16,128,768]{2,1,0:T(8,128)(2,1)} %get-tuple-element.176), calls=%async_computation.5 | async-start | bytes 6291456 | tf_op jit(solution)/shard_map/all_to_all | solution.py:743
  276.0 6.6 %fusion.27 = (bf16[2,768,384]{2,1,0:T(8,128)(2,1)}, bf16[2,768,384]{2,1,0:T(8,128)(2,1)}, bf16[2,768,384]{2,1,0:T(8,128)(2,1)}, bf16[2,768,384]{2,1,0:T(8,128)(2,1)}) fusion(bf16[4,2,768,384]{3,2,1,0:T(8,128)(2,1)} %collective-permute-done.1, s32[]{:T(128)S(6)} %select_n.196, bf16[4,2,768,384]{3,2,1,0:T(8,128)(2,1)} %weight_grads.3, s32[]{:T(128)S(6)} %select_n.195, ...), kind=kLoop, calls=%fused_computation.39 | loop fusion | flops 9437184 | bytes 14155792 | tf_op jit(solution)/shard_map/convert_element_type | solution.py:763
  288.8 16.5 %route_back.1 = (f32[1024,768]{1,0:T(8,128)}, bf16[1024,768]{1,0:T(8,128)(2,1)}, bf16[1024,768]{1,0:T(8,128)(2,1)}, f32[24,768]{1,0:T(8,128)}) custom-call(s32[1024,1]{1,0:T(8,128)} %get-tuple-element.135.t1, s32[1024,1]{1,0:T(8,128)} %get-tuple-element.136.t2, s32[1024,2]{1,0:T(8,128)} %bitcast.100, f32[1024,16]{1,0:T(8,128)} %get-tuple-element.286.probs, ...), custom_call_target="tpu_custom_call" | custom-call | flops 196608 | bytes 196608 | tf_op jit(solution)/shard_map/route_back/pallas_call | solution.py:713
  305.3 20.8 %attend_back.3 = (bf16[1024,256]{1,0:T(8,128)(2,1)}, bf16[2,1024,256]{2,1,0:T(8,128)(2,1)}, bf16[2,1024,256]{2,1,0:T(8,128)(2,1)}) custom-call(bf16[1024,768]{1,0:T(8,128)(2,1)} %get-tuple-element.131.q_ref, bf16[1024,1536]{1,0:T(8,128)(2,1)} %get-tuple-element.132.k0.v0, bf16[1024,1536]{1,0:T(8,128)(2,1)} %copy-done, ...), custom_call_target="tpu_custom_call" | custom-call | flops 196608 | bytes 196608 | tf_op jit(solution)/shard_map/attend_back/pallas_call | solution.py:215
  326.1 21.0 %attend_back.4 = (bf16[1024,256]{1,0:T(8,128)(2,1)}, bf16[2,1024,256]{2,1,0:T(8,128)(2,1)}, bf16[2,1024,256]{2,1,0:T(8,128)(2,1)}) custom-call(bf16[1024,768]{1,0:T(8,128)(2,1)} %get-tuple-element.131.q_ref, bf16[1024,1536]{1,0:T(8,128)(2,1)} %get-tuple-element.132.k0.v0, bf16[1024,1536]{1,0:T(8,128)(2,1)} %copy-done, ...), custom_call_target="tpu_custom_call" | custom-call | flops 196608 | bytes 196608 | tf_op jit(solution)/shard_map/attend_back/pallas_call | solution.py:215
  349.3 7.9 %unseat.1 = bf16[1024,768]{1,0:T(8,128)(2,1)} custom-call(s32[1024,1]{1,0:T(8,128)} %get-tuple-element.135.t1, s32[1024,1]{1,0:T(8,128)} %get-tuple-element.136.t2, f32[1024,768]{1,0:T(8,128)} %copy-done.1, bf16[16,128,768]{2,1,0:T(8,128)(2,1)} %copy-done.9), custom_call_target="tpu_custom_call" | custom-call | flops 196608 | bytes 196608 | tf_op jit(solution)/shard_map/unseat/pallas_call | solution.py:655
  357.1 9.6 %grad_qkv.3 = (bf16[768,2432]{1,0:T(8,128)(2,1)}, bf16[1024,1536]{1,0:T(8,128)(2,1)}) custom-call(s32[1]{0:T(128)} %constant.165.clone.1.core, bf16[1024,768]{1,0:T(8,128)(2,1)} %get-tuple-element.179.normed, bf16[1024,256]{1,0:T(8,128)(2,1)} %get-tuple-element.171.refs_0_, bf16[1024,256]{1,0:T(8,128)(2,1)} %get-tuple-element.174.refs_1_, ...), custom_call_target="tpu_custom_call" | custom-call | flops 196608 | bytes 196608 | tf_op jit(solution)/shard_map/grad_qkv/pallas_call | solution.py:287
  372.2 4.0 collective-permute-done.7
  386.7 20.7 %attend_back.5 = (bf16[1024,256]{1,0:T(8,128)(2,1)}, bf16[2,1024,256]{2,1,0:T(8,128)(2,1)}, bf16[2,1024,256]{2,1,0:T(8,128)(2,1)}) custom-call(bf16[1024,768]{1,0:T(8,128)(2,1)} %get-tuple-element.131.q_ref, bf16[1024,1536]{1,0:T(8,128)(2,1)} %get-tuple-element.132.k0.v0, bf16[1024,1536]{1,0:T(8,128)(2,1)} %copy-done, ...), custom_call_target="tpu_custom_call" | custom-call | flops 196608 | bytes 196608 | tf_op jit(solution)/shard_map/attend_back/pallas_call | solution.py:215
  415.5 3.8 grad_qkv.4
  430.7 4.6 collective-permute-done.16
  453.0 6.5 %spread.1 = (f32[4,768,384]{2,1,0:T(8,128)}, f32[4,384,768]{2,1,0:T(8,128)}) custom-call(s32[1]{0:T(128)} %bitcast.11.which.at, bf16[2,768,384]{2,1,0:T(8,128)(2,1)} %get-tuple-element.225.refs_0_, bf16[2,768,384]{2,1,0:T(8,128)(2,1)} %collective-permute-done.4.refs_1_, bf16[2,768,384]{2,1,0:T(8,128)(2,1)} %collective-permute-done.5.refs_2_, ...), custom_call_target="tpu_custom_call" | custom-call | flops 73728 | bytes 3538944 | tf_op jit(solution)/shard_map/spread/pallas_call | solution.py:837
  488.8 9.8 %assemble.1 = (f32[768,2304]{1,0:T(8,128)}, f32[768,768]{1,0:T(8,128)}, f32[768,128]{1,0:T(8,128)}, f32[768,1]{1,0:T(8,128)}) custom-call(s32[3]{0:T(128)} %pad_add_fusion.at, bf16[768,2304]{1,0:T(8,128)(2,1)} %w_ref.3, bf16[4,4,24,2432]{3,2,1,0:T(8,128)(2,1)} %copy-done.10, bf16[4,4,24,768]{3,2,1,0:T(8,128)(2,1)} %copy-done.14, ...), custom_call_target="tpu_custom_call" | custom-call | flops 442368 | bytes 5308416 | tf_op jit(solution)/shard_map/assemble/pallas_call | solution.py:806
  (197 shorter events, 116.0 us)
Async XLA Ops:
  13.4 79.0 %all-to-all-start = ((bf16[16,128,768]{2,1,0:T(8,128)(2,1)}), bf16[16,128,768]{2,1,0:T(8,128)(2,1)}, u32[]{:S(2)}, u32[]{:S(2)}) async-start(bf16[16,128,768]{2,1,0:T(8,128)(2,1)} %seat_rows.3), calls=%async_computation | async-start | bytes 6291456 | tf_op jit(solution)/shard_map/all_to_all | solution.py:743
  92.4 44.6 %all-to-all-start.1 = ((bf16[16,72,768]{2,1,0:T(8,128)(2,1)}), bf16[16,72,768]{2,1,0:T(8,128)(2,1)S(1)}, u32[]{:S(2)}, u32[]{:S(2)}) async-start(bf16[16,72,768]{2,1,0:T(8,128)(2,1)} %seat_rows.4), calls=%async_computation.1 | async-start | bytes 3538944 | tf_op jit(solution)/shard_map/all_to_all | solution.py:743
  137.0 42.5 %all-to-all-start.2 = ((bf16[16,64,768]{2,1,0:T(8,128)(2,1)}), bf16[16,64,768]{2,1,0:T(8,128)(2,1)S(1)}, u32[]{:S(2)}, u32[]{:S(2)}) async-start(bf16[16,64,768]{2,1,0:T(8,128)(2,1)} %seat_rows.5), calls=%async_computation.2 | async-start | bytes 3145728 | tf_op jit(solution)/shard_map/all_to_all | solution.py:743
  179.5 41.1 %all-to-all-start.3 = ((bf16[16,64,768]{2,1,0:T(8,128)(2,1)}), bf16[16,64,768]{2,1,0:T(8,128)(2,1)S(1)}, u32[]{:S(2)}, u32[]{:S(2)}) async-start(bf16[16,64,768]{2,1,0:T(8,128)(2,1)} %get-tuple-element.146), calls=%async_computation.3 | async-start | bytes 3145728 | tf_op jit(solution)/shard_map/all_to_all | solution.py:743
  221.9 44.7 %all-to-all-start.4 = ((bf16[16,72,768]{2,1,0:T(8,128)(2,1)}), bf16[16,72,768]{2,1,0:T(8,128)(2,1)S(1)}, u32[]{:S(2)}, u32[]{:S(2)}) async-start(bf16[16,72,768]{2,1,0:T(8,128)(2,1)} %get-tuple-element.149), calls=%async_computation.4 | async-start | bytes 3538944 | tf_op jit(solution)/shard_map/all_to_all | solution.py:743
  266.6 9.4 %collective-permute-start.1 = (bf16[4,2,768,384]{3,2,1,0:T(8,128)(2,1)}, bf16[4,2,768,384]{3,2,1,0:T(8,128)(2,1)}, u32[]{:S(2)}, u32[]{:S(2)}) collective-permute-start(bf16[4,2,768,384]{3,2,1,0:T(8,128)(2,1)} %get-tuple-element.164), channel_id=1, source_target_pairs={{0,4},{4,0},{1,5},{5,1},{2,6},{6,2},{3,7},{7,3},{8,12},{12,8},{9,1... | collective-permute-start | bytes 14155784 | tf_op jit(solution)/shard_map/ppermute | solution.py:739
  267.8 79.8 %all-to-all-start.5 = ((bf16[16,128,768]{2,1,0:T(8,128)(2,1)}), bf16[16,128,768]{2,1,0:T(8,128)(2,1)S(1)}, u32[]{:S(2)}, u32[]{:S(2)}) async-start(bf16[16,128,768]{2,1,0:T(8,128)(2,1)} %get-tuple-element.176), calls=%async_computation.5 | async-start | bytes 6291456 | tf_op jit(solution)/shard_map/all_to_all | solution.py:743
  282.6 84.2 %collective-permute-start.4 = (bf16[2,768,384]{2,1,0:T(8,128)(2,1)}, bf16[2,768,384]{2,1,0:T(8,128)(2,1)}, u32[]{:S(2)}, u32[]{:S(2)}) collective-permute-start(bf16[2,768,384]{2,1,0:T(8,128)(2,1)} %get-tuple-element.188), channel_id=1, source_target_pairs={{0,1},{1,2},{2,3},{3,0},{4,5},{5,6},{6,7},{7,4},{8,9},{9,10},{10,1... | collective-permute-start | bytes 3538952 | tf_op jit(solution)/shard_map/ppermute | solution.py:748
  284.5 82.3 %collective-permute-start.5 = (bf16[2,768,384]{2,1,0:T(8,128)(2,1)}, bf16[2,768,384]{2,1,0:T(8,128)(2,1)}, u32[]{:S(2)}, u32[]{:S(2)}) collective-permute-start(bf16[2,768,384]{2,1,0:T(8,128)(2,1)} %get-tuple-element.189), channel_id=1, source_target_pairs={{0,2},{1,3},{2,0},{3,1},{4,6},{5,7},{6,4},{7,5},{8,10},{9,11},{10,... | collective-permute-start | bytes 3538952 | tf_op jit(solution)/shard_map/ppermute | solution.py:748
  286.0 83.3 %collective-permute-start.6 = (bf16[2,768,384]{2,1,0:T(8,128)(2,1)}, bf16[2,768,384]{2,1,0:T(8,128)(2,1)}, u32[]{:S(2)}, u32[]{:S(2)}) collective-permute-start(bf16[2,768,384]{2,1,0:T(8,128)(2,1)} %get-tuple-element.190), channel_id=1, source_target_pairs={{0,3},{1,0},{2,1},{3,2},{4,7},{5,4},{6,5},{7,6},{8,11},{9,8},{10,9... | collective-permute-start | bytes 3538952 | tf_op jit(solution)/shard_map/ppermute | solution.py:748
  347.1 10.0 %collective-permute-start.3 = (bf16[2,1024,256]{2,1,0:T(8,128)(2,1)}, bf16[2,1024,256]{2,1,0:T(8,128)(2,1)}, u32[]{:S(2)}, u32[]{:S(2)}) collective-permute-start(bf16[2,1024,256]{2,1,0:T(8,128)(2,1)} %get-tuple-element.173), channel_id=1, source_target_pairs={{0,4},{4,0},{1,5},{5,1},{2,6},{6,2},{3,7},{7,3},{8,12},{12,8},{9,1... | collective-permute-start | bytes 3145736 | tf_op jit(solution)/shard_map/ppermute | solution.py:739
  347.1 10.0 %collective-permute-start.2 = (bf16[2,1024,256]{2,1,0:T(8,128)(2,1)}, bf16[2,1024,256]{2,1,0:T(8,128)(2,1)}, u32[]{:S(2)}, u32[]{:S(2)}) collective-permute-start(bf16[2,1024,256]{2,1,0:T(8,128)(2,1)} %get-tuple-element.170), channel_id=1, source_target_pairs={{0,4},{4,0},{1,5},{5,1},{2,6},{6,2},{3,7},{7,3},{8,12},{12,8},{9,1... | collective-permute-start | bytes 3145736 | tf_op jit(solution)/shard_map/ppermute | solution.py:739
  378.3 29.1 %collective-permute-start.10 = (bf16[96,2432]{1,0:T(8,128)(2,1)S(1)}, bf16[96,2432]{1,0:T(8,128)(2,1)S(1)}, u32[]{:S(2)}, u32[]{:S(2)}) collective-permute-start(bf16[96,2432]{1,0:T(8,128)(2,1)S(1)} %get-tuple-element.297), channel_id=1, source_target_pairs={{0,3},{1,0},{2,1},{3,2},{4,7},{5,4},{6,5},{7,6},{8,11},{9,8},{10,9... | collective-permute-start | bytes 1400840 | tf_op jit(solution)/shard_map/ppermute | solution.py:748
  381.0 26.4 %collective-permute-start.8 = (bf16[96,2432]{1,0:T(8,128)(2,1)S(1)}, bf16[96,2432]{1,0:T(8,128)(2,1)}, u32[]{:S(2)}, u32[]{:S(2)}) collective-permute-start(bf16[96,2432]{1,0:T(8,128)(2,1)S(1)} %get-tuple-element.299), channel_id=1, source_target_pairs={{0,1},{1,2},{2,3},{3,0},{4,5},{5,6},{6,7},{7,4},{8,9},{9,10},{10,1... | collective-permute-start | bytes 1400840 | tf_op jit(solution)/shard_map/ppermute | solution.py:748
  381.0 26.4 %collective-permute-start.9 = (bf16[96,2432]{1,0:T(8,128)(2,1)S(1)}, bf16[96,2432]{1,0:T(8,128)(2,1)}, u32[]{:S(2)}, u32[]{:S(2)}) collective-permute-start(bf16[96,2432]{1,0:T(8,128)(2,1)S(1)} %get-tuple-element.298), channel_id=1, source_target_pairs={{0,2},{1,3},{2,0},{3,1},{4,6},{5,7},{6,4},{7,5},{8,10},{9,11},{10,... | collective-permute-start | bytes 1400840 | tf_op jit(solution)/shard_map/ppermute | solution.py:748
  409.1 13.5 %collective-permute-start.12 = (bf16[24,2432]{1,0:T(8,128)(2,1)S(1)}, bf16[24,2432]{1,0:T(8,128)(2,1)S(1)}, u32[]{:S(2)}, u32[]{:S(2)}) collective-permute-start(bf16[24,2432]{1,0:T(8,128)(2,1)S(1)} %get-tuple-element.309), channel_id=1, source_target_pairs={{0,8},{8,16},{16,24},{24,0},{1,9},{9,17},{17,25},{25,1},{2,10},{10... | collective-permute-start | bytes 350216 | tf_op jit(solution)/shard_map/ppermute | solution.py:748
  411.6 11.0 %collective-permute-start.13 = (bf16[24,2432]{1,0:T(8,128)(2,1)S(1)}, bf16[24,2432]{1,0:T(8,128)(2,1)S(1)}, u32[]{:S(2)}, u32[]{:S(2)}) collective-permute-start(bf16[24,2432]{1,0:T(8,128)(2,1)S(1)} %get-tuple-element.308), channel_id=1, source_target_pairs={{0,16},{8,24},{16,0},{24,8},{1,17},{9,25},{17,1},{25,9},{2,18},{10... | collective-permute-start | bytes 350216 | tf_op jit(solution)/shard_map/ppermute | solution.py:748
  411.6 11.0 %collective-permute-start.14 = (bf16[24,2432]{1,0:T(8,128)(2,1)S(1)}, bf16[24,2432]{1,0:T(8,128)(2,1)S(1)}, u32[]{:S(2)}, u32[]{:S(2)}) collective-permute-start(bf16[24,2432]{1,0:T(8,128)(2,1)S(1)} %get-tuple-element.307), channel_id=1, source_target_pairs={{0,24},{8,0},{16,8},{24,16},{1,25},{9,1},{17,9},{25,17},{2,26},{10... | collective-permute-start | bytes 350216 | tf_op jit(solution)/shard_map/ppermute | solution.py:748
  422.7 7.9 %collective-permute-start.15 = (bf16[24,2432]{1,0:T(8,128)(2,1)S(1)}, bf16[24,2432]{1,0:T(8,128)(2,1)S(1)}, u32[]{:S(2)}, u32[]{:S(2)}) collective-permute-start(bf16[24,2432]{1,0:T(8,128)(2,1)S(1)} %add_convert_fusion.7), channel_id=1, source_target_pairs={{0,8},{8,16},{16,24},{24,0},{1,9},{9,17},{17,25},{25,1},{2,10},{10... | collective-permute-start | bytes 350216 | tf_op jit(solution)/shard_map/ppermute | solution.py:748
  424.7 10.5 %collective-permute-start.16 = (bf16[24,2432]{1,0:T(8,128)(2,1)S(1)}, bf16[24,2432]{1,0:T(8,128)(2,1)S(1)}, u32[]{:S(2)}, u32[]{:S(2)}) collective-permute-start(bf16[24,2432]{1,0:T(8,128)(2,1)S(1)} %add_convert_fusion.7), channel_id=1, source_target_pairs={{0,16},{8,24},{16,0},{24,8},{1,17},{9,25},{17,1},{25,9},{2,18},{10... | collective-permute-start | bytes 350216 | tf_op jit(solution)/shard_map/ppermute | solution.py:748
  425.9 9.3 %collective-permute-start.17 = (bf16[24,2432]{1,0:T(8,128)(2,1)S(1)}, bf16[24,2432]{1,0:T(8,128)(2,1)S(1)}, u32[]{:S(2)}, u32[]{:S(2)}) collective-permute-start(bf16[24,2432]{1,0:T(8,128)(2,1)S(1)} %add_convert_fusion.7), channel_id=1, source_target_pairs={{0,24},{8,0},{16,8},{24,16},{1,25},{9,1},{17,9},{25,17},{2,26},{10... | collective-permute-start | bytes 350216 | tf_op jit(solution)/shard_map/ppermute | solution.py:748
  436.7 7.9 %collective-permute-start.20 = (bf16[96,768]{1,0:T(8,128)(2,1)S(1)}, bf16[96,768]{1,0:T(8,128)(2,1)S(1)}, u32[]{:S(2)}, u32[]{:S(2)}) collective-permute-start(bf16[96,768]{1,0:T(8,128)(2,1)S(1)} %get-tuple-element.302), channel_id=1, source_target_pairs={{0,2},{1,3},{2,0},{3,1},{4,6},{5,7},{6,4},{7,5},{8,10},{9,11},{10,... | collective-permute-start | bytes 442376 | tf_op jit(solution)/shard_map/ppermute | solution.py:748
  444.8 14.7 %collective-permute-start.25 = (bf16[24,768]{1,0:T(8,128)(2,1)S(1)}, bf16[24,768]{1,0:T(8,128)(2,1)S(1)}, u32[]{:S(2)}, u32[]{:S(2)}) collective-permute-start(bf16[24,768]{1,0:T(8,128)(2,1)S(1)} %get-tuple-element.313), channel_id=1, source_target_pairs={{0,8},{8,16},{16,24},{24,0},{1,9},{9,17},{17,25},{25,1},{2,10},{10... | collective-permute-start | bytes 110600 | tf_op jit(solution)/shard_map/ppermute | solution.py:748
  447.9 13.0 %collective-permute-start.26 = (bf16[24,768]{1,0:T(8,128)(2,1)S(1)}, bf16[24,768]{1,0:T(8,128)(2,1)S(1)}, u32[]{:S(2)}, u32[]{:S(2)}) collective-permute-start(bf16[24,768]{1,0:T(8,128)(2,1)S(1)} %get-tuple-element.312), channel_id=1, source_target_pairs={{0,16},{8,24},{16,0},{24,8},{1,17},{9,25},{17,1},{25,9},{2,18},{10... | collective-permute-start | bytes 110600 | tf_op jit(solution)/shard_map/ppermute | solution.py:748
  448.7 12.1 %collective-permute-start.27 = (bf16[24,768]{1,0:T(8,128)(2,1)S(1)}, bf16[24,768]{1,0:T(8,128)(2,1)S(1)}, u32[]{:S(2)}, u32[]{:S(2)}) collective-permute-start(bf16[24,768]{1,0:T(8,128)(2,1)S(1)} %get-tuple-element.311), channel_id=1, source_target_pairs={{0,24},{8,0},{16,8},{24,16},{1,25},{9,1},{17,9},{25,17},{2,26},{10... | collective-permute-start | bytes 110600 | tf_op jit(solution)/shard_map/ppermute | solution.py:748
  450.3 22.2 %collective-permute-start.22 = (bf16[4,24,2432]{2,1,0:T(8,128)(2,1)S(1)}, bf16[4,24,2432]{2,1,0:T(8,128)(2,1)S(1)}, u32[]{:S(2)}, u32[]{:S(2)}) collective-permute-start(bf16[4,24,2432]{2,1,0:T(8,128)(2,1)S(1)} %pad_maximum_fusion.2), channel_id=1, source_target_pairs={{0,1},{1,2},{2,3},{3,0},{4,5},{5,6},{6,7},{7,4},{8,9},{9,10},{10,1... | collective-permute-start | bytes 1400840 | tf_op jit(solution)/shard_map/ppermute | solution.py:748
  452.0 22.6 %collective-permute-start.23 = (bf16[4,24,2432]{2,1,0:T(8,128)(2,1)S(1)}, bf16[4,24,2432]{2,1,0:T(8,128)(2,1)S(1)}, u32[]{:S(2)}, u32[]{:S(2)}) collective-permute-start(bf16[4,24,2432]{2,1,0:T(8,128)(2,1)S(1)} %pad_maximum_fusion.2), channel_id=1, source_target_pairs={{0,2},{1,3},{2,0},{3,1},{4,6},{5,7},{6,4},{7,5},{8,10},{9,11},{10,... | collective-permute-start | bytes 1400840 | tf_op jit(solution)/shard_map/ppermute | solution.py:748
  459.5 15.1 %collective-permute-start.24 = (bf16[4,24,2432]{2,1,0:T(8,128)(2,1)S(1)}, bf16[4,24,2432]{2,1,0:T(8,128)(2,1)S(1)}, u32[]{:S(2)}, u32[]{:S(2)}) collective-permute-start(bf16[4,24,2432]{2,1,0:T(8,128)(2,1)S(1)} %pad_maximum_fusion.2), channel_id=1, source_target_pairs={{0,3},{1,0},{2,1},{3,2},{4,7},{5,4},{6,5},{7,6},{8,11},{9,8},{10,9... | collective-permute-start | bytes 1400840 | tf_op jit(solution)/shard_map/ppermute | solution.py:748
  470.8 15.0 %collective-permute-start.31 = (bf16[4,24,768]{2,1,0:T(8,128)(2,1)S(1)}, bf16[4,24,768]{2,1,0:T(8,128)(2,1)S(1)}, u32[]{:S(2)}, u32[]{:S(2)}) collective-permute-start(bf16[4,24,768]{2,1,0:T(8,128)(2,1)S(1)} %pad_maximum_fusion.3), channel_id=1, source_target_pairs={{0,1},{1,2},{2,3},{3,0},{4,5},{5,6},{6,7},{7,4},{8,9},{9,10},{10,1... | collective-permute-start | bytes 442376 | tf_op jit(solution)/shard_map/ppermute | solution.py:748
  471.5 14.3 %collective-permute-start.32 = (bf16[4,24,768]{2,1,0:T(8,128)(2,1)S(1)}, bf16[4,24,768]{2,1,0:T(8,128)(2,1)S(1)}, u32[]{:S(2)}, u32[]{:S(2)}) collective-permute-start(bf16[4,24,768]{2,1,0:T(8,128)(2,1)S(1)} %pad_maximum_fusion.3), channel_id=1, source_target_pairs={{0,2},{1,3},{2,0},{3,1},{4,6},{5,7},{6,4},{7,5},{8,10},{9,11},{10,... | collective-permute-start | bytes 442376 | tf_op jit(solution)/shard_map/ppermute | solution.py:748
  472.5 13.3 %collective-permute-start.33 = (bf16[4,24,768]{2,1,0:T(8,128)(2,1)S(1)}, bf16[4,24,768]{2,1,0:T(8,128)(2,1)S(1)}, u32[]{:S(2)}, u32[]{:S(2)}) collective-permute-start(bf16[4,24,768]{2,1,0:T(8,128)(2,1)S(1)} %pad_maximum_fusion.3), channel_id=1, source_target_pairs={{0,3},{1,0},{2,1},{3,2},{4,7},{5,4},{6,5},{7,6},{8,11},{9,8},{10,9... | collective-permute-start | bytes 442376 | tf_op jit(solution)/shard_map/ppermute | solution.py:748
  476.8 11.2 %collective-permute-start.34 = (bf16[4,4,24,2432]{3,2,1,0:T(8,128)(2,1)S(1)}, bf16[4,4,24,2432]{3,2,1,0:T(8,128)(2,1)}, u32[]{:S(2)}, u32[]{:S(2)}) collective-permute-start(bf16[4,4,24,2432]{3,2,1,0:T(8,128)(2,1)S(1)} %pad_maximum_fusion.refs_0_), channel_id=1, source_target_pairs={{0,4},{4,0},{1,5},{5,1},{2,6},{6,2},{3,7},{7,3},{8,12},{12,8},{9,1... | collective-permute-start | bytes 5603336 | tf_op jit(solution)/shard_map/ppermute | solution.py:739
  (43 other events, 206.9 us)

commit v5 on v4

--- a/solution.py
+++ b/solution.py
@@ -768,7 +768,7 @@
     return [x] + [shift(x, axis, s) for s in range(1, n)]
 
 
-def assemble_kernel(at, w_ref, *refs, groups, spans):
+def assemble_kernel(at, w_ref, *refs, groups, spans, n_small):
     ins, outs = refs[: 2 * groups], refs[2 * groups :]
     me = at[2]
     owners, rows = ins[0].shape[1], ins[0].shape[2]
@@ -784,10 +784,12 @@
     is_mine = pl.program_id(0) == at[0]
     pl.when(is_mine)(lambda: write(ins[:groups]))
     pl.when(jnp.logical_not(is_mine))(lambda: write(ins[groups:]))
+    both = outs[2][...]
+    outs[2][:, 0:n_small] = both[:, 0:n_small] + both[:, n_small : 2 * n_small]
     outs[-1][...] = jnp.sum(outs[0][...] * w_ref[...].astype(F32), axis=1, keepdims=True)
 
 
-def assemble(sums, spans, widths, w_qkv):
+def assemble(sums, spans, widths, w_qkv, n_small):
     n_dp, owners, rows, _ = sums[0][0].shape
     n_ctx = lax.axis_size("ctx")
     block = owners * rows
@@ -804,7 +806,7 @@
     line = lambda cols: pl.BlockSpec((block, cols), lambda c, d, at: (c * n_dp + d, 0))
     widths = [*widths, 1]
     return pl.pallas_call(
-        functools.partial(assemble_kernel, groups=len(sums), spans=spans),
+        functools.partial(assemble_kernel, groups=len(sums), spans=spans, n_small=n_small),
         grid_spec=pltpu.PrefetchScalarGridSpec(
             num_scalar_prefetch=1,
             grid=(n_ctx, n_dp),
@@ -1030,10 +1032,8 @@
         [(m * cols_b // 3, 0, m * width + start_b, cols_b // 3) for m in range(3)],
     ]
     grad_w_qkv, grad_w_out, small_sum, gain_sum = assemble(
-        [all_a, all_b], spans, (3 * width, width, SMALL), w_qkv
+        [all_a, all_b], spans, (3 * width, width, SMALL), w_qkv, small.shape[0]
     )
-    n_small = small.shape[0]
-    small_sum = small_sum[:, :n_small] + small_sum[:, n_small : 2 * n_small]
     return (
         result.reshape(image_count, half_len, width),
         d_tokens.reshape(image_count, half_len, width),

time: 511 us -> 512 us (level)
  no operation moved by 1% of the time
where the time goes in v5:
time: 512 us; the launch traced here: 504 us
  Pallas kernels  278 us (54%)
  starting transfers between devices  89.8 us (18%)
  waiting for transfers between devices  70.5 us (14%)
  other arithmetic  26.9 us (5%)
  local copies, waits for them, and re-layouts  26.4 us (5%)
  matrix products  10.9 us (2%)
    pallas_call x3, Pallas kernels, attend_back(): pl.pallas_call(functools.partial(attend_back_kernel, scale=1.0 / math.sqr...  62.5 us
    pallas_call x2, Pallas kernels, run_expert(): pl.pallas_call(functools.partial(expert_kernel, part=part, parts=parts, s...  58.6 us
    all_to_all x6, starting transfers between devices, exchange(): return lax.all_to_all(value, axes, 0, 0, tiled=True)  48 us
    ppermute x28, starting transfers between devices, shift(): return lax.ppermute(value, axis, [(i, (i + by) % n) for i in range(n)])  41.1 us
    all_to_all x6, waiting for transfers between devices, exchange(): return lax.all_to_all(value, axes, 0, 0, tiled=True)  39.9 us
    pallas_call x1, Pallas kernels, attend(): pl.pallas_call(functools.partial(attend_kernel, scale=1.0 / math.sqrt(wid...  37.6 us
    pallas_call x2, Pallas kernels, weight_grads(): pl.pallas_call(functools.partial(weights_kernel, count=len(acts), pieces=...  36.2 us
    ppermute x28, waiting for transfers between devices, shift(): return lax.ppermute(value, axis, [(i, (i + by) % n) for i in range(n)])  24.3 us
  transfers between devices with their start and end apart: 42, of which 15 were waited for; matrix products, arithmetic and copies ran while one was open for 7% of the time, Pallas kernels for 52%

profile of v5, /device:TPU:0, one launch (start us, length us, event | category | flops | bytes accessed | tf_op | source)
XLA Modules:
  0.0 504.2 jit_solution(7462292757898711591)
XLA Ops:
  6.9 6.5 %seat_rows.3 = bf16[16,128,768]{2,1,0:T(8,128)(2,1)} custom-call(s32[1,1024]{1,0:T(1,128)} %compare_select_fusion.1.t1, s32[1,1024]{1,0:T(1,128)} %compare_select_fusion.t2, bf16[1024,768]{1,0:T(8,128)(2,1)} %bitcast.103), custom_call_target="tpu_custom_call" | custom-call | flops 805306368 | bytes 786432 | tf_op jit(solution)/shard_map/seat_rows/pallas_call | solution.py:607
  13.4 8.5 %all-to-all-start = ((bf16[16,128,768]{2,1,0:T(8,128)(2,1)}), bf16[16,128,768]{2,1,0:T(8,128)(2,1)}, u32[]{:S(2)}, u32[]{:S(2)}) async-start(bf16[16,128,768]{2,1,0:T(8,128)(2,1)} %seat_rows.3), calls=%async_computation | async-start | bytes 6291456 | tf_op jit(solution)/shard_map/all_to_all | solution.py:743
  22.5 8.3 %project.1 = (bf16[1024,768]{1,0:T(8,128)(2,1)}, bf16[1024,768]{1,0:T(8,128)(2,1)}, bf16[1024,1536]{1,0:T(8,128)(2,1)}) custom-call(bf16[1024,768]{1,0:T(8,128)(2,1)} %bitcast.98, f32[1,768]{1,0:T(1,128)} %broadcast_in_dim.25.gain, bf16[768,2304]{1,0:T(8,128)(2,1)} %w_ref.3), custom_call_target="tpu_custom_call" | custom-call | flops 905969664 | bytes 3932160 | tf_op jit(solution)/shard_map/project/pallas_call | solution.py:61
  31.8 4.9 collective-permute-done.k1.v1
  38.4 37.6 %attend.1 = (bf16[1024,768]{1,0:T(8,128)(2,1)}, bf16[12,1024,2048]{2,1,0:T(8,128)(2,1)}, f32[1024,768]{1,0:T(8,128)}) custom-call(bf16[1024,768]{1,0:T(8,128)(2,1)} %get-tuple-element.131.q_ref, bf16[1024,1536]{1,0:T(8,128)(2,1)} %get-tuple-element.132.k0.v0, bf16[1024,1536]{1,0:T(8,128)(2,1)} %copy-done, bf16[1024,1536]{1,0:T(8,128)(2,1)} %get-tuple-element.132.k0.v0, ...), custom_call_target="tpu_custom_call" | custom-call | flops 196608 | bytes 196608 | tf_op jit(solution)/shard_map/attend/pallas_call | solution.py:130
  76.0 3.8 fusion.69
  85.7 6.7 %seat_rows.4 = bf16[16,72,768]{2,1,0:T(8,128)(2,1)} custom-call(s32[1,1024]{1,0:T(1,128)} %compare_select_fusion.1.t1, s32[1,1024]{1,0:T(1,128)} %compare_select_fusion.t2, f32[1,1024]{1,0:T(1,128)} %bitcast.136, f32[1,1024]{1,0:T(1,128)} %bitcast.135, bf16[1024,768]{1,0:T(8,128)(2,1)} %copy-done.4), custom_call_target="tpu_custom_call" | custom-call | flops 452984832 | bytes 786432 | tf_op jit(solution)/shard_map/seat_rows/pallas_call | solution.py:607
  92.4 7.0 %all-to-all-start.1 = ((bf16[16,72,768]{2,1,0:T(8,128)(2,1)}), bf16[16,72,768]{2,1,0:T(8,128)(2,1)S(1)}, u32[]{:S(2)}, u32[]{:S(2)}) async-start(bf16[16,72,768]{2,1,0:T(8,128)(2,1)} %seat_rows.4), calls=%async_computation.1 | async-start | bytes 3538944 | tf_op jit(solution)/shard_map/all_to_all | solution.py:743
  101.8 4.4 seat_rows.5
  106.2 30.8 %all-to-all-done.1.x_in.gate_in.refs_4_ = bf16[16,72,768]{2,1,0:T(8,128)(2,1)S(1)} async-done(((bf16[16,72,768]{2,1,0:T(8,128)(2,1)}), bf16[16,72,768]{2,1,0:T(8,128)(2,1)S(1)}, u32[]{:S(2)}, u32[]{:S(2)}) %all-to-all-start.1) | async-done | bytes 1769504 | tf_op jit(solution)/shard_map/all_to_all | solution.py:743
  137.0 9.0 %all-to-all-start.2 = ((bf16[16,64,768]{2,1,0:T(8,128)(2,1)}), bf16[16,64,768]{2,1,0:T(8,128)(2,1)S(1)}, u32[]{:S(2)}, u32[]{:S(2)}) async-start(bf16[16,64,768]{2,1,0:T(8,128)(2,1)} %seat_rows.5), calls=%async_computation.2 | async-start | bytes 3145728 | tf_op jit(solution)/shard_map/all_to_all | solution.py:743
  146.0 29.3 %expert.2 = (bf16[16,128,768]{2,1,0:T(8,128)(2,1)}, bf16[16,64,768]{2,1,0:T(8,128)(2,1)}, bf16[1024,3072]{1,0:T(8,128)(2,1)}, bf16[1024,3072]{1,0:T(8,128)(2,1)}...) custom-call(s32[1]{0:T(128)} %bitcast.11.which.at, bf16[16,72,768]{2,1,0:T(8,128)(2,1)} %copy-done.2, ...), custom_call_target="tpu_custom_call" | custom-call | flops 4831838208 | bytes 2359296 | tf_op jit(solution)/shard_map/expert/pallas_call | solution.py:429
  175.3 4.2 all-to-all-done.2.x_in.refs_5_
  179.5 7.6 %all-to-all-start.3 = ((bf16[16,64,768]{2,1,0:T(8,128)(2,1)}), bf16[16,64,768]{2,1,0:T(8,128)(2,1)S(1)}, u32[]{:S(2)}, u32[]{:S(2)}) async-start(bf16[16,64,768]{2,1,0:T(8,128)(2,1)} %get-tuple-element.146), calls=%async_computation.3 | async-start | bytes 3145728 | tf_op jit(solution)/shard_map/all_to_all | solution.py:743
  187.1 29.3 %expert.3 = (bf16[16,128,768]{2,1,0:T(8,128)(2,1)}, bf16[16,72,768]{2,1,0:T(8,128)(2,1)}, bf16[1024,3072]{1,0:T(8,128)(2,1)}, bf16[1024,3072]{1,0:T(8,128)(2,1)}, bf16[1024,768]{1,0:T(8,128)(2,1)}) custom-call(s32[1]{0:T(128)} %bitcast.11.which.at, bf16[16,64,768]{2,1,0:T(8,128)(2,1)} %copy-done.8, ...), custom_call_target="tpu_custom_call", output_to_operand_aliasing={{0}: (4, {})} | custom-call | flops 4831838208 | bytes 2359296 | tf_op jit(solution)/shard_map/expert/pallas_call | solution.py:429
  216.5 4.2 all-to-all-done.3.refs_0_
  221.9 7.8 %all-to-all-start.4 = ((bf16[16,72,768]{2,1,0:T(8,128)(2,1)}), bf16[16,72,768]{2,1,0:T(8,128)(2,1)S(1)}, u32[]{:S(2)}, u32[]{:S(2)}) async-start(bf16[16,72,768]{2,1,0:T(8,128)(2,1)} %get-tuple-element.149), calls=%async_computation.4 | async-start | bytes 3538944 | tf_op jit(solution)/shard_map/all_to_all | solution.py:743
  229.7 19.5 %weight_grads.2 = (bf16[4,2,768,384]{3,2,1,0:T(8,128)(2,1)}, bf16[768,2048]{1,0:T(8,128)(2,1)}, bf16[768,2048]{1,0:T(8,128)(2,1)}) custom-call(s32[1]{0:T(128)} %bitcast.12.at.core, bf16[1024,3072]{1,0:T(8,128)(2,1)} %get-tuple-element.150.refs_0_, bf16[1024,3072]{1,0:T(8,128)(2,1)} %get-tuple-element.151.refs_1_, ...), custom_call_target="tpu_custom_call" | custom-call | flops 393216 | bytes 393216 | tf_op jit(solution)/shard_map/weight_grads/pallas_call | solution.py:509
  249.2 16.7 %weight_grads.3 = bf16[4,2,768,384]{3,2,1,0:T(8,128)(2,1)} custom-call(s32[1]{0:T(128)} %bitcast.13.at.core, bf16[1024,3072]{1,0:T(8,128)(2,1)} %get-tuple-element.150.refs_0_, bf16[1024,3072]{1,0:T(8,128)(2,1)} %get-tuple-element.151.refs_1_, bf16[1024,3072]{1,0:T(8,128)(2,1)} %get-tuple-element.152.refs_2_, bf16[1024,3072]{1,0:T(8,128)(2,1)} %get-tuple-element.153.refs_3_, ...), custom_call_target="tpu_custom_call" | custom-call | flops 393216 | bytes 393216 | tf_op jit(solution)/shard_map/weight_grads/pallas_call | solution.py:509
  267.8 8.2 %all-to-all-start.5 = ((bf16[16,128,768]{2,1,0:T(8,128)(2,1)}), bf16[16,128,768]{2,1,0:T(8,128)(2,1)S(1)}, u32[]{:S(2)}, u32[]{:S(2)}) async-start(bf16[16,128,768]{2,1,0:T(8,128)(2,1)} %get-tuple-element.176), calls=%async_computation.5 | async-start | bytes 6291456 | tf_op jit(solution)/shard_map/all_to_all | solution.py:743
  276.0 6.6 %fusion.27 = (bf16[2,768,384]{2,1,0:T(8,128)(2,1)}, bf16[2,768,384]{2,1,0:T(8,128)(2,1)}, bf16[2,768,384]{2,1,0:T(8,128)(2,1)}, bf16[2,768,384]{2,1,0:T(8,128)(2,1)}) fusion(bf16[4,2,768,384]{3,2,1,0:T(8,128)(2,1)} %collective-permute-done.1, s32[]{:T(128)S(6)} %select_n.196, bf16[4,2,768,384]{3,2,1,0:T(8,128)(2,1)} %weight_grads.3, s32[]{:T(128)S(6)} %select_n.195, ...), kind=kLoop, calls=%fused_computation.39 | loop fusion | flops 9437184 | bytes 14155792 | tf_op jit(solution)/shard_map/convert_element_type | solution.py:763
  288.8 16.5 %route_back.1 = (f32[1024,768]{1,0:T(8,128)}, bf16[1024,768]{1,0:T(8,128)(2,1)}, bf16[1024,768]{1,0:T(8,128)(2,1)}, f32[24,768]{1,0:T(8,128)}) custom-call(s32[1024,1]{1,0:T(8,128)} %get-tuple-element.135.t1, s32[1024,1]{1,0:T(8,128)} %get-tuple-element.136.t2, s32[1024,2]{1,0:T(8,128)} %bitcast.100, f32[1024,16]{1,0:T(8,128)} %get-tuple-element.286.probs, ...), custom_call_target="tpu_custom_call" | custom-call | flops 196608 | bytes 196608 | tf_op jit(solution)/shard_map/route_back/pallas_call | solution.py:713
  305.3 20.8 %attend_back.3 = (bf16[1024,256]{1,0:T(8,128)(2,1)}, bf16[2,1024,256]{2,1,0:T(8,128)(2,1)}, bf16[2,1024,256]{2,1,0:T(8,128)(2,1)}) custom-call(bf16[1024,768]{1,0:T(8,128)(2,1)} %get-tuple-element.131.q_ref, bf16[1024,1536]{1,0:T(8,128)(2,1)} %get-tuple-element.132.k0.v0, bf16[1024,1536]{1,0:T(8,128)(2,1)} %copy-done, ...), custom_call_target="tpu_custom_call" | custom-call | flops 196608 | bytes 196608 | tf_op jit(solution)/shard_map/attend_back/pallas_call | solution.py:215
  326.1 21.0 %attend_back.4 = (bf16[1024,256]{1,0:T(8,128)(2,1)}, bf16[2,1024,256]{2,1,0:T(8,128)(2,1)}, bf16[2,1024,256]{2,1,0:T(8,128)(2,1)}) custom-call(bf16[1024,768]{1,0:T(8,128)(2,1)} %get-tuple-element.131.q_ref, bf16[1024,1536]{1,0:T(8,128)(2,1)} %get-tuple-element.132.k0.v0, bf16[1024,1536]{1,0:T(8,128)(2,1)} %copy-done, ...), custom_call_target="tpu_custom_call" | custom-call | flops 196608 | bytes 196608 | tf_op jit(solution)/shard_map/attend_back/pallas_call | solution.py:215
  349.3 7.9 %unseat.1 = bf16[1024,768]{1,0:T(8,128)(2,1)} custom-call(s32[1024,1]{1,0:T(8,128)} %get-tuple-element.135.t1, s32[1024,1]{1,0:T(8,128)} %get-tuple-element.136.t2, f32[1024,768]{1,0:T(8,128)} %copy-done.1, bf16[16,128,768]{2,1,0:T(8,128)(2,1)} %copy-done.9), custom_call_target="tpu_custom_call" | custom-call | flops 196608 | bytes 196608 | tf_op jit(solution)/shard_map/unseat/pallas_call | solution.py:655
  357.1 9.6 %grad_qkv.3 = (bf16[768,2432]{1,0:T(8,128)(2,1)}, bf16[1024,1536]{1,0:T(8,128)(2,1)}) custom-call(s32[1]{0:T(128)} %constant.165.clone.1.core, bf16[1024,768]{1,0:T(8,128)(2,1)} %get-tuple-element.179.normed, bf16[1024,256]{1,0:T(8,128)(2,1)} %get-tuple-element.171.refs_0_, bf16[1024,256]{1,0:T(8,128)(2,1)} %get-tuple-element.174.refs_1_, ...), custom_call_target="tpu_custom_call" | custom-call | flops 196608 | bytes 196608 | tf_op jit(solution)/shard_map/grad_qkv/pallas_call | solution.py:287
  372.2 4.0 collective-permute-done.7
  386.7 20.7 %attend_back.5 = (bf16[1024,256]{1,0:T(8,128)(2,1)}, bf16[2,1024,256]{2,1,0:T(8,128)(2,1)}, bf16[2,1024,256]{2,1,0:T(8,128)(2,1)}) custom-call(bf16[1024,768]{1,0:T(8,128)(2,1)} %get-tuple-element.131.q_ref, bf16[1024,1536]{1,0:T(8,128)(2,1)} %get-tuple-element.132.k0.v0, bf16[1024,1536]{1,0:T(8,128)(2,1)} %copy-done, ...), custom_call_target="tpu_custom_call" | custom-call | flops 196608 | bytes 196608 | tf_op jit(solution)/shard_map/attend_back/pallas_call | solution.py:215
  415.5 3.8 grad_qkv.4
  430.7 4.6 collective-permute-done.16
  453.0 6.5 %spread.1 = (f32[4,768,384]{2,1,0:T(8,128)}, f32[4,384,768]{2,1,0:T(8,128)}) custom-call(s32[1]{0:T(128)} %bitcast.11.which.at, bf16[2,768,384]{2,1,0:T(8,128)(2,1)} %get-tuple-element.225.refs_0_, bf16[2,768,384]{2,1,0:T(8,128)(2,1)} %collective-permute-done.4.refs_1_, bf16[2,768,384]{2,1,0:T(8,128)(2,1)} %collective-permute-done.5.refs_2_, ...), custom_call_target="tpu_custom_call" | custom-call | flops 73728 | bytes 3538944 | tf_op jit(solution)/shard_map/spread/pallas_call | solution.py:839
  488.8 9.9 %assemble.1 = (f32[768,2304]{1,0:T(8,128)}, f32[768,768]{1,0:T(8,128)}, f32[768,128]{1,0:T(8,128)}, f32[768,1]{1,0:T(8,128)}) custom-call(s32[3]{0:T(128)} %pad_add_fusion.at, bf16[768,2304]{1,0:T(8,128)(2,1)} %w_ref.3, bf16[4,4,24,2432]{3,2,1,0:T(8,128)(2,1)} %copy-done.10, bf16[4,4,24,768]{3,2,1,0:T(8,128)(2,1)} %copy-done.14, ...), custom_call_target="tpu_custom_call" | custom-call | flops 442368 | bytes 5308416 | tf_op jit(solution)/shard_map/assemble/pallas_call | solution.py:808
  (196 shorter events, 116.7 us)
Async XLA Ops:
  13.4 79.0 %all-to-all-start = ((bf16[16,128,768]{2,1,0:T(8,128)(2,1)}), bf16[16,128,768]{2,1,0:T(8,128)(2,1)}, u32[]{:S(2)}, u32[]{:S(2)}) async-start(bf16[16,128,768]{2,1,0:T(8,128)(2,1)} %seat_rows.3), calls=%async_computation | async-start | bytes 6291456 | tf_op jit(solution)/shard_map/all_to_all | solution.py:743
  92.4 44.6 %all-to-all-start.1 = ((bf16[16,72,768]{2,1,0:T(8,128)(2,1)}), bf16[16,72,768]{2,1,0:T(8,128)(2,1)S(1)}, u32[]{:S(2)}, u32[]{:S(2)}) async-start(bf16[16,72,768]{2,1,0:T(8,128)(2,1)} %seat_rows.4), calls=%async_computation.1 | async-start | bytes 3538944 | tf_op jit(solution)/shard_map/all_to_all | solution.py:743
  137.0 42.5 %all-to-all-start.2 = ((bf16[16,64,768]{2,1,0:T(8,128)(2,1)}), bf16[16,64,768]{2,1,0:T(8,128)(2,1)S(1)}, u32[]{:S(2)}, u32[]{:S(2)}) async-start(bf16[16,64,768]{2,1,0:T(8,128)(2,1)} %seat_rows.5), calls=%async_computation.2 | async-start | bytes 3145728 | tf_op jit(solution)/shard_map/all_to_all | solution.py:743
  179.5 41.1 %all-to-all-start.3 = ((bf16[16,64,768]{2,1,0:T(8,128)(2,1)}), bf16[16,64,768]{2,1,0:T(8,128)(2,1)S(1)}, u32[]{:S(2)}, u32[]{:S(2)}) async-start(bf16[16,64,768]{2,1,0:T(8,128)(2,1)} %get-tuple-element.146), calls=%async_computation.3 | async-start | bytes 3145728 | tf_op jit(solution)/shard_map/all_to_all | solution.py:743
  221.9 44.7 %all-to-all-start.4 = ((bf16[16,72,768]{2,1,0:T(8,128)(2,1)}), bf16[16,72,768]{2,1,0:T(8,128)(2,1)S(1)}, u32[]{:S(2)}, u32[]{:S(2)}) async-start(bf16[16,72,768]{2,1,0:T(8,128)(2,1)} %get-tuple-element.149), calls=%async_computation.4 | async-start | bytes 3538944 | tf_op jit(solution)/shard_map/all_to_all | solution.py:743
  266.6 9.4 %collective-permute-start.1 = (bf16[4,2,768,384]{3,2,1,0:T(8,128)(2,1)}, bf16[4,2,768,384]{3,2,1,0:T(8,128)(2,1)}, u32[]{:S(2)}, u32[]{:S(2)}) collective-permute-start(bf16[4,2,768,384]{3,2,1,0:T(8,128)(2,1)} %get-tuple-element.164), channel_id=1, source_target_pairs={{0,4},{4,0},{1,5},{5,1},{2,6},{6,2},{3,7},{7,3},{8,12},{12,8},{9,1... | collective-permute-start | bytes 14155784 | tf_op jit(solution)/shard_map/ppermute | solution.py:739
  267.8 79.8 %all-to-all-start.5 = ((bf16[16,128,768]{2,1,0:T(8,128)(2,1)}), bf16[16,128,768]{2,1,0:T(8,128)(2,1)S(1)}, u32[]{:S(2)}, u32[]{:S(2)}) async-start(bf16[16,128,768]{2,1,0:T(8,128)(2,1)} %get-tuple-element.176), calls=%async_computation.5 | async-start | bytes 6291456 | tf_op jit(solution)/shard_map/all_to_all | solution.py:743
  282.6 84.2 %collective-permute-start.4 = (bf16[2,768,384]{2,1,0:T(8,128)(2,1)}, bf16[2,768,384]{2,1,0:T(8,128)(2,1)}, u32[]{:S(2)}, u32[]{:S(2)}) collective-permute-start(bf16[2,768,384]{2,1,0:T(8,128)(2,1)} %get-tuple-element.188), channel_id=1, source_target_pairs={{0,1},{1,2},{2,3},{3,0},{4,5},{5,6},{6,7},{7,4},{8,9},{9,10},{10,1... | collective-permute-start | bytes 3538952 | tf_op jit(solution)/shard_map/ppermute | solution.py:748
  284.5 82.3 %collective-permute-start.5 = (bf16[2,768,384]{2,1,0:T(8,128)(2,1)}, bf16[2,768,384]{2,1,0:T(8,128)(2,1)}, u32[]{:S(2)}, u32[]{:S(2)}) collective-permute-start(bf16[2,768,384]{2,1,0:T(8,128)(2,1)} %get-tuple-element.189), channel_id=1, source_target_pairs={{0,2},{1,3},{2,0},{3,1},{4,6},{5,7},{6,4},{7,5},{8,10},{9,11},{10,... | collective-permute-start | bytes 3538952 | tf_op jit(solution)/shard_map/ppermute | solution.py:748
  286.0 83.3 %collective-permute-start.6 = (bf16[2,768,384]{2,1,0:T(8,128)(2,1)}, bf16[2,768,384]{2,1,0:T(8,128)(2,1)}, u32[]{:S(2)}, u32[]{:S(2)}) collective-permute-start(bf16[2,768,384]{2,1,0:T(8,128)(2,1)} %get-tuple-element.190), channel_id=1, source_target_pairs={{0,3},{1,0},{2,1},{3,2},{4,7},{5,4},{6,5},{7,6},{8,11},{9,8},{10,9... | collective-permute-start | bytes 3538952 | tf_op jit(solution)/shard_map/ppermute | solution.py:748
  347.1 10.0 %collective-permute-start.3 = (bf16[2,1024,256]{2,1,0:T(8,128)(2,1)}, bf16[2,1024,256]{2,1,0:T(8,128)(2,1)}, u32[]{:S(2)}, u32[]{:S(2)}) collective-permute-start(bf16[2,1024,256]{2,1,0:T(8,128)(2,1)} %get-tuple-element.173), channel_id=1, source_target_pairs={{0,4},{4,0},{1,5},{5,1},{2,6},{6,2},{3,7},{7,3},{8,12},{12,8},{9,1... | collective-permute-start | bytes 3145736 | tf_op jit(solution)/shard_map/ppermute | solution.py:739
  347.1 10.0 %collective-permute-start.2 = (bf16[2,1024,256]{2,1,0:T(8,128)(2,1)}, bf16[2,1024,256]{2,1,0:T(8,128)(2,1)}, u32[]{:S(2)}, u32[]{:S(2)}) collective-permute-start(bf16[2,1024,256]{2,1,0:T(8,128)(2,1)} %get-tuple-element.170), channel_id=1, source_target_pairs={{0,4},{4,0},{1,5},{5,1},{2,6},{6,2},{3,7},{7,3},{8,12},{12,8},{9,1... | collective-permute-start | bytes 3145736 | tf_op jit(solution)/shard_map/ppermute | solution.py:739
  378.3 29.1 %collective-permute-start.10 = (bf16[96,2432]{1,0:T(8,128)(2,1)S(1)}, bf16[96,2432]{1,0:T(8,128)(2,1)S(1)}, u32[]{:S(2)}, u32[]{:S(2)}) collective-permute-start(bf16[96,2432]{1,0:T(8,128)(2,1)S(1)} %get-tuple-element.297), channel_id=1, source_target_pairs={{0,3},{1,0},{2,1},{3,2},{4,7},{5,4},{6,5},{7,6},{8,11},{9,8},{10,9... | collective-permute-start | bytes 1400840 | tf_op jit(solution)/shard_map/ppermute | solution.py:748
  381.0 26.4 %collective-permute-start.8 = (bf16[96,2432]{1,0:T(8,128)(2,1)S(1)}, bf16[96,2432]{1,0:T(8,128)(2,1)}, u32[]{:S(2)}, u32[]{:S(2)}) collective-permute-start(bf16[96,2432]{1,0:T(8,128)(2,1)S(1)} %get-tuple-element.299), channel_id=1, source_target_pairs={{0,1},{1,2},{2,3},{3,0},{4,5},{5,6},{6,7},{7,4},{8,9},{9,10},{10,1... | collective-permute-start | bytes 1400840 | tf_op jit(solution)/shard_map/ppermute | solution.py:748
  381.0 26.4 %collective-permute-start.9 = (bf16[96,2432]{1,0:T(8,128)(2,1)S(1)}, bf16[96,2432]{1,0:T(8,128)(2,1)}, u32[]{:S(2)}, u32[]{:S(2)}) collective-permute-start(bf16[96,2432]{1,0:T(8,128)(2,1)S(1)} %get-tuple-element.298), channel_id=1, source_target_pairs={{0,2},{1,3},{2,0},{3,1},{4,6},{5,7},{6,4},{7,5},{8,10},{9,11},{10,... | collective-permute-start | bytes 1400840 | tf_op jit(solution)/shard_map/ppermute | solution.py:748
  409.1 13.5 %collective-permute-start.12 = (bf16[24,2432]{1,0:T(8,128)(2,1)S(1)}, bf16[24,2432]{1,0:T(8,128)(2,1)S(1)}, u32[]{:S(2)}, u32[]{:S(2)}) collective-permute-start(bf16[24,2432]{1,0:T(8,128)(2,1)S(1)} %get-tuple-element.309), channel_id=1, source_target_pairs={{0,8},{8,16},{16,24},{24,0},{1,9},{9,17},{17,25},{25,1},{2,10},{10... | collective-permute-start | bytes 350216 | tf_op jit(solution)/shard_map/ppermute | solution.py:748
  411.6 11.0 %collective-permute-start.13 = (bf16[24,2432]{1,0:T(8,128)(2,1)S(1)}, bf16[24,2432]{1,0:T(8,128)(2,1)S(1)}, u32[]{:S(2)}, u32[]{:S(2)}) collective-permute-start(bf16[24,2432]{1,0:T(8,128)(2,1)S(1)} %get-tuple-element.308), channel_id=1, source_target_pairs={{0,16},{8,24},{16,0},{24,8},{1,17},{9,25},{17,1},{25,9},{2,18},{10... | collective-permute-start | bytes 350216 | tf_op jit(solution)/shard_map/ppermute | solution.py:748
  411.6 11.0 %collective-permute-start.14 = (bf16[24,2432]{1,0:T(8,128)(2,1)S(1)}, bf16[24,2432]{1,0:T(8,128)(2,1)S(1)}, u32[]{:S(2)}, u32[]{:S(2)}) collective-permute-start(bf16[24,2432]{1,0:T(8,128)(2,1)S(1)} %get-tuple-element.307), channel_id=1, source_target_pairs={{0,24},{8,0},{16,8},{24,16},{1,25},{9,1},{17,9},{25,17},{2,26},{10... | collective-permute-start | bytes 350216 | tf_op jit(solution)/shard_map/ppermute | solution.py:748
  422.7 7.9 %collective-permute-start.15 = (bf16[24,2432]{1,0:T(8,128)(2,1)S(1)}, bf16[24,2432]{1,0:T(8,128)(2,1)S(1)}, u32[]{:S(2)}, u32[]{:S(2)}) collective-permute-start(bf16[24,2432]{1,0:T(8,128)(2,1)S(1)} %add_convert_fusion.7), channel_id=1, source_target_pairs={{0,8},{8,16},{16,24},{24,0},{1,9},{9,17},{17,25},{25,1},{2,10},{10... | collective-permute-start | bytes 350216 | tf_op jit(solution)/shard_map/ppermute | solution.py:748
  424.7 10.5 %collective-permute-start.16 = (bf16[24,2432]{1,0:T(8,128)(2,1)S(1)}, bf16[24,2432]{1,0:T(8,128)(2,1)S(1)}, u32[]{:S(2)}, u32[]{:S(2)}) collective-permute-start(bf16[24,2432]{1,0:T(8,128)(2,1)S(1)} %add_convert_fusion.7), channel_id=1, source_target_pairs={{0,16},{8,24},{16,0},{24,8},{1,17},{9,25},{17,1},{25,9},{2,18},{10... | collective-permute-start | bytes 350216 | tf_op jit(solution)/shard_map/ppermute | solution.py:748
  425.9 9.3 %collective-permute-start.17 = (bf16[24,2432]{1,0:T(8,128)(2,1)S(1)}, bf16[24,2432]{1,0:T(8,128)(2,1)S(1)}, u32[]{:S(2)}, u32[]{:S(2)}) collective-permute-start(bf16[24,2432]{1,0:T(8,128)(2,1)S(1)} %add_convert_fusion.7), channel_id=1, source_target_pairs={{0,24},{8,0},{16,8},{24,16},{1,25},{9,1},{17,9},{25,17},{2,26},{10... | collective-permute-start | bytes 350216 | tf_op jit(solution)/shard_map/ppermute | solution.py:748
  436.7 7.9 %collective-permute-start.20 = (bf16[96,768]{1,0:T(8,128)(2,1)S(1)}, bf16[96,768]{1,0:T(8,128)(2,1)S(1)}, u32[]{:S(2)}, u32[]{:S(2)}) collective-permute-start(bf16[96,768]{1,0:T(8,128)(2,1)S(1)} %get-tuple-element.302), channel_id=1, source_target_pairs={{0,2},{1,3},{2,0},{3,1},{4,6},{5,7},{6,4},{7,5},{8,10},{9,11},{10,... | collective-permute-start | bytes 442376 | tf_op jit(solution)/shard_map/ppermute | solution.py:748
  444.8 14.7 %collective-permute-start.25 = (bf16[24,768]{1,0:T(8,128)(2,1)S(1)}, bf16[24,768]{1,0:T(8,128)(2,1)S(1)}, u32[]{:S(2)}, u32[]{:S(2)}) collective-permute-start(bf16[24,768]{1,0:T(8,128)(2,1)S(1)} %get-tuple-element.313), channel_id=1, source_target_pairs={{0,8},{8,16},{16,24},{24,0},{1,9},{9,17},{17,25},{25,1},{2,10},{10... | collective-permute-start | bytes 110600 | tf_op jit(solution)/shard_map/ppermute | solution.py:748
  447.9 13.0 %collective-permute-start.26 = (bf16[24,768]{1,0:T(8,128)(2,1)S(1)}, bf16[24,768]{1,0:T(8,128)(2,1)S(1)}, u32[]{:S(2)}, u32[]{:S(2)}) collective-permute-start(bf16[24,768]{1,0:T(8,128)(2,1)S(1)} %get-tuple-element.312), channel_id=1, source_target_pairs={{0,16},{8,24},{16,0},{24,8},{1,17},{9,25},{17,1},{25,9},{2,18},{10... | collective-permute-start | bytes 110600 | tf_op jit(solution)/shard_map/ppermute | solution.py:748
  448.7 12.1 %collective-permute-start.27 = (bf16[24,768]{1,0:T(8,128)(2,1)S(1)}, bf16[24,768]{1,0:T(8,128)(2,1)S(1)}, u32[]{:S(2)}, u32[]{:S(2)}) collective-permute-start(bf16[24,768]{1,0:T(8,128)(2,1)S(1)} %get-tuple-element.311), channel_id=1, source_target_pairs={{0,24},{8,0},{16,8},{24,16},{1,25},{9,1},{17,9},{25,17},{2,26},{10... | collective-permute-start | bytes 110600 | tf_op jit(solution)/shard_map/ppermute | solution.py:748
  450.3 22.2 %collective-permute-start.22 = (bf16[4,24,2432]{2,1,0:T(8,128)(2,1)S(1)}, bf16[4,24,2432]{2,1,0:T(8,128)(2,1)S(1)}, u32[]{:S(2)}, u32[]{:S(2)}) collective-permute-start(bf16[4,24,2432]{2,1,0:T(8,128)(2,1)S(1)} %pad_maximum_fusion.2), channel_id=1, source_target_pairs={{0,1},{1,2},{2,3},{3,0},{4,5},{5,6},{6,7},{7,4},{8,9},{9,10},{10,1... | collective-permute-start | bytes 1400840 | tf_op jit(solution)/shard_map/ppermute | solution.py:748
  452.0 22.6 %collective-permute-start.23 = (bf16[4,24,2432]{2,1,0:T(8,128)(2,1)S(1)}, bf16[4,24,2432]{2,1,0:T(8,128)(2,1)S(1)}, u32[]{:S(2)}, u32[]{:S(2)}) collective-permute-start(bf16[4,24,2432]{2,1,0:T(8,128)(2,1)S(1)} %pad_maximum_fusion.2), channel_id=1, source_target_pairs={{0,2},{1,3},{2,0},{3,1},{4,6},{5,7},{6,4},{7,5},{8,10},{9,11},{10,... | collective-permute-start | bytes 1400840 | tf_op jit(solution)/shard_map/ppermute | solution.py:748
  459.5 15.1 %collective-permute-start.24 = (bf16[4,24,2432]{2,1,0:T(8,128)(2,1)S(1)}, bf16[4,24,2432]{2,1,0:T(8,128)(2,1)S(1)}, u32[]{:S(2)}, u32[]{:S(2)}) collective-permute-start(bf16[4,24,2432]{2,1,0:T(8,128)(2,1)S(1)} %pad_maximum_fusion.2), channel_id=1, source_target_pairs={{0,3},{1,0},{2,1},{3,2},{4,7},{5,4},{6,5},{7,6},{8,11},{9,8},{10,9... | collective-permute-start | bytes 1400840 | tf_op jit(solution)/shard_map/ppermute | solution.py:748
  470.8 15.0 %collective-permute-start.31 = (bf16[4,24,768]{2,1,0:T(8,128)(2,1)S(1)}, bf16[4,24,768]{2,1,0:T(8,128)(2,1)S(1)}, u32[]{:S(2)}, u32[]{:S(2)}) collective-permute-start(bf16[4,24,768]{2,1,0:T(8,128)(2,1)S(1)} %pad_maximum_fusion.3), channel_id=1, source_target_pairs={{0,1},{1,2},{2,3},{3,0},{4,5},{5,6},{6,7},{7,4},{8,9},{9,10},{10,1... | collective-permute-start | bytes 442376 | tf_op jit(solution)/shard_map/ppermute | solution.py:748
  471.5 14.3 %collective-permute-start.32 = (bf16[4,24,768]{2,1,0:T(8,128)(2,1)S(1)}, bf16[4,24,768]{2,1,0:T(8,128)(2,1)S(1)}, u32[]{:S(2)}, u32[]{:S(2)}) collective-permute-start(bf16[4,24,768]{2,1,0:T(8,128)(2,1)S(1)} %pad_maximum_fusion.3), channel_id=1, source_target_pairs={{0,2},{1,3},{2,0},{3,1},{4,6},{5,7},{6,4},{7,5},{8,10},{9,11},{10,... | collective-permute-start | bytes 442376 | tf_op jit(solution)/shard_map/ppermute | solution.py:748
  472.5 13.3 %collective-permute-start.33 = (bf16[4,24,768]{2,1,0:T(8,128)(2,1)S(1)}, bf16[4,24,768]{2,1,0:T(8,128)(2,1)S(1)}, u32[]{:S(2)}, u32[]{:S(2)}) collective-permute-start(bf16[4,24,768]{2,1,0:T(8,128)(2,1)S(1)} %pad_maximum_fusion.3), channel_id=1, source_target_pairs={{0,3},{1,0},{2,1},{3,2},{4,7},{5,4},{6,5},{7,6},{8,11},{9,8},{10,9... | collective-permute-start | bytes 442376 | tf_op jit(solution)/shard_map/ppermute | solution.py:748
  476.8 11.2 %collective-permute-start.34 = (bf16[4,4,24,2432]{3,2,1,0:T(8,128)(2,1)S(1)}, bf16[4,4,24,2432]{3,2,1,0:T(8,128)(2,1)}, u32[]{:S(2)}, u32[]{:S(2)}) collective-permute-start(bf16[4,4,24,2432]{3,2,1,0:T(8,128)(2,1)S(1)} %pad_maximum_fusion.refs_0_), channel_id=1, source_target_pairs={{0,4},{4,0},{1,5},{5,1},{2,6},{6,2},{3,7},{7,3},{8,12},{12,8},{9,1... | collective-permute-start | bytes 5603336 | tf_op jit(solution)/shard_map/ppermute | solution.py:739
  (43 other events, 206.9 us)
